TPU v7x, 32 devices: a whole 2x2x4 slice. The times are simulated.
32 devices in a mesh: tm: 4 (over z), height: 4 (over y, x), width: 2 (over core).
Axes of the slice: x: 2, y: 2, z: 4, core: 2. Of those that a mesh axis runs over, the one named last changes fastest.
Arguments:
- video: bfloat16 [2, 128, 8, 256, 128], P('width', ('tm', 'height')), may hold values from -6 to 6
- out_grad: bfloat16 [2, 128, 8, 256, 128], P('width', None, 'tm', 'height'), may hold values from -6 to 6
- lengths: int32 [4], replicated, may hold values from 1 to 3, 8 in all
- temporal_weight: bfloat16 [3, 128, 128], replicated, may hold values from -0.3125 to 0.3125
- spatial_weight: bfloat16 [3, 3, 128, 128], replicated, may hold values from -0.1875 to 0.1875
Outputs:
- video_grad: bfloat16 [2, 128, 8, 256, 128], P('width', ('tm', 'height'))
- temporal_grad: float32 [3, 128, 128], replicated
- spatial_grad: float32 [3, 3, 128, 128], replicated
Inputs may be any that keep to these rules, and one draw needn't show every extreme that they name: The 4 clips lie end to end in frame order, their lengths sum to 8, and the longest clip has exactly 3 frames.
All inputs are finite; a program needn't handle non-finite values.
Results may differ from a plain program's by a relative error of at most 0.008.
Values may be sent and summed in bfloat16 or wider, within the bound.
No kernel may reach another device: no remote copies, remote signals or barrier semaphores. Data moves between devices by JAX's collectives and lax.ppermute only.
A program may use at most 192 MiB of HBM per device.

v0:
```python
import jax
import jax.numpy as jnp
from jax import lax
from jax.sharding import PartitionSpec as P


def with_halo(cells, sides, width):
    for axis, dim in sides:
        count = lax.axis_size(axis)
        ends = count - 1
        head = lax.slice_in_dim(cells, 0, width, axis=dim)
        tail = lax.slice_in_dim(cells, cells.shape[dim] - width, cells.shape[dim], axis=dim)
        cells = jnp.concatenate(
            [
                lax.ppermute(tail, axis, [(i, (i + 1) % count) for i in range(ends)]),
                cells,
                lax.ppermute(head, axis, [((i + 1) % count, i) for i in range(ends)]),
            ],
            axis=dim,
        )
    return cells


def frame_masks(lengths, frames):
    ends = jnp.cumsum(lengths, dtype=jnp.int32)
    starts = ends - lengths
    frame_index = jnp.arange(frames, dtype=jnp.int32)
    inside = (frame_index[:, None] >= starts[None, :]) & (frame_index[:, None] < ends[None, :])
    first = jnp.sum(jnp.where(inside, starts[None, :], 0), axis=1, dtype=jnp.int32)
    return jnp.stack([frame_index - lag >= first for lag in range(3)]).astype(jnp.bfloat16)


def silu_slope(pre, grads):
    sig = jax.nn.sigmoid(pre)
    return grads.astype(jnp.float32) * sig * (1.0 + pre * (1.0 - sig))


def flatten(block):
    return block.reshape(-1, block.shape[-1])


def spatial_forward(padded, weights, cols, rows):
    total = None
    for row_off in range(3):
        for col_off in range(3):
            piece = flatten(padded[col_off : col_off + cols, :, row_off : row_off + rows])
            term = jnp.dot(piece, weights[row_off, col_off], preferred_element_type=jnp.float32)
            total = term if total is None else total + term
    return total


def shards(video, out_grad, lengths, temporal_weight, spatial_weight):
    width_loc = video.shape[1]
    frames = video.shape[2]
    rows = video.shape[3]
    chans = video.shape[4]
    n_tm = lax.axis_size("tm")
    n_height = lax.axis_size("height")
    frames_dev = frames // n_tm
    rows_dev = rows // n_height
    cols_half = out_grad.shape[1]
    total_cols = cols_half * lax.axis_size("width")
    masks = frame_masks(lengths, frames)
    local_video = video[0]
    padded_video = jnp.pad(local_video, ((0, 0), (2, 0), (0, 0), (0, 0)))
    taps = [
        padded_video[:, 2 - lag : 2 - lag + frames] * masks[lag][None, :, None, None]
        for lag in range(3)
    ]
    total = None
    for lag in range(3):
        term = jnp.dot(flatten(taps[lag]), temporal_weight[lag], preferred_element_type=jnp.float32)
        total = term if total is None else total + term
    act_time = total.astype(jnp.bfloat16).reshape(local_video.shape)
    arranged = act_time.reshape(width_loc, n_tm, frames_dev, n_height, rows_dev, chans)
    arranged = arranged.transpose(1, 3, 0, 2, 4, 5).reshape(
        n_tm * n_height * width_loc, frames_dev, rows_dev, chans
    )
    act_space = lax.all_to_all(arranged, ("tm", "height"), split_axis=0, concat_axis=0, tiled=True)
    grad_space = out_grad[0]
    padded_act = with_halo(act_space, (("height", 2), ("width", 0)), 1)
    pre = spatial_forward(padded_act, spatial_weight, cols_half, rows_dev)
    delta = silu_slope(pre, flatten(grad_space)).astype(jnp.bfloat16).reshape(act_space.shape)
    padded_delta = with_halo(delta, (("height", 2), ("width", 0)), 1)
    flat_delta = flatten(delta)
    back = None
    spatial_terms = []
    for row_off in range(3):
        line = []
        for col_off in range(3):
            piece = flatten(
                padded_delta[
                    2 - col_off : 2 - col_off + cols_half, :, 2 - row_off : 2 - row_off + rows_dev
                ]
            )
            term = jnp.dot(
                piece, spatial_weight[row_off, col_off].T, preferred_element_type=jnp.float32
            )
            back = term if back is None else back + term
            source = flatten(
                padded_act[col_off : col_off + cols_half, :, row_off : row_off + rows_dev]
            )
            line.append(
                lax.dot_general(
                    source, flat_delta, (((0,), (0,)), ((), ())), preferred_element_type=jnp.float32
                )
            )
        spatial_terms.append(jnp.stack(line))
    spatial_local = jnp.stack(spatial_terms)
    grad_act_space = back.astype(jnp.bfloat16).reshape(act_space.shape)
    received = lax.all_to_all(
        grad_act_space, ("tm", "height"), split_axis=0, concat_axis=0, tiled=True
    )
    received = received.reshape(n_tm, n_height, width_loc, frames_dev, rows_dev, chans)
    grad_time = received.transpose(2, 0, 3, 1, 4, 5).reshape(width_loc, frames, rows, chans)
    flat_grad = flatten(grad_time)
    frame_total = None
    temporal_terms = []
    for lag in range(3):
        temporal_terms.append(
            lax.dot_general(
                flatten(taps[lag]),
                flat_grad,
                (((0,), (0,)), ((), ())),
                preferred_element_type=jnp.float32,
            )
        )
        masked = flatten(grad_time * masks[lag][None, :, None, None])
        product = jnp.dot(
            masked, temporal_weight[lag].T, preferred_element_type=jnp.float32
        ).reshape(grad_time.shape)
        moved = jnp.pad(product[:, lag:], ((0, 0), (0, lag), (0, 0), (0, 0)))
        frame_total = moved if frame_total is None else frame_total + moved
    temporal_local = jnp.stack(temporal_terms)
    video_grad = frame_total.astype(jnp.bfloat16)[None]
    scale = float(frames * rows * total_cols) ** (-0.5)
    temporal_grad, spatial_grad = lax.psum(
        (temporal_local * scale, spatial_local * scale), ("tm", "height", "width")
    )
    return (video_grad, temporal_grad, spatial_grad)


def solution(mesh):
    placed = (
        P("width", ("tm", "height"), None, None, None),
        P("width", None, "tm", "height", None),
        P(),
        P(),
        P(),
    )
    return jax.shard_map(
        shards,
        mesh=mesh,
        in_specs=placed,
        out_specs=(P("width", ("tm", "height"), None, None, None), P(), P()),
        check_vma=False,
    )
```

profile of v0, /device:TPU:0, one launch (start us, length us, event | category | flops | bytes accessed | tf_op | source)
XLA Modules:
  0.0 558.3 jit_solution(17389231994226346784)
XLA Ops:
  22.1 101.9 %all_to_all.10 = bf16[128,2,64,128]{3,2,1,0:T(8,128)(2,1)S(1)} all-to-all(bf16[128,2,64,128]{3,2,1,0:T(8,128)(2,1)S(1)} %bitcast.248), channel_id=1, replica_groups=mesh['tm'=4,'height'=4,'width'=2] {'tm','height'}, dimensions={0} | all-to-all | bytes 8388608 | tf_op jit(solution)/shard_map/all_to_all | solution.py:79
  136.5 6.4 %pad_maximum_fusion.4 = (bf16[128,2,64,128]{3,2,1,0:T(8,128)(2,1)}, bf16[128,2,64,128]{3,2,1,0:T(8,128)(2,1)S(1)}) fusion(bf16[128,2,1,128]{3,2,1,0:T(2,128)(2,1)S(1)} %collective-permute-done.1, bf16[128,2,64,128]{3,2,1,0:T(8,128)(2,1)S(1)} %all_to_all.10, bf16[128,2,1,128]{3,2,1,0:T(2,128)(2,1)S(1)} %collective-permute-done), kind=kLoop, calls=%fused_computation.35 | loop fusion | flops 16777216 | bytes 12713984 | tf_op jit(solution)/shard_map/concatenate | solution.py:13
  142.9 4.6 fusion.32
  147.5 9.2 %maximum_maximum_fusion = (bf16[129,2,66,128]{3,2,1,0:T(8,128)(2,1)}, bf16[129,2,66,128]{3,2,1,0:T(8,128)(2,1)}) fusion(bf16[128,2,1,128]{3,2,1,0:T(2,128)(2,1)S(1)} %collective-permute-done.1, bf16[128,2,64,128]{3,2,1,0:T(8,128)(2,1)S(1)} %all_to_all.10, bf16[128,2,1,128]{3,2,1,0:T(2,128)(2,1)S(1)} %collective-permute-done, ...), kind=kLoop, calls=%fused_computation.26 | loop fusion | flops 34873344 | bytes 13111296 | tf_op jit(solution)/shard_map/concatenate | solution.py:13
  156.7 21.7 %fusion.67 = (bf16[128,2,64,128]{3,2,1,0:T(8,128)(2,1)S(1)}, bf16[128,2,64,128]{3,2,1,0:T(8,128)(2,1)S(1)}, bf16[128,2,64,128]{3,2,1,0:T(8,128)(2,1)}, bf16[128,...) fusion(bf16[129,2,66,128]{3,2,1,0:T(8,128)(2,1)} %get-tuple-element.24, ...), kind=kLoop, calls=%fused_computation.136 | loop fusion | bytes 50331648 | tf_op jit(solution)/shard_map/slice | solution.py:46
  178.4 9.9 %fusion.16 = f32[16384,128]{1,0:T(8,128)} fusion(bf16[16384,128]{1,0:T(8,128)(2,1)} %bitcast.229, bf16[3,3,128,128]{3,2,1,0:T(8,128)(2,1)S(1)} %copy-done.29), kind=kOutput, calls=%fused_computation.71 | convolution fusion | flops 536870912 | bytes 12615680 | tf_op jit(solution)/shard_map/dot_general | solution.py:47
  188.3 8.1 %convolution_add_fusion.13 = f32[16384,128]{1,0:T(8,128)} fusion(f32[16384,128]{1,0:T(8,128)} %fusion.32, bf16[16384,128]{1,0:T(8,128)(2,1)S(1)} %bitcast.223, bf16[3,3,128,128]{3,2,1,0:T(8,128)(2,1)S(1)} %copy-done.29), kind=kOutput, calls=%fused_computation.15 | convolution fusion | flops 538968064 | bytes 21004288 | tf_op jit(solution)/shard_map/dot_general | solution.py:47
  196.4 7.9 %convolution_add_fusion.12 = f32[16384,128]{1,0:T(8,128)} fusion(f32[16384,128]{1,0:T(8,128)} %convolution_add_fusion.13, bf16[16384,128]{1,0:T(8,128)(2,1)S(1)} %bitcast.225, bf16[3,3,128,128]{3,2,1,0:T(8,128)(2,1)S(1)} %copy-done.29), kind=kOutput, calls=%fused_computation.14 | convolution fusion | flops 538968064 | bytes 21004288 | tf_op jit(solution)/shard_map/dot_general | solution.py:47
  204.3 4.7 convolution_add_fusion.11
  209.0 4.6 convolution_add_fusion.10
  213.6 4.7 convolution_add_fusion.9
  218.3 5.5 convolution_add_fusion.8
  224.7 8.0 %fusion.5 = bf16[16384,128]{1,0:T(8,128)(2,1)S(1)} fusion(bf16[16384,128]{1,0:T(8,128)(2,1)S(1)} %bitcast.250, f32[16384,128]{1,0:T(8,128)} %fusion.16, f32[16384,128]{1,0:T(8,128)} %convolution_add_fusion.8, bf16[16384,128]{1,0:T(8,128)(2,1)S(1)} %bitcast.233, bf16[3,3,128,128]{3,2,1,0:T(8,128)(2,1)S(1)} %copy-done.29), kind=kOutput, calls=%fused_computation.22 | convolution fusion | flops 562036736 | bytes 29392896 | tf_op jit(solution)/shard_map/dot_general | solution.py:47
  232.9 4.6 collective-permute-start.4
  250.0 6.9 %pad_maximum_fusion.2 = (bf16[128,2,64,128]{3,2,1,0:T(8,128)(2,1)}, bf16[128,2,64,128]{3,2,1,0:T(8,128)(2,1)S(1)}) fusion(bf16[128,2,64,128]{3,2,1,0:T(8,128)(2,1)S(1)} %bitcast.206, bf16[128,2,1,128]{3,2,1,0:T(2,128)(2,1)S(1)} %collective-permute-done.4, bf16[128,2,1,128]{3,2,1,0:T(2,128)(2,1)S(1)} %collective-permute-done.5), kind=kLoop, calls=%fused_computation.33 | loop fusion | flops 16777216 | bytes 12713984 | tf_op jit(solution)/shard_map/concatenate | solution.py:13
  258.2 7.1 %pad_maximum_fusion.1 = (bf16[129,2,66,128]{3,2,1,0:T(8,128)(2,1)S(1)}, bf16[129,2,66,128]{3,2,1,0:T(8,128)(2,1)S(1)}) fusion(bf16[1,2,66,128]{3,2,1,0:T(8,128)(2,1)S(1)} %collective-permute-done.6, bf16[128,2,1,128]{3,2,1,0:T(2,128)(2,1)S(1)} %collective-permute-done.5, bf16[128,2,64,128]{3,2,1,0:T(8,128)(2,1)S(1)} %bitcast.207, ...), kind=kLoop, calls=%fused_computation.28 | loop fusion | flops 34873344 | bytes 13111296 | tf_op jit(solution)/shard_map/concatenate | solution.py:13
  265.2 6.3 %fusion.65 = (bf16[128,2,64,128]{3,2,1,0:T(8,128)(2,1)}, bf16[128,2,64,128]{3,2,1,0:T(8,128)(2,1)}, bf16[128,2,64,128]{3,2,1,0:T(8,128)(2,1)}) fusion(bf16[129,2,66,128]{3,2,1,0:T(8,128)(2,1)S(1)} %get-tuple-element.20), kind=kLoop, calls=%fused_computation.134 | loop fusion | bytes 25165824 | tf_op jit(solution)/shard_map/slice | solution.py:92
  271.5 5.7 %fusion.66 = (bf16[128,2,64,128]{3,2,1,0:T(8,128)(2,1)}, bf16[128,2,64,128]{3,2,1,0:T(8,128)(2,1)}, bf16[128,2,64,128]{3,2,1,0:T(8,128)(2,1)}) fusion(bf16[129,2,66,128]{3,2,1,0:T(8,128)(2,1)S(1)} %get-tuple-element.21), kind=kLoop, calls=%fused_computation.135 | loop fusion | bytes 25165824 | tf_op jit(solution)/shard_map/slice | solution.py:92
  292.5 5.7 %fusion.3 = bf16[16384,128]{1,0:T(8,128)(2,1)} fusion(f32[16384,128]{1,0:T(8,128)S(1)} %fusion.14, f32[16384,128]{1,0:T(8,128)S(1)} %convolution_add_fusion.1, bf16[16384,128]{1,0:T(8,128)(2,1)} %bitcast.246, bf16[3,3,128,128]{3,2,1,0:T(8,128)(2,1)S(1)} %copy-done.29), kind=kOutput, calls=%fused_computation.19 | convolution fusion | flops 543162368 | bytes 25198592 | tf_op jit(solution)/shard_map/dot_general | solution.py:96
  298.2 4.7 all-to-all-start.1
  303.4 4.9 convolution_bitcast_fusion.7
  326.9 55.2 %all-to-all-done.1 = bf16[128,2,64,128]{3,2,1,0:T(8,128)(2,1)} async-done(((bf16[128,2,64,128]{3,2,1,0:T(8,128)(2,1)}), bf16[128,2,64,128]{3,2,1,0:T(8,128)(2,1)}, u32[]{:S(2)}, u32[]{:S(2)}) %all-to-all-start.1) | async-done | bytes 4194336 | tf_op jit(solution)/shard_map/all_to_all | solution.py:111
  403.9 9.4 %fusion.8 = bf16[1,8,8,256,128]{4,3,2,1,0:T(8,128)(2,1)} fusion(f32[8,6,256,128]{3,2,1,0:T(8,128)} %fusion.9, f32[8,7,256,128]{3,2,1,0:T(8,128)} %fusion.11, bf16[8,8,256,128]{3,2,1,0:T(8,128)(2,1)} %bitcast.247, bf16[3,128,128]{2,1,0:T(8,128)(2,1)S(1)} %copy-done.31), kind=kOutput, calls=%fused_computation.32 | convolution fusion | flops 543162368 | bytes 22052864 | tf_op jit(solution)/shard_map/dot_general | solution.py:129
  413.3 134.2 %all-reduce.6.cloned.1.call-done = (f32[3,128,128]{2,1,0:T(8,128)}, f32[3,3,128,128]{3,2,1,0:T(8,128)}) async-done(((f32[3,128,128]{2,1,0:T(8,128)}, f32[3,3,128,128]{3,2,1,0:T(8,128)}), (f32[3,128,128]{2,1,0:T(8,128)}, f32[3,3,128,128]{3,2,1,0:T(8,128)})) %all-reduce.6.cloned.1.call-update) | async-done | bytes 786448 | tf_op jit(solution)/shard_map/psum | solution.py:137
  (138 shorter events, 101.7 us)
Async XLA Ops:
  124.0 85.0 %copy-start.2 = (bf16[128,2,64,128]{3,2,1,0:T(8,128)(2,1)}, bf16[128,2,64,128]{3,2,1,0:T(8,128)(2,1)S(1)}, u32[]{:S(2)}) copy-start(bf16[128,2,64,128]{3,2,1,0:T(8,128)(2,1)S(1)} %all_to_all.10) | copy-start | bytes 12582916
  124.2 5.0 collective-permute-start
  126.7 6.9 %collective-permute-start.1 = (bf16[128,2,1,128]{3,2,1,0:T(2,128)(2,1)S(1)}, bf16[128,2,1,128]{3,2,1,0:T(2,128)(2,1)S(1)}, u32[]{:S(2)}, u32[]{:S(2)}) collective-permute-start(bf16[128,2,1,128]{3,2,1,0:T(2,128)(2,1)S(1)} %get-tuple-element.38), channel_id=1, source_target_pairs={{2,0},{4,2},{6,4},{3,1},{5,3},{7,5},{10,8},{12,10},{14,12},{11,9},... | collective-permute-start | bytes 196616 | tf_op jit(solution)/shard_map/ppermute | solution.py:17
  133.6 13.9 %collective-permute-start.2 = (bf16[1,2,66,128]{3,2,1,0:T(8,128)(2,1)S(1)}, bf16[1,2,66,128]{3,2,1,0:T(8,128)(2,1)S(1)}, u32[]{:S(2)}, u32[]{:S(2)}) collective-permute-start(bf16[1,2,66,128]{3,2,1,0:T(8,128)(2,1)S(1)} %get-tuple-element.26), channel_id=1, source_target_pairs={{0,1},{2,3},{4,5},{6,7},{8,9},{10,11},{12,13},{14,15},{16,17},{18,... | collective-permute-start | bytes 101384 | tf_op jit(solution)/shard_map/ppermute | solution.py:15
  134.9 8.0 %copy-start.29 = (bf16[3,3,128,128]{3,2,1,0:T(8,128)(2,1)S(1)}, bf16[3,3,128,128]{3,2,1,0:T(8,128)(2,1)}, u32[]{:S(2)}) copy-start(bf16[3,3,128,128]{3,2,1,0:T(8,128)(2,1)} %param.9) | copy-start | bytes 884740
  134.9 12.6 %collective-permute-start.3 = (bf16[1,2,66,128]{3,2,1,0:T(8,128)(2,1)S(1)}, bf16[1,2,66,128]{3,2,1,0:T(8,128)(2,1)S(1)}, u32[]{:S(2)}, u32[]{:S(2)}) collective-permute-start(bf16[1,2,66,128]{3,2,1,0:T(8,128)(2,1)S(1)} %get-tuple-element.27), channel_id=1, source_target_pairs={{1,0},{3,2},{5,4},{7,6},{9,8},{11,10},{13,12},{15,14},{17,16},{19,... | collective-permute-start | bytes 101384 | tf_op jit(solution)/shard_map/ppermute | solution.py:17
  178.4 25.9 %copy-start.10 = (bf16[128,2,64,128]{3,2,1,0:T(8,128)(2,1)}, bf16[128,2,64,128]{3,2,1,0:T(8,128)(2,1)S(1)}, u32[]{:S(2)}) copy-start(bf16[128,2,64,128]{3,2,1,0:T(8,128)(2,1)S(1)} %get-tuple-element.15) | copy-start | bytes 12582916
  178.4 35.2 %copy-start.12 = (bf16[128,2,64,128]{3,2,1,0:T(8,128)(2,1)}, bf16[128,2,64,128]{3,2,1,0:T(8,128)(2,1)S(1)}, u32[]{:S(2)}) copy-start(bf16[128,2,64,128]{3,2,1,0:T(8,128)(2,1)S(1)} %get-tuple-element.49) | copy-start | bytes 12582916
  178.4 39.8 %copy-start.8 = (bf16[128,2,64,128]{3,2,1,0:T(8,128)(2,1)}, bf16[128,2,64,128]{3,2,1,0:T(8,128)(2,1)S(1)}, u32[]{:S(2)}) copy-start(bf16[128,2,64,128]{3,2,1,0:T(8,128)(2,1)S(1)} %get-tuple-element.14) | copy-start | bytes 12582916
  178.4 9.9 %copy-start.14 = (bf16[128,2,64,128]{3,2,1,0:T(8,128)(2,1)S(1)}, bf16[128,2,64,128]{3,2,1,0:T(8,128)(2,1)}, u32[]{:S(2)}) copy-start(bf16[128,2,64,128]{3,2,1,0:T(8,128)(2,1)} %get-tuple-element.16) | copy-start | bytes 12582916
  188.3 8.1 %copy-start.16 = (bf16[128,2,64,128]{3,2,1,0:T(8,128)(2,1)S(1)}, bf16[128,2,64,128]{3,2,1,0:T(8,128)(2,1)}, u32[]{:S(2)}) copy-start(bf16[128,2,64,128]{3,2,1,0:T(8,128)(2,1)} %get-tuple-element.47) | copy-start | bytes 12582916
  218.3 5.5 copy-start.22
  218.3 6.4 %copy-start.35 = (bf16[1,128,2,64,128]{4,3,2,1,0:T(8,128)(2,1)S(1)}, bf16[1,128,2,64,128]{4,3,2,1,0:T(8,128)(2,1)}, u32[]{:S(2)}) copy-start(bf16[1,128,2,64,128]{4,3,2,1,0:T(8,128)(2,1)} %param.6) | copy-start | bytes 12582916
  232.6 50.8 %copy-start = (bf16[16384,128]{1,0:T(8,128)(2,1)}, bf16[16384,128]{1,0:T(8,128)(2,1)S(1)}, u32[]{:S(2)}) copy-start(bf16[16384,128]{1,0:T(8,128)(2,1)S(1)} %fusion.5) | copy-start | bytes 12582916
  232.9 8.3 %collective-permute-start.4 = (bf16[128,2,1,128]{3,2,1,0:T(2,128)(2,1)S(1)}, bf16[128,2,1,128]{3,2,1,0:T(2,128)(2,1)S(1)}, u32[]{:S(2)}, u32[]{:S(2)}) collective-permute-start(bf16[128,2,1,128]{3,2,1,0:T(2,128)(2,1)S(1)} %get-tuple-element.33), channel_id=1, source_target_pairs={{0,2},{2,4},{4,6},{1,3},{3,5},{5,7},{8,10},{10,12},{12,14},{9,11},... | collective-permute-start | bytes 196616 | tf_op jit(solution)/shard_map/ppermute | solution.py:15
  237.5 8.1 %collective-permute-start.5 = (bf16[128,2,1,128]{3,2,1,0:T(2,128)(2,1)S(1)}, bf16[128,2,1,128]{3,2,1,0:T(2,128)(2,1)S(1)}, u32[]{:S(2)}, u32[]{:S(2)}) collective-permute-start(bf16[128,2,1,128]{3,2,1,0:T(2,128)(2,1)S(1)} %get-tuple-element.34), channel_id=1, source_target_pairs={{2,0},{4,2},{6,4},{3,1},{5,3},{7,5},{10,8},{12,10},{14,12},{11,9},... | collective-permute-start | bytes 196616 | tf_op jit(solution)/shard_map/ppermute | solution.py:17
  245.7 12.5 %collective-permute-start.6 = (bf16[1,2,66,128]{3,2,1,0:T(8,128)(2,1)S(1)}, bf16[1,2,66,128]{3,2,1,0:T(8,128)(2,1)S(1)}, u32[]{:S(2)}, u32[]{:S(2)}) collective-permute-start(bf16[1,2,66,128]{3,2,1,0:T(8,128)(2,1)S(1)} %get-tuple-element.22), channel_id=1, source_target_pairs={{1,0},{3,2},{5,4},{7,6},{9,8},{11,10},{13,12},{15,14},{17,16},{19,... | collective-permute-start | bytes 101384 | tf_op jit(solution)/shard_map/ppermute | solution.py:17
  247.0 11.2 %collective-permute-start.7 = (bf16[1,2,66,128]{3,2,1,0:T(8,128)(2,1)S(1)}, bf16[1,2,66,128]{3,2,1,0:T(8,128)(2,1)S(1)}, u32[]{:S(2)}, u32[]{:S(2)}) collective-permute-start(bf16[1,2,66,128]{3,2,1,0:T(8,128)(2,1)S(1)} %get-tuple-element.23), channel_id=1, source_target_pairs={{0,1},{2,3},{4,5},{6,7},{8,9},{10,11},{12,13},{14,15},{16,17},{18,... | collective-permute-start | bytes 101384 | tf_op jit(solution)/shard_map/ppermute | solution.py:15
  271.5 5.7 %copy-start.26 = (bf16[128,2,64,128]{3,2,1,0:T(8,128)(2,1)S(1)}, bf16[128,2,64,128]{3,2,1,0:T(8,128)(2,1)}, u32[]{:S(2)}) copy-start(bf16[128,2,64,128]{3,2,1,0:T(8,128)(2,1)} %get-tuple-element.10) | copy-start | bytes 12582916
  298.2 5.1 copy-start.33
  298.2 5.1 copy-start.32
  298.2 83.9 %all-to-all-start.1 = ((bf16[128,2,64,128]{3,2,1,0:T(8,128)(2,1)}), bf16[128,2,64,128]{3,2,1,0:T(8,128)(2,1)}, u32[]{:S(2)}, u32[]{:S(2)}) async-start(bf16[128,2,64,128]{3,2,1,0:T(8,128)(2,1)} %bitcast.249), calls=%async_computation.1 | async-start | bytes 8388608 | tf_op jit(solution)/shard_map/all_to_all | solution.py:111
  302.9 244.6 %all-reduce.6.cloned.1.call-start = ((), (), s32[]{:S(2)}) async-start(), calls=%async_computation.2 | async-start | bytes 1572864 | tf_op jit(solution)/shard_map/psum | solution.py:137
  303.4 5.9 %copy-start.17 = (bf16[128,2,64,128]{3,2,1,0:T(8,128)(2,1)S(1)}, bf16[128,2,64,128]{3,2,1,0:T(8,128)(2,1)}, u32[]{:S(2)}) copy-start(bf16[128,2,64,128]{3,2,1,0:T(8,128)(2,1)} %get-tuple-element.47) | copy-start | bytes 12582916
  (22 other events, 63.6 us)
Sparse Core Ops, SparseCore 0:
  404.0 143.4 all-reduce.5
where the time goes:
time: 564 us; the launch traced here: 558 us
  waiting for transfers between devices  202 us (36%)
  matrix products  118 us (21%)
  blocking collectives  102 us (18%)
  local copies, waits for them, and re-layouts  59.2 us (10%)
  other arithmetic  40.5 us (7%)
  starting transfers between devices  21.9 us (4%)
  between operations  15 us (3%)
    psum x1, waiting for transfers between devices, shards(): lax.psum((temporal_local * scale, spatial_local * scale), ('tm', 'height'...  134 us
    all_to_all x1, blocking collectives, shards(): lax.all_to_all(arranged, ('tm', 'height'), split_axis=0, concat_axis=0, t...  102 us
    dot_general x9, matrix products, spatial_forward(): jnp.dot(piece, weights[row_off, col_off], preferred_element_type=jnp.floa...  57.8 us
    all_to_all x1, waiting for transfers between devices, shards(): lax.all_to_all(grad_act_space, ('tm', 'height'), split_axis=0, concat_axi...  55.2 us
    concatenate x4, other arithmetic, with_halo(): jnp.concatenate([lax.ppermute(tail, axis, [(i, (i + 1) % count) for i in...  29.5 us
    slice x1, local copies, waits for them, and re-layouts, spatial_forward(): piece = flatten(padded[col_off:col_off + cols, :, row_off:row_off + rows])  21.7 us
    dot_general x9, matrix products, shards(): jnp.dot(piece, spatial_weight[row_off, col_off].T, preferred_element_type...  20.2 us
    unnamed x74, local copies, waits for them, and re-layouts  19.8 us
  transfers between devices with their start and end apart: 10, of which 6 were waited for; matrix products, arithmetic and copies ran while one was open for 8% of the time, Pallas kernels for 0%

commit v1 on v0

v1 whole, which is shorter than its diff:
```python
import functools

import jax
import jax.numpy as jnp
from jax import lax
from jax.experimental import pallas as pl
from jax.experimental.pallas import tpu as pltpu
from jax.sharding import PartitionSpec as P

MESH_AXES = ("tm", "height", "width")
VMEM = 40 * 1024 * 1024


def frame_masks(lengths, frames):
    ends = jnp.cumsum(lengths, dtype=jnp.int32)
    starts = ends - lengths
    frame_index = jnp.arange(frames, dtype=jnp.int32)
    inside = (frame_index[:, None] >= starts[None, :]) & (frame_index[:, None] < ends[None, :])
    first = jnp.sum(jnp.where(inside, starts[None, :], 0), axis=1, dtype=jnp.int32)
    return jnp.stack([frame_index - lag >= first for lag in range(3)]).astype(jnp.bfloat16)


def column_neighbours(first, last):
    n_tm, n_height, n_width = (lax.axis_size(axis) for axis in MESH_AXES)
    blocks = n_tm * n_height
    place = [(pos % blocks) * n_width + pos // blocks for pos in range(blocks * n_width)]
    pairs = list(zip(place[:-1], place[1:]))
    left = lax.ppermute(last, MESH_AXES, pairs)
    right = lax.ppermute(first, MESH_AXES, [(b, a) for a, b in pairs])
    return left, right


def block_table(rows, cols, entry):
    blocks = [[entry(i, j) for j in range(cols)] for i in range(rows)]
    some = next(b for line in blocks for b in line if b is not None)
    zero = jnp.zeros_like(some)
    return jnp.concatenate(
        [jnp.concatenate([zero if b is None else b for b in line], axis=-1) for line in blocks],
        axis=-2,
    )


def row_shifts(block, rows):
    index = lax.broadcasted_iota(jnp.int32, block.shape, 0)
    above = jnp.where(index == 0, 0.0, pltpu.roll(block, 1, 0))
    below = jnp.where(index == rows - 1, 0.0, pltpu.roll(block, rows - 1, 0))
    return above.astype(jnp.bfloat16), below.astype(jnp.bfloat16)


def lanes(parts):
    return parts[0] if len(parts) == 1 else jnp.concatenate(parts, axis=1)


def forward_kernel(group, width, lag, *refs):
    now, before = refs[:group], refs[group : 2 * group]
    left, left_before, right, right_before, temporal, spatial, slope, cube, held = refs[2 * group :]
    step = pl.program_id(1)
    rows, chans = slope.shape[2], slope.shape[3]
    sources = []
    for e in range(group):
        ext = step * group + e
        line = []
        for ours, l_ref, r_ref in ((before[e], left_before, right_before), (now[e], left, right)):
            for frame in range(2):
                tile = ours[0, frame]
                tile = jnp.where(ext == 0, l_ref[0, frame], tile)
                tile = jnp.where(ext == width + 1, r_ref[0, frame], tile)
                line.append(tile)
        sources.append(lanes(line))
    mixed = jnp.dot(
        jnp.concatenate(sources, axis=0), temporal[0], preferred_element_type=jnp.float32
    ).astype(jnp.bfloat16)
    for e in range(group):
        act = mixed[e * rows : (e + 1) * rows]
        above, below = row_shifts(act.astype(jnp.float32), rows)
        for frame in range(2):
            at = slice(frame * chans, (frame + 1) * chans)
            value = lanes([above[:, at], act[:, at], below[:, at]])
            held[step * group + e, frame] = value
            cube[e, frame] = value

    @pl.when(step >= lag)
    def _():
        base = (step - lag) * group
        source = lanes([held[base + k].reshape(2 * rows, 3 * chans) for k in range(group + 2)])
        pre = jnp.dot(source, spatial[...], preferred_element_type=jnp.float32)
        sig = jax.nn.sigmoid(pre)
        value = sig * (1.0 + pre * (1.0 - sig))
        for e in range(group):
            slope[e] = value[:, e * chans : (e + 1) * chans].reshape(2, rows, chans)


def forward(video, left, right, temporal, spatial, group):
    width, frames, rows, chans = video.shape
    lag = 2 // group
    steps = (width + 2) // group

    def own(e, back):
        return pl.BlockSpec(
            (1, 2, rows, chans),
            lambda p, j: (
                jnp.clip(j * group + e - 1, 0, width - 1),
                jnp.maximum(p - back, 0),
                0,
                0,
            ),
        )

    def edge(back):
        return pl.BlockSpec((1, 2, rows, chans), lambda p, j: (0, jnp.maximum(p - back, 0), 0, 0))

    pixels = width * frames * rows
    return pl.pallas_call(
        functools.partial(forward_kernel, group, width, lag),
        grid=(frames // 2, steps),
        in_specs=[own(e, 0) for e in range(group)]
        + [own(e, 1) for e in range(group)]
        + [
            edge(0),
            edge(1),
            edge(0),
            edge(1),
            pl.BlockSpec((1, 4 * chans, 2 * chans), lambda p, j: (p, 0, 0)),
            pl.BlockSpec(spatial.shape, lambda p, j: (0, 0)),
        ],
        out_specs=[
            pl.BlockSpec(
                (group, 2, rows, chans), lambda p, j: (jnp.maximum(j - lag, 0), p, 0, 0)
            ),
            pl.BlockSpec((group, 2, rows, 3 * chans), lambda p, j: (j, p, 0, 0)),
        ],
        out_shape=[
            jax.ShapeDtypeStruct((width, frames, rows, chans), jnp.float32),
            jax.ShapeDtypeStruct((width + 2, frames, rows, 3 * chans), jnp.bfloat16),
        ],
        scratch_shapes=[pltpu.VMEM((width + 2, 2, rows, 3 * chans), jnp.bfloat16)],
        compiler_params=pltpu.CompilerParams(vmem_limit_bytes=VMEM),
        cost_estimate=pl.CostEstimate(
            flops=pixels * chans * chans * 2 * 24,
            bytes_accessed=pixels * chans * 14,
            transcendentals=pixels * chans,
        ),
    )(*([video] * (2 * group)), left, left, right, right, temporal, spatial)


def slope_kernel(group, extra, *refs):
    grads, slope = refs[:2]
    cubes = refs[2 : 2 + extra]
    delta, total = refs[2 + extra :]
    bands, band = grads.shape[1], grads.shape[4]
    rows, chans = slope.shape[2], slope.shape[3]
    for e in range(group):
        for frame in range(2):
            for b in range(bands):
                at = slice(b * band, (b + 1) * band)
                value = grads[0, b, e, frame].astype(jnp.float32) * slope[e, frame, at]
                delta[e, frame, at] = value.astype(jnp.bfloat16)
    first = (pl.program_id(0) == 0) & (pl.program_id(1) == 0)

    @pl.when(first)
    def _():
        total[...] = jnp.zeros_like(total)

    own = lanes([delta[e].reshape(2 * rows, chans) for e in range(group)])
    source = lanes(
        [
            cubes[k // group][k % group].reshape(2 * rows, 3 * chans)
            for k in range(group + 2)
        ]
    )
    total[...] += lax.dot_general(
        own, source, (((0,), (0,)), ((), ())), preferred_element_type=jnp.float32
    )


def slopes(received, slope, cube, group):
    width, frames, rows, chans = slope.shape
    bands, band = received.shape[1], received.shape[4]
    extra = 2 // group + 1
    pixels = width * frames * rows
    return pl.pallas_call(
        functools.partial(slope_kernel, group, extra),
        grid=(frames // 2, width // group),
        in_specs=[
            pl.BlockSpec((1, bands, group, 2, band, chans), lambda p, i: (p, 0, i, 0, 0, 0)),
            pl.BlockSpec((group, 2, rows, chans), lambda p, i: (i, p, 0, 0)),
        ]
        + [
            pl.BlockSpec(
                (group, 2, rows, 3 * chans), functools.partial(lambda k, p, i: (i + k, p, 0, 0), k)
            )
            for k in range(extra)
        ],
        out_specs=[
            pl.BlockSpec((group, 2, rows, chans), lambda p, i: (i, p, 0, 0)),
            pl.BlockSpec((group * chans, (group + 2) * 3 * chans), lambda p, i: (0, 0)),
        ],
        out_shape=[
            jax.ShapeDtypeStruct((width, frames, rows, chans), jnp.bfloat16),
            jax.ShapeDtypeStruct((group * chans, (group + 2) * 3 * chans), jnp.float32),
        ],
        compiler_params=pltpu.CompilerParams(vmem_limit_bytes=VMEM),
        cost_estimate=pl.CostEstimate(
            flops=pixels * chans * chans * 2 * 18,
            bytes_accessed=pixels * chans * 20,
            transcendentals=0,
        ),
    )(received, slope, *([cube] * extra))


def backward_kernel(group, width, lag, *refs):
    now = refs[:group]
    left, right, clip, clip_before, spatial, grad, total, held = refs[group:]
    step = pl.program_id(1)
    rows, chans = grad.shape[2], grad.shape[3]
    for e in range(group):
        ext = step * group + e
        tiles = []
        for frame in range(2):
            tile = now[e][0, frame]
            tile = jnp.where(ext == 0, left[0, frame], tile)
            tiles.append(jnp.where(ext == width + 1, right[0, frame], tile))
        delta = lanes(tiles)
        above, below = row_shifts(delta.astype(jnp.float32), rows)
        for frame in range(2):
            at = slice(frame * chans, (frame + 1) * chans)
            held[step * group + e, frame] = lanes([below[:, at], delta[:, at], above[:, at]])

    @pl.when(step >= lag)
    def _():
        base = (step - lag) * group
        source = lanes([held[base + k].reshape(2 * rows, 3 * chans) for k in range(group + 2)])
        back = jnp.dot(source, spatial[...], preferred_element_type=jnp.float32)
        back = back.astype(jnp.bfloat16)
        for e in range(group):
            grad[e] = back[:, e * chans : (e + 1) * chans].reshape(2, rows, chans)
        ours = jnp.concatenate(
            [lanes([grad[e, frame] for frame in range(2)]) for e in range(group)], axis=0
        )
        taps = jnp.concatenate(
            [
                lanes([ref[e, frame] for ref in (clip_before, clip) for frame in range(2)])
                for e in range(group)
            ],
            axis=0,
        )
        term = lax.dot_general(
            ours, taps, (((0,), (0,)), ((), ())), preferred_element_type=jnp.float32
        )

        @pl.when(step == lag)
        def _():
            total[0] = term

        @pl.when(step > lag)
        def _():
            total[0] += term


def backward(delta, left, right, video, spatial, group):
    width, frames, rows, chans = video.shape
    lag = 2 // group
    steps = (width + 2) // group

    def own(e):
        return pl.BlockSpec(
            (1, 2, rows, chans),
            lambda p, j: (jnp.clip(j * group + e - 1, 0, width - 1), p, 0, 0),
        )

    edge = pl.BlockSpec((1, 2, rows, chans), lambda p, j: (0, p, 0, 0))
    pixels = width * frames * rows
    return pl.pallas_call(
        functools.partial(backward_kernel, group, width, lag),
        grid=(frames // 2, steps),
        in_specs=[own(e) for e in range(group)]
        + [
            edge,
            edge,
            pl.BlockSpec((group, 2, rows, chans), lambda p, j: (jnp.maximum(j - lag, 0), p, 0, 0)),
            pl.BlockSpec(
                (group, 2, rows, chans),
                lambda p, j: (jnp.maximum(j - lag, 0), jnp.maximum(p - 1, 0), 0, 0),
            ),
            pl.BlockSpec(spatial.shape, lambda p, j: (0, 0)),
        ],
        out_specs=[
            pl.BlockSpec(
                (group, 2, rows, chans), lambda p, j: (jnp.maximum(j - lag, 0), p, 0, 0)
            ),
            pl.BlockSpec((1, 2 * chans, 4 * chans), lambda p, j: (p, 0, 0)),
        ],
        out_shape=[
            jax.ShapeDtypeStruct((width, frames, rows, chans), jnp.bfloat16),
            jax.ShapeDtypeStruct((frames // 2, 2 * chans, 4 * chans), jnp.float32),
        ],
        scratch_shapes=[pltpu.VMEM((width + 2, 2, rows, 3 * chans), jnp.bfloat16)],
        compiler_params=pltpu.CompilerParams(vmem_limit_bytes=VMEM),
        cost_estimate=pl.CostEstimate(
            flops=pixels * chans * chans * 2 * 24,
            bytes_accessed=pixels * chans * 8,
            transcendentals=0,
        ),
    )(*([delta] * group), left, right, video, video, spatial)


def video_kernel(now, after, weights, out):
    cols, _, rows, chans = now.shape
    source = jnp.concatenate(
        [
            lanes([ref[e, frame] for ref in (now, after) for frame in range(2)])
            for e in range(cols)
        ],
        axis=0,
    )
    value = jnp.dot(source, weights[0], preferred_element_type=jnp.float32).astype(jnp.bfloat16)
    for e in range(cols):
        for frame in range(2):
            out[e, frame] = value[e * rows : (e + 1) * rows, frame * chans : (frame + 1) * chans]


def video_gradient(grad, weights):
    width, frames, rows, chans = grad.shape
    cols = 4 if width % 4 == 0 else 1
    last = frames // 2 - 1
    pixels = width * frames * rows
    return pl.pallas_call(
        video_kernel,
        grid=(frames // 2, width // cols),
        in_specs=[
            pl.BlockSpec((cols, 2, rows, chans), lambda p, i: (i, p, 0, 0)),
            pl.BlockSpec((cols, 2, rows, chans), lambda p, i: (i, jnp.minimum(p + 1, last), 0, 0)),
            pl.BlockSpec((1, 4 * chans, 2 * chans), lambda p, i: (p, 0, 0)),
        ],
        out_specs=pl.BlockSpec((cols, 2, rows, chans), lambda p, i: (i, p, 0, 0)),
        out_shape=jax.ShapeDtypeStruct(grad.shape, jnp.bfloat16),
        compiler_params=pltpu.CompilerParams(vmem_limit_bytes=VMEM),
        cost_estimate=pl.CostEstimate(
            flops=pixels * chans * chans * 2 * 6,
            bytes_accessed=pixels * chans * 6,
            transcendentals=0,
        ),
    )(grad, grad, weights)


def exchanged(axis, parts):
    count = lax.axis_size(axis)
    return [
        lax.ppermute(parts(s), axis, [(i, i ^ s) for i in range(count)]) for s in range(1, count)
    ]


def sum_over_devices(local):
    def scatter(value, axis):
        me = lax.axis_index(axis)
        blocks = value.reshape(lax.axis_size(axis), -1, value.shape[-1])
        pick = lambda s: lax.dynamic_index_in_dim(blocks, me ^ s, 0, keepdims=False)
        return functools.reduce(jnp.add, exchanged(axis, pick), pick(0))

    def spread(value, axis):
        count = lax.axis_size(axis)
        me = lax.axis_index(axis)
        parts = jnp.stack([value] + exchanged(axis, lambda s: value))
        order = jnp.arange(count, dtype=jnp.int32) ^ me
        return jnp.take(parts, order, axis=0).reshape(-1, value.shape[-1])

    value = scatter(scatter(local, "width"), "height")
    value = functools.reduce(jnp.add, exchanged("tm", lambda s: value), value)
    return spread(spread(value, "height"), "width")


def shards(video, out_grad, lengths, temporal_weight, spatial_weight):
    clip = video[0]
    width, frames, rows, chans = clip.shape
    n_tm = lax.axis_size("tm")
    n_height = lax.axis_size("height")
    frames_dev, rows_dev = out_grad.shape[2], out_grad.shape[3]
    assert frames_dev == 2
    total_cols = out_grad.shape[1] * lax.axis_size("width")
    group = 2 if width % 2 == 0 else 1
    pairs = frames // 2

    received = lax.all_to_all(out_grad[0], ("tm", "height"), split_axis=0, concat_axis=0, tiled=True)
    received = received.reshape(n_tm, n_height, width, frames_dev, rows_dev, chans)
    left, right = column_neighbours(clip[:1], clip[width - 1 :])

    masks = frame_masks(lengths, frames)
    paired = masks.reshape(3, pairs, 2)
    late = jnp.pad(paired, ((0, 0), (0, 1), (0, 0)))

    def tap_block(i, j):
        k = 2 + j - i
        return paired[k, :, j, None, None] * temporal_weight[k] if 0 <= k < 3 else None

    def back_block(i, j):
        k = i - j
        if not 0 <= k < 3:
            return None
        return late[k, i // 2 : i // 2 + pairs, i % 2, None, None] * temporal_weight[k].T

    temporal_mix = block_table(4, 2, tap_block)
    temporal_back = block_table(4, 2, back_block)

    def pre_block(i, j):
        b = i // 3 - j
        return spatial_weight[i % 3, b] if 0 <= b < 3 else None

    def grad_block(i, j):
        b = j + 2 - i // 3
        return spatial_weight[i % 3, b].T if 0 <= b < 3 else None

    spatial_mix = block_table(3 * (group + 2), group, pre_block)
    spatial_back = block_table(3 * (group + 2), group, grad_block)

    slope, cube = forward(clip, left, right, temporal_mix, spatial_mix, group)

    def edge_delta(col):
        grads = received[:, :, col].transpose(0, 2, 1, 3, 4).reshape(1, frames, rows, chans)
        return (grads.astype(jnp.float32) * slope[col][None]).astype(jnp.bfloat16)

    delta_left, delta_right = column_neighbours(edge_delta(0), edge_delta(width - 1))
    delta, spatial_terms = slopes(received, slope, cube, group)

    scale = float(frames * rows * total_cols) ** (-0.5)
    blocks = spatial_terms.reshape(group, chans, group + 2, 3, chans)
    spatial_local = jnp.stack(
        [sum(blocks[j, :, j + b] for j in range(group)) for b in range(3)], axis=2
    )
    spatial_local = (spatial_local * scale).transpose(1, 2, 3, 0).reshape(-1, chans)
    spatial_grad = sum_over_devices(spatial_local).reshape(3, 3, chans, chans)

    grad, temporal_terms = backward(delta, delta_left, delta_right, clip, spatial_back, group)
    video_grad = video_gradient(grad, temporal_back)

    blocks = temporal_terms.reshape(pairs, 2, chans, 4, chans)
    weights = paired.astype(jnp.float32) * scale
    temporal_local = jnp.stack(
        [
            sum(
                jnp.sum(weights[k, :, j, None, None] * blocks[:, j, :, 2 + j - k], axis=0)
                for j in range(2)
            ).T
            for k in range(3)
        ]
    )
    temporal_grad = sum_over_devices(temporal_local.reshape(-1, chans)).reshape(3, chans, chans)
    return video_grad[None], temporal_grad, spatial_grad


def solution(mesh):
    placed = (
        P("width", ("tm", "height"), None, None, None),
        P("width", None, "tm", "height", None),
        P(),
        P(),
        P(),
    )
    return jax.shard_map(
        shards,
        mesh=mesh,
        in_specs=placed,
        out_specs=(P("width", ("tm", "height"), None, None, None), P(), P()),
        check_vma=False,
    )
```

time: 564 us -> 266 us (0.47)
  waiting for transfers between devices: 202 us -> 70.6 us
  matrix products: 118 us -> 0 us
  blocking collectives: 102 us -> 0 us
  Pallas kernels: 0 us -> 71.4 us
  starting transfers between devices: 21.9 us -> 85.9 us
  local copies, waits for them, and re-layouts: 59.2 us -> 27.1 us
  other arithmetic: 40.5 us -> 8.93 us
  between operations: 15 us -> 1.59 us
    psum x1 -> x0, waiting for transfers between devices: 134 us -> none  [shards(): lax.psum((temporal_local * scale, spatial_local * scale), ('tm', 'height'...]
    dot_general x34 -> x0, matrix products: 110 us -> none  [the longest x9 57.8 us: spatial_forward(): jnp.dot(piece, weights[row_off, col_off], preferred_element_type=jnp.floa...]
    all_to_all x1 -> x0, blocking collectives: 102 us -> none  [shards(): lax.all_to_all(arranged, ('tm', 'height'), split_axis=0, concat_axis=0, t...]
    pallas_call x0 -> x4, Pallas kernels: none -> 71.4 us  [the longest x1 25.2 us: backward(): pl.pallas_call(functools.partial(backward_kernel, group, width, lag), gri...]
    ppermute x8 -> x26, starting transfers between devices: 16.9 us -> 77.6 us  [the longest x22 67.5 us: exchanged(): lax.ppermute(parts(s), axis, [(i, i ^ s) for i in range(count)])]
    ppermute x8 -> x26, waiting for transfers between devices: 12.4 us -> 68.5 us  [the longest x2 38.8 us: column_neighbours(): right = lax.ppermute(first, MESH_AXES, [(b, a) for a, b in pairs])]
    all_to_all x1, waiting for transfers between devices: 55.2 us -> 2.15 us  [shards(): lax.all_to_all(out_grad[0], ('tm', 'height'), split_axis=0, concat_axis=0...]
    concatenate x4 -> x2, other arithmetic: 29.5 us -> 0.18 us  [block_table(): jnp.concatenate([jnp.concatenate([zero if b is None else b for b in line]...]
  transfers between devices with their start and end apart: 10 -> 27, of which waited for: 6 -> 12; matrix products, arithmetic and copies ran while one was open for 8% -> 9% of each run, Pallas kernels for 0% -> 19%
where the time goes in v1:
time: 266 us
  starting transfers between devices  85.9 us (32%)
  Pallas kernels  71.4 us (27%)
  waiting for transfers between devices  70.6 us (27%)
  local copies, waits for them, and re-layouts  27.1 us (10%)
  other arithmetic  8.93 us (3%)
    ppermute x22, starting transfers between devices, exchanged(): lax.ppermute(parts(s), axis, [(i, i ^ s) for i in range(count)])  67.5 us
    ppermute x2, waiting for transfers between devices, column_neighbours(): right = lax.ppermute(first, MESH_AXES, [(b, a) for a, b in pairs])  38.8 us
    pallas_call x1, Pallas kernels, backward(): pl.pallas_call(functools.partial(backward_kernel, group, width, lag), gri...  25.2 us
    pallas_call x1, Pallas kernels, forward(): pl.pallas_call(functools.partial(forward_kernel, group, width, lag), grid...  20.2 us
    pallas_call x1, Pallas kernels, slopes(): pl.pallas_call(functools.partial(slope_kernel, group, extra), grid=(frame...  20.2 us
    ppermute x22, waiting for transfers between devices, exchanged(): lax.ppermute(parts(s), axis, [(i, i ^ s) for i in range(count)])  20.1 us
    ppermute x2, waiting for transfers between devices, column_neighbours(): left = lax.ppermute(last, MESH_AXES, pairs)  9.63 us
    all_to_all x1, starting transfers between devices, shards(): lax.all_to_all(out_grad[0], ('tm', 'height'), split_axis=0, concat_axis=0...  8.38 us
  transfers between devices with their start and end apart: 27, of which 12 were waited for; matrix products, arithmetic and copies ran while one was open for 9% of the time, Pallas kernels for 19%

profile of v1, /device:TPU:0, one launch (start us, length us, event | category | flops | bytes accessed | tf_op | source)
XLA Modules:
  0.0 265.6 jit_solution(799680841501005003)
XLA Ops:
  0.6 8.4 %all-to-all-start = ((bf16[128,2,64,128]{3,2,1,0:T(8,128)(2,1)}), bf16[128,2,64,128]{3,2,1,0:T(8,128)(2,1)}, u32[]{:S(2)}, u32[]{:S(2)}) async-start(bf16[128,2,64,128]{3,2,1,0:T(8,128)(2,1)} %bitcast.182), calls=%async_computation | async-start | bytes 8388608 | tf_op jit(solution)/shard_map/all_to_all | solution.py:383
  9.0 2.1 slice_bitcast_fusion.2
  11.2 3.8 %collective-permute-start = (bf16[1,8,256,128]{3,2,1,0:T(8,128)(2,1)}, bf16[1,8,256,128]{3,2,1,0:T(8,128)(2,1)S(1)}, u32[]{:S(2)}, u32[]{:S(2)}) collective-permute-start(bf16[1,8,256,128]{3,2,1,0:T(8,128)(2,1)} %get-tuple-element.35), channel_id=1, source_target_pairs={{0,2},{2,4},{4,6},{6,8},{8,10},{10,12},{12,14},{14,16},{16,18},{18... | collective-permute-start | bytes 1572872 | tf_op jit(solution)/shard_map/ppermute | solution.py:28
  23.5 9.6 %collective-permute-done.refs_4_.refs_5_ = bf16[1,8,256,128]{3,2,1,0:T(8,128)(2,1)S(1)} collective-permute-done((bf16[1,8,256,128]{3,2,1,0:T(8,128)(2,1)}, bf16[1,8,256,128]{3,2,1,0:T(8,128)(2,1)S(1)}, u32[]{:S(2)}, u32[]{:S(2)}) %collective-permute-start) | collective-permute-done | bytes 524320 | tf_op jit(solution)/shard_map/ppermute | solution.py:28
  33.1 38.8 %collective-permute-done.1.refs_6_.refs_7_ = bf16[1,8,256,128]{3,2,1,0:T(8,128)(2,1)S(1)} collective-permute-done((bf16[1,8,256,128]{3,2,1,0:T(8,128)(2,1)S(1)}, bf16[1,8,256,128]{3,2,1,0:T(8,128)(2,1)S(1)}, u32[]{:S(2)}, u32[]{:S(2)}) %collective-permute-start.1) | collective-permute-done | bytes 524320 | tf_op jit(solution)/shard_map/ppermute | solution.py:29
  71.9 20.2 %shard_map.76 = (f32[8,8,256,128]{3,2,1,0:T(8,128)}, bf16[10,8,256,384]{3,2,1,0:T(8,128)(2,1)}) custom-call(bf16[8,8,256,128]{3,2,1,0:T(8,128)(2,1)S(1)} %bitcast.176, bf16[8,8,256,128]{3,2,1,0:T(8,128)(2,1)S(1)} %bitcast.177, bf16[8,8,256,128]{3,2,1,0:T(8,128)(2,1)S(1)} %bitcast.178, bf16[8,8,256,128]{3,2,1,0:T(8,128)(2,1)S(1)} %bitcast.179, ...), custom_call_target="tpu_custom_call" | custom-call | flops 12884901888 | bytes 29360128 | tf_op jit(solution)/shard_map/pallas_call | solution.py:113
  92.1 2.2 all-to-all-done
  94.2 20.2 %shard_map.77 = (bf16[8,8,256,128]{3,2,1,0:T(8,128)(2,1)S(1)}, f32[256,1536]{1,0:T(8,128)S(1)}) custom-call(bf16[4,4,8,2,64,128]{5,4,3,2,1,0:T(8,128)(2,1)} %bitcast.1.refs_0_, f32[8,8,256,128]{3,2,1,0:T(8,128)} %get-tuple-element.9.refs_1_, bf16[10,8,256,384]{3,2,1,0:T(8,128)(2,1)} %get-tuple-element.10.refs_2_.refs_3_, ...), custom_call_target="tpu_custom_call" | custom-call | flops 9663676416 | bytes 41943040 | tf_op jit(solution)/shard_map/pallas_call | solution.py:181
  114.4 2.0 copy-done.5
  118.0 2.1 reshape.334
  121.2 16.8 %collective-permute-start.15 = (f32[576,128]{1,0:T(8,128)S(1)}, f32[576,128]{1,0:T(8,128)S(1)}, u32[]{:S(2)}, u32[]{:S(2)}) collective-permute-start(f32[576,128]{1,0:T(8,128)S(1)} %dynamic-slice_bitcast_fusion), channel_id=1, source_target_pairs={{0,1},{1,0},{2,3},{3,2},{4,5},{5,4},{6,7},{7,6},{8,9},{9,8},{10,11... | collective-permute-start | bytes 884744 | tf_op jit(solution)/shard_map/ppermute | solution.py:349
  140.5 4.3 %collective-permute-start.17 = (f32[144,128]{1,0:T(8,128)S(1)}, f32[144,128]{1,0:T(8,128)S(1)}, u32[]{:S(2)}, u32[]{:S(2)}) collective-permute-start(f32[144,128]{1,0:T(8,128)S(1)} %get-tuple-element.49), channel_id=1, source_target_pairs={{0,4},{2,6},{4,0},{6,2},{1,5},{3,7},{5,1},{7,3},{8,12},{10,14},{12... | collective-permute-start | bytes 221192 | tf_op jit(solution)/shard_map/ppermute | solution.py:349
  146.7 3.5 %collective-permute-start.2 = (bf16[1,8,256,128]{3,2,1,0:T(8,128)(2,1)S(1)}, bf16[1,8,256,128]{3,2,1,0:T(8,128)(2,1)S(1)}, u32[]{:S(2)}, u32[]{:S(2)}) collective-permute-start(bf16[1,8,256,128]{3,2,1,0:T(8,128)(2,1)S(1)} %get-tuple-element.31), channel_id=1, source_target_pairs={{0,2},{2,4},{4,6},{6,8},{8,10},{10,12},{12,14},{14,16},{16,18},{18... | collective-permute-start | bytes 1572872 | tf_op jit(solution)/shard_map/ppermute | solution.py:28
  151.8 25.6 %collective-permute-start.19 = (f32[144,128]{1,0:T(8,128)S(1)}, f32[144,128]{1,0:T(8,128)S(1)}, u32[]{:S(2)}, u32[]{:S(2)}) collective-permute-start(f32[144,128]{1,0:T(8,128)S(1)} %fusion.12), channel_id=1, source_target_pairs={{0,8},{8,0},{16,24},{24,16},{1,9},{9,1},{17,25},{25,17},{2,10},{10... | collective-permute-start | bytes 221192 | tf_op jit(solution)/shard_map/ppermute | solution.py:349
  177.4 4.0 %collective-permute-start.20 = (f32[144,128]{1,0:T(8,128)S(1)}, f32[144,128]{1,0:T(8,128)S(1)}, u32[]{:S(2)}, u32[]{:S(2)}) collective-permute-start(f32[144,128]{1,0:T(8,128)S(1)} %fusion.12), channel_id=1, source_target_pairs={{0,16},{8,24},{16,0},{24,8},{1,17},{9,25},{17,1},{25,9},{2,18},{10... | collective-permute-start | bytes 221192 | tf_op jit(solution)/shard_map/ppermute | solution.py:349
  182.8 7.0 %collective-permute-done.19 = f32[144,128]{1,0:T(8,128)S(1)} collective-permute-done((f32[144,128]{1,0:T(8,128)S(1)}, f32[144,128]{1,0:T(8,128)S(1)}, u32[]{:S(2)}, u32[]{:S(2)}) %collective-permute-start.19) | collective-permute-done | bytes 73760 | tf_op jit(solution)/shard_map/ppermute | solution.py:349
  189.8 7.7 %collective-permute-done.20 = f32[144,128]{1,0:T(8,128)S(1)} collective-permute-done((f32[144,128]{1,0:T(8,128)S(1)}, f32[144,128]{1,0:T(8,128)S(1)}, u32[]{:S(2)}, u32[]{:S(2)}) %collective-permute-start.20) | collective-permute-done | bytes 73760 | tf_op jit(solution)/shard_map/ppermute | solution.py:349
  197.7 3.4 %collective-permute-start.24 = (f32[144,128]{1,0:T(8,128)S(1)}, f32[144,128]{1,0:T(8,128)S(1)}, u32[]{:S(2)}, u32[]{:S(2)}) collective-permute-start(f32[144,128]{1,0:T(8,128)S(1)} %add_add_fusion), channel_id=1, source_target_pairs={{0,6},{2,4},{4,2},{6,0},{1,7},{3,5},{5,3},{7,1},{8,14},{10,12},{12... | collective-permute-start | bytes 221192 | tf_op jit(solution)/shard_map/ppermute | solution.py:349
  201.1 25.2 %shard_map.78 = (bf16[8,8,256,128]{3,2,1,0:T(8,128)(2,1)S(1)}, f32[4,256,512]{2,1,0:T(8,128)S(1)}) custom-call(bf16[8,8,256,128]{3,2,1,0:T(8,128)(2,1)S(1)} %copy-done.6, bf16[8,8,256,128]{3,2,1,0:T(8,128)(2,1)S(1)} %copy-done.6, bf16[1,8,256,128]{3,2,1,0:T(8,128)(2,1)S(1)} %collective-permute-done.2.refs_2_, ...), custom_call_target="tpu_custom_call" | custom-call | flops 12884901888 | bytes 16777216 | tf_op jit(solution)/shard_map/pallas_call | solution.py:273
  230.1 4.6 %fusion.22 = (f32[4,1,128,1,128]{4,3,2,1,0:T(1,128)S(1)}, f32[4,1,128,1,128]{4,3,2,1,0:T(1,128)S(1)}, f32[4,1,128,1,128]{4,3,2,1,0:T(1,128)S(1)}, f32[4,1,128,1,...) fusion(f32[4,2,128,4,128]{4,3,2,1,0:T(4,128)} %reshape.332), kind=kLoop, calls=%fused_computation.148 | loop fusion | bytes 3145728 | tf_op jit(solution)/shard_map/slice | solution.py:440
  237.6 2.9 %collective-permute-start.7 = (f32[48,128]{1,0:T(8,128)S(1)}, f32[48,128]{1,0:T(8,128)S(1)}, u32[]{:S(2)}, u32[]{:S(2)}) collective-permute-start(f32[48,128]{1,0:T(8,128)S(1)} %get-tuple-element.60), channel_id=1, source_target_pairs={{0,6},{2,4},{4,2},{6,0},{1,7},{3,5},{5,3},{7,1},{8,14},{10,12},{12... | collective-permute-start | bytes 73736 | tf_op jit(solution)/shard_map/ppermute | solution.py:349
  243.9 3.0 %collective-permute-start.9 = (f32[48,128]{1,0:T(8,128)S(1)}, f32[48,128]{1,0:T(8,128)S(1)}, u32[]{:S(2)}, u32[]{:S(2)}) collective-permute-start(f32[48,128]{1,0:T(8,128)S(1)} %fusion.14), channel_id=1, source_target_pairs={{0,16},{8,24},{16,0},{24,8},{1,17},{9,25},{17,1},{25,9},{2,18},{10... | collective-permute-start | bytes 73736 | tf_op jit(solution)/shard_map/ppermute | solution.py:349
  252.5 2.2 copy-done.1
  254.7 5.8 %shard_map.79 = bf16[8,8,256,128]{3,2,1,0:T(8,128)(2,1)} custom-call(bf16[8,8,256,128]{3,2,1,0:T(8,128)(2,1)S(1)} %copy-done.1, bf16[8,8,256,128]{3,2,1,0:T(8,128)(2,1)S(1)} %copy-done.1, bf16[4,512,256]{2,1,0:T(8,128)(2,1)S(1)} %fusion.9.weights), custom_call_target="tpu_custom_call" | custom-call | flops 3221225472 | bytes 12582912 | tf_op jit(solution)/shard_map/pallas_call | solution.py:327
  (183 shorter events, 38.7 us)
Async XLA Ops:
  0.6 93.6 %all-to-all-start = ((bf16[128,2,64,128]{3,2,1,0:T(8,128)(2,1)}), bf16[128,2,64,128]{3,2,1,0:T(8,128)(2,1)}, u32[]{:S(2)}, u32[]{:S(2)}) async-start(bf16[128,2,64,128]{3,2,1,0:T(8,128)(2,1)} %bitcast.182), calls=%async_computation | async-start | bytes 8388608 | tf_op jit(solution)/shard_map/all_to_all | solution.py:383
  11.2 21.9 %collective-permute-start = (bf16[1,8,256,128]{3,2,1,0:T(8,128)(2,1)}, bf16[1,8,256,128]{3,2,1,0:T(8,128)(2,1)S(1)}, u32[]{:S(2)}, u32[]{:S(2)}) collective-permute-start(bf16[1,8,256,128]{3,2,1,0:T(8,128)(2,1)} %get-tuple-element.35), channel_id=1, source_target_pairs={{0,2},{2,4},{4,6},{6,8},{8,10},{10,12},{12,14},{14,16},{16,18},{18... | collective-permute-start | bytes 1572872 | tf_op jit(solution)/shard_map/ppermute | solution.py:28
  15.0 56.9 %collective-permute-start.1 = (bf16[1,8,256,128]{3,2,1,0:T(8,128)(2,1)S(1)}, bf16[1,8,256,128]{3,2,1,0:T(8,128)(2,1)S(1)}, u32[]{:S(2)}, u32[]{:S(2)}) collective-permute-start(bf16[1,8,256,128]{3,2,1,0:T(8,128)(2,1)S(1)} %get-tuple-element.34), channel_id=1, source_target_pairs={{2,0},{4,2},{6,4},{8,6},{10,8},{12,10},{14,12},{16,14},{18,16},{20... | collective-permute-start | bytes 1572872 | tf_op jit(solution)/shard_map/ppermute | solution.py:29
  121.2 19.1 %collective-permute-start.15 = (f32[576,128]{1,0:T(8,128)S(1)}, f32[576,128]{1,0:T(8,128)S(1)}, u32[]{:S(2)}, u32[]{:S(2)}) collective-permute-start(f32[576,128]{1,0:T(8,128)S(1)} %dynamic-slice_bitcast_fusion), channel_id=1, source_target_pairs={{0,1},{1,0},{2,3},{3,2},{4,5},{5,4},{6,7},{7,6},{8,9},{9,8},{10,11... | collective-permute-start | bytes 884744 | tf_op jit(solution)/shard_map/ppermute | solution.py:349
  140.4 11.4 %collective-permute-start.16 = (f32[144,128]{1,0:T(8,128)S(1)}, f32[144,128]{1,0:T(8,128)S(1)}, u32[]{:S(2)}, u32[]{:S(2)}) collective-permute-start(f32[144,128]{1,0:T(8,128)S(1)} %get-tuple-element.47), channel_id=1, source_target_pairs={{0,2},{2,0},{4,6},{6,4},{1,3},{3,1},{5,7},{7,5},{8,10},{10,8},{12,... | collective-permute-start | bytes 221192 | tf_op jit(solution)/shard_map/ppermute | solution.py:349
  140.5 11.3 %collective-permute-start.17 = (f32[144,128]{1,0:T(8,128)S(1)}, f32[144,128]{1,0:T(8,128)S(1)}, u32[]{:S(2)}, u32[]{:S(2)}) collective-permute-start(f32[144,128]{1,0:T(8,128)S(1)} %get-tuple-element.49), channel_id=1, source_target_pairs={{0,4},{2,6},{4,0},{6,2},{1,5},{3,7},{5,1},{7,3},{8,12},{10,14},{12... | collective-permute-start | bytes 221192 | tf_op jit(solution)/shard_map/ppermute | solution.py:349
  144.8 7.0 %collective-permute-start.18 = (f32[144,128]{1,0:T(8,128)S(1)}, f32[144,128]{1,0:T(8,128)S(1)}, u32[]{:S(2)}, u32[]{:S(2)}) collective-permute-start(f32[144,128]{1,0:T(8,128)S(1)} %get-tuple-element.48), channel_id=1, source_target_pairs={{0,6},{2,4},{4,2},{6,0},{1,7},{3,5},{5,3},{7,1},{8,14},{10,12},{12... | collective-permute-start | bytes 221192 | tf_op jit(solution)/shard_map/ppermute | solution.py:349
  146.7 54.4 %collective-permute-start.2 = (bf16[1,8,256,128]{3,2,1,0:T(8,128)(2,1)S(1)}, bf16[1,8,256,128]{3,2,1,0:T(8,128)(2,1)S(1)}, u32[]{:S(2)}, u32[]{:S(2)}) collective-permute-start(bf16[1,8,256,128]{3,2,1,0:T(8,128)(2,1)S(1)} %get-tuple-element.31), channel_id=1, source_target_pairs={{0,2},{2,4},{4,6},{6,8},{8,10},{10,12},{12,14},{14,16},{16,18},{18... | collective-permute-start | bytes 1572872 | tf_op jit(solution)/shard_map/ppermute | solution.py:28
  150.3 50.8 %collective-permute-start.3 = (bf16[1,8,256,128]{3,2,1,0:T(8,128)(2,1)S(1)}, bf16[1,8,256,128]{3,2,1,0:T(8,128)(2,1)S(1)}, u32[]{:S(2)}, u32[]{:S(2)}) collective-permute-start(bf16[1,8,256,128]{3,2,1,0:T(8,128)(2,1)S(1)} %get-tuple-element.30), channel_id=1, source_target_pairs={{2,0},{4,2},{6,4},{8,6},{10,8},{12,10},{14,12},{16,14},{18,16},{20... | collective-permute-start | bytes 1572872 | tf_op jit(solution)/shard_map/ppermute | solution.py:29
  151.8 38.0 %collective-permute-start.19 = (f32[144,128]{1,0:T(8,128)S(1)}, f32[144,128]{1,0:T(8,128)S(1)}, u32[]{:S(2)}, u32[]{:S(2)}) collective-permute-start(f32[144,128]{1,0:T(8,128)S(1)} %fusion.12), channel_id=1, source_target_pairs={{0,8},{8,0},{16,24},{24,16},{1,9},{9,1},{17,25},{25,17},{2,10},{10... | collective-permute-start | bytes 221192 | tf_op jit(solution)/shard_map/ppermute | solution.py:349
  177.4 20.1 %collective-permute-start.20 = (f32[144,128]{1,0:T(8,128)S(1)}, f32[144,128]{1,0:T(8,128)S(1)}, u32[]{:S(2)}, u32[]{:S(2)}) collective-permute-start(f32[144,128]{1,0:T(8,128)S(1)} %fusion.12), channel_id=1, source_target_pairs={{0,16},{8,24},{16,0},{24,8},{1,17},{9,25},{17,1},{25,9},{2,18},{10... | collective-permute-start | bytes 221192 | tf_op jit(solution)/shard_map/ppermute | solution.py:349
  181.4 16.1 %collective-permute-start.21 = (f32[144,128]{1,0:T(8,128)S(1)}, f32[144,128]{1,0:T(8,128)S(1)}, u32[]{:S(2)}, u32[]{:S(2)}) collective-permute-start(f32[144,128]{1,0:T(8,128)S(1)} %fusion.12), channel_id=1, source_target_pairs={{0,24},{8,16},{16,8},{24,0},{1,25},{9,17},{17,9},{25,1},{2,26},{10... | collective-permute-start | bytes 221192 | tf_op jit(solution)/shard_map/ppermute | solution.py:349
  197.6 38.1 %collective-permute-start.22 = (f32[144,128]{1,0:T(8,128)S(1)}, f32[144,128]{1,0:T(8,128)S(1)}, u32[]{:S(2)}, u32[]{:S(2)}) collective-permute-start(f32[144,128]{1,0:T(8,128)S(1)} %add_add_fusion), channel_id=1, source_target_pairs={{0,2},{2,0},{4,6},{6,4},{1,3},{3,1},{5,7},{7,5},{8,10},{10,8},{12,... | collective-permute-start | bytes 221192 | tf_op jit(solution)/shard_map/ppermute | solution.py:349
  197.6 38.1 %collective-permute-start.23 = (f32[144,128]{1,0:T(8,128)S(1)}, f32[144,128]{1,0:T(8,128)S(1)}, u32[]{:S(2)}, u32[]{:S(2)}) collective-permute-start(f32[144,128]{1,0:T(8,128)S(1)} %add_add_fusion), channel_id=1, source_target_pairs={{0,4},{2,6},{4,0},{6,2},{1,5},{3,7},{5,1},{7,3},{8,12},{10,14},{12... | collective-permute-start | bytes 221192 | tf_op jit(solution)/shard_map/ppermute | solution.py:349
  197.7 38.0 %collective-permute-start.24 = (f32[144,128]{1,0:T(8,128)S(1)}, f32[144,128]{1,0:T(8,128)S(1)}, u32[]{:S(2)}, u32[]{:S(2)}) collective-permute-start(f32[144,128]{1,0:T(8,128)S(1)} %add_add_fusion), channel_id=1, source_target_pairs={{0,6},{2,4},{4,2},{6,0},{1,7},{3,5},{5,3},{7,1},{8,14},{10,12},{12... | collective-permute-start | bytes 221192 | tf_op jit(solution)/shard_map/ppermute | solution.py:349
  237.0 3.9 %collective-permute-start.5 = (f32[48,128]{1,0:T(8,128)S(1)}, f32[48,128]{1,0:T(8,128)S(1)}, u32[]{:S(2)}, u32[]{:S(2)}) collective-permute-start(f32[48,128]{1,0:T(8,128)S(1)} %get-tuple-element.59), channel_id=1, source_target_pairs={{0,2},{2,0},{4,6},{6,4},{1,3},{3,1},{5,7},{7,5},{8,10},{10,8},{12,... | collective-permute-start | bytes 73736 | tf_op jit(solution)/shard_map/ppermute | solution.py:349
  237.6 4.7 %collective-permute-start.7 = (f32[48,128]{1,0:T(8,128)S(1)}, f32[48,128]{1,0:T(8,128)S(1)}, u32[]{:S(2)}, u32[]{:S(2)}) collective-permute-start(f32[48,128]{1,0:T(8,128)S(1)} %get-tuple-element.60), channel_id=1, source_target_pairs={{0,6},{2,4},{4,2},{6,0},{1,7},{3,5},{5,3},{7,1},{8,14},{10,12},{12... | collective-permute-start | bytes 73736 | tf_op jit(solution)/shard_map/ppermute | solution.py:349
  240.7 23.2 %collective-permute-start.25 = (f32[576,128]{1,0:T(8,128)S(1)}, f32[576,128]{1,0:T(8,128)S(1)}, u32[]{:S(2)}, u32[]{:S(2)}) collective-permute-start(f32[576,128]{1,0:T(8,128)S(1)} %bitcast_select_fusion), channel_id=1, source_target_pairs={{0,1},{1,0},{2,3},{3,2},{4,5},{5,4},{6,7},{7,6},{8,9},{9,8},{10,11... | collective-permute-start | bytes 884744 | tf_op jit(solution)/shard_map/ppermute | solution.py:349
  242.4 5.7 %collective-permute-start.10 = (f32[48,128]{1,0:T(8,128)S(1)}, f32[48,128]{1,0:T(8,128)S(1)}, u32[]{:S(2)}, u32[]{:S(2)}) collective-permute-start(f32[48,128]{1,0:T(8,128)S(1)} %fusion.14), channel_id=1, source_target_pairs={{0,24},{8,16},{16,8},{24,0},{1,25},{9,17},{17,9},{25,1},{2,26},{10... | collective-permute-start | bytes 73736 | tf_op jit(solution)/shard_map/ppermute | solution.py:349
  242.5 5.6 %collective-permute-start.8 = (f32[48,128]{1,0:T(8,128)S(1)}, f32[48,128]{1,0:T(8,128)S(1)}, u32[]{:S(2)}, u32[]{:S(2)}) collective-permute-start(f32[48,128]{1,0:T(8,128)S(1)} %fusion.14), channel_id=1, source_target_pairs={{0,8},{8,0},{16,24},{24,16},{1,9},{9,1},{17,25},{25,17},{2,10},{10... | collective-permute-start | bytes 73736 | tf_op jit(solution)/shard_map/ppermute | solution.py:349
  243.9 5.0 %collective-permute-start.9 = (f32[48,128]{1,0:T(8,128)S(1)}, f32[48,128]{1,0:T(8,128)S(1)}, u32[]{:S(2)}, u32[]{:S(2)}) collective-permute-start(f32[48,128]{1,0:T(8,128)S(1)} %fusion.14), channel_id=1, source_target_pairs={{0,16},{8,24},{16,0},{24,8},{1,17},{9,25},{17,1},{25,9},{2,18},{10... | collective-permute-start | bytes 73736 | tf_op jit(solution)/shard_map/ppermute | solution.py:349
  248.9 11.5 %collective-permute-start.11 = (f32[48,128]{1,0:T(8,128)S(1)}, f32[48,128]{1,0:T(8,128)S(1)}, u32[]{:S(2)}, u32[]{:S(2)}) collective-permute-start(f32[48,128]{1,0:T(8,128)S(1)} %add_add_fusion.1), channel_id=1, source_target_pairs={{0,2},{2,0},{4,6},{6,4},{1,3},{3,1},{5,7},{7,5},{8,10},{10,8},{12,... | collective-permute-start | bytes 73736 | tf_op jit(solution)/shard_map/ppermute | solution.py:349
  250.6 9.9 %collective-permute-start.12 = (f32[48,128]{1,0:T(8,128)S(1)}, f32[48,128]{1,0:T(8,128)S(1)}, u32[]{:S(2)}, u32[]{:S(2)}) collective-permute-start(f32[48,128]{1,0:T(8,128)S(1)} %add_add_fusion.1), channel_id=1, source_target_pairs={{0,4},{2,6},{4,0},{6,2},{1,5},{3,7},{5,1},{7,3},{8,12},{10,14},{12... | collective-permute-start | bytes 73736 | tf_op jit(solution)/shard_map/ppermute | solution.py:349
  252.5 8.0 %collective-permute-start.13 = (f32[48,128]{1,0:T(8,128)S(1)}, f32[48,128]{1,0:T(8,128)S(1)}, u32[]{:S(2)}, u32[]{:S(2)}) collective-permute-start(f32[48,128]{1,0:T(8,128)S(1)} %add_add_fusion.1), channel_id=1, source_target_pairs={{0,6},{2,4},{4,2},{6,0},{1,7},{3,5},{5,3},{7,1},{8,14},{10,12},{12... | collective-permute-start | bytes 73736 | tf_op jit(solution)/shard_map/ppermute | solution.py:349
  (20 other events, 237.7 us)

commit v2 on v1

v2 whole, which is shorter than its diff:
```python
import functools

import jax
import jax.numpy as jnp
from jax import lax
from jax.experimental import pallas as pl
from jax.experimental.pallas import tpu as pltpu
from jax.sharding import PartitionSpec as P

MESH_AXES = ("tm", "height", "width")
VMEM = 40 * 1024 * 1024


def frame_masks(lengths, frames):
    ends = jnp.cumsum(lengths, dtype=jnp.int32)
    starts = ends - lengths
    frame_index = jnp.arange(frames, dtype=jnp.int32)
    inside = (frame_index[:, None] >= starts[None, :]) & (frame_index[:, None] < ends[None, :])
    first = jnp.sum(jnp.where(inside, starts[None, :], 0), axis=1, dtype=jnp.int32)
    return jnp.stack([frame_index - lag >= first for lag in range(3)]).astype(jnp.bfloat16)


def column_neighbours(first, last):
    n_tm, n_height, n_width = (lax.axis_size(axis) for axis in MESH_AXES)
    blocks = n_tm * n_height
    place = [(pos % blocks) * n_width + pos // blocks for pos in range(blocks * n_width)]
    pairs = list(zip(place[:-1], place[1:]))
    left = lax.ppermute(last, MESH_AXES, pairs)
    right = lax.ppermute(first, MESH_AXES, [(b, a) for a, b in pairs])
    return left, right


def block_table(rows, cols, entry):
    blocks = [[entry(i, j) for j in range(cols)] for i in range(rows)]
    some = next(b for line in blocks for b in line if b is not None)
    zero = jnp.zeros_like(some)
    return jnp.concatenate(
        [jnp.concatenate([zero if b is None else b for b in line], axis=-1) for line in blocks],
        axis=-2,
    )


def row_shifts(block, rows):
    index = lax.broadcasted_iota(jnp.int32, block.shape, 0)
    above = jnp.where(index == 0, 0.0, pltpu.roll(block, 1, 0))
    below = jnp.where(index == rows - 1, 0.0, pltpu.roll(block, rows - 1, 0))
    return above.astype(jnp.bfloat16), below.astype(jnp.bfloat16)


def lanes(parts):
    return parts[0] if len(parts) == 1 else jnp.concatenate(parts, axis=1)


def forward_kernel(group, width, lag, *refs):
    now, before = refs[:group], refs[group : 2 * group]
    left, left_before, right, right_before, temporal, spatial, slope, act, held = refs[2 * group :]
    step = pl.program_id(1)
    rows, chans = slope.shape[2], slope.shape[3]
    sources = []
    for e in range(group):
        line = []
        for ours, l_ref, r_ref in ((before[e], left_before, right_before), (now[e], left, right)):
            for frame in range(2):
                tile = ours[0, frame]
                if e == 0:
                    tile = jnp.where(step == 0, l_ref[0, frame], tile)
                if e == group - 1:
                    tile = jnp.where(step * group + e == width + 1, r_ref[0, frame], tile)
                line.append(tile)
        sources.append(lanes(line))
    mixed = jnp.dot(
        jnp.concatenate(sources, axis=0), temporal[0], preferred_element_type=jnp.float32
    ).astype(jnp.bfloat16)
    for e in range(group):
        value = mixed[e * rows : (e + 1) * rows]
        above, below = row_shifts(value.astype(jnp.float32), rows)
        for frame in range(2):
            at = slice(frame * chans, (frame + 1) * chans)
            held[step * group + e, frame] = lanes([above[:, at], value[:, at], below[:, at]])

    @pl.when(step >= lag)
    def _():
        base = (step - lag) * group
        source = lanes([held[base + k].reshape(2 * rows, 3 * chans) for k in range(group + 2)])
        pre = jnp.dot(source, spatial[...], preferred_element_type=jnp.float32)
        sig = jax.nn.sigmoid(pre)
        value = sig * (1.0 + pre * (1.0 - sig))
        for e in range(group):
            slope[e] = value[:, e * chans : (e + 1) * chans].reshape(2, rows, chans)
            for frame in range(2):
                act[e, frame] = held[base + e + 1, frame, :, chans : 2 * chans]


def forward(video, left, right, temporal, spatial, group):
    width, frames, rows, chans = video.shape
    lag = 2 // group
    steps = (width + 2) // group

    def own(e, back):
        return pl.BlockSpec(
            (1, 2, rows, chans),
            lambda p, j: (
                jnp.clip(j * group + e - 1, 0, width - 1),
                jnp.maximum(p - back, 0),
                0,
                0,
            ),
        )

    def edge(back):
        return pl.BlockSpec((1, 2, rows, chans), lambda p, j: (0, jnp.maximum(p - back, 0), 0, 0))

    out = pl.BlockSpec((group, 2, rows, chans), lambda p, j: (jnp.maximum(j - lag, 0), p, 0, 0))
    pixels = width * frames * rows
    return pl.pallas_call(
        functools.partial(forward_kernel, group, width, lag),
        grid=(frames // 2, steps),
        in_specs=[own(e, 0) for e in range(group)]
        + [own(e, 1) for e in range(group)]
        + [
            edge(0),
            edge(1),
            edge(0),
            edge(1),
            pl.BlockSpec((1, 4 * chans, 2 * chans), lambda p, j: (p, 0, 0)),
            pl.BlockSpec(spatial.shape, lambda p, j: (0, 0)),
        ],
        out_specs=[out, out],
        out_shape=[
            jax.ShapeDtypeStruct((width, frames, rows, chans), jnp.float32),
            jax.ShapeDtypeStruct((width, frames, rows, chans), jnp.bfloat16),
        ],
        scratch_shapes=[pltpu.VMEM((width + 2, 2, rows, 3 * chans), jnp.bfloat16)],
        compiler_params=pltpu.CompilerParams(vmem_limit_bytes=VMEM),
        cost_estimate=pl.CostEstimate(
            flops=pixels * chans * chans * 2 * 24,
            bytes_accessed=pixels * chans * 14,
            transcendentals=pixels * chans,
        ),
    )(*([video] * (2 * group)), left, left, right, right, temporal, spatial)


def backward_kernel(group, inner, lag, scale, masks, *refs):
    edge_left, edge_right, left, right = refs[:4]
    refs = refs[4:]
    if inner:
        grads, slopes, refs = refs[0], refs[1 : 1 + group], refs[1 + group :]
    clip, clip_before, act, spatial, grad, sums, held, spatial_sum, temporal_sum = refs
    pair, step = pl.program_id(0), pl.program_id(1)
    last_pair, last = pl.num_programs(0) - 1, pl.num_programs(1) - 1
    rows, chans = grad.shape[2], grad.shape[3]

    def hold(e, delta):
        above, below = row_shifts(delta.astype(jnp.float32), rows)
        for frame in range(2):
            at = slice(frame * chans, (frame + 1) * chans)
            held[step * group + e, frame] = lanes([below[:, at], delta[:, at], above[:, at]])

    def hold_edges(tiles):
        for e, ref in enumerate(tiles):
            hold(e, lanes([ref[0, frame] for frame in range(2)]))

    @pl.when((pair == 0) & (step == 0))
    def _():
        spatial_sum[...] = jnp.zeros_like(spatial_sum)
        temporal_sum[...] = jnp.zeros_like(temporal_sum)

    @pl.when(step == 0)
    def _():
        hold_edges([left, edge_left][:group])

    @pl.when(step == last)
    def _():
        hold_edges([edge_right, right][-group:])

    @pl.when((step > 0) & (step < last))
    def _():
        if inner:
            bands, band = grads.shape[1], grads.shape[4]
            for e in range(group):
                hold(
                    e,
                    jnp.concatenate(
                        [
                            lanes(
                                [
                                    (
                                        grads[0, b, e, frame].astype(jnp.float32)
                                        * slopes[e][0, frame, b * band : (b + 1) * band]
                                    ).astype(jnp.bfloat16)
                                    for frame in range(2)
                                ]
                            )
                            for b in range(bands)
                        ],
                        axis=0,
                    ),
                )
        else:
            hold_edges([edge_left])

    @pl.when(step >= lag)
    def _():
        base = (step - lag) * group
        source = lanes([held[base + k].reshape(2 * rows, 3 * chans) for k in range(group + 2)])
        back = jnp.dot(source, spatial[...], preferred_element_type=jnp.float32)
        back = back.astype(jnp.bfloat16)
        for e in range(group):
            grad[e] = back[:, e * chans : (e + 1) * chans].reshape(2, rows, chans)
        own = lanes([act[e].reshape(2 * rows, chans) for e in range(group)])
        spatial_sum[...] += lax.dot_general(
            own, source, (((0,), (0,)), ((), ())), preferred_element_type=jnp.float32
        )
        ours = jnp.concatenate(
            [
                lanes(
                    [
                        back[f * rows : (f + 1) * rows, e * chans : (e + 1) * chans]
                        for f in range(2)
                    ]
                )
                for e in range(group)
            ],
            axis=0,
        )
        taps = jnp.concatenate(
            [
                lanes([ref[e, frame] for ref in (clip_before, clip) for frame in range(2)])
                for e in range(group)
            ],
            axis=0,
        )
        term = lax.dot_general(
            ours, taps, (((0,), (0,)), ((), ())), preferred_element_type=jnp.float32
        )
        for k in range(3):
            temporal_sum[k] += sum(
                masks[k, 2 * pair + j]
                * term[j * chans : (j + 1) * chans, (2 + j - k) * chans : (3 + j - k) * chans]
                for j in range(2)
            )

    @pl.when((pair == last_pair) & (step == last))
    def _():
        for k in range(3):
            sums[k] = temporal_sum[k].T * scale
        for a in range(3):
            for b in range(3):
                value = sum(
                    spatial_sum[
                        j * chans : (j + 1) * chans,
                        ((j + 2 - b) * 3 + a) * chans : ((j + 2 - b) * 3 + a + 1) * chans,
                    ]
                    for j in range(group)
                )
                sums[3 + 3 * a + b] = value * scale


def backward(edges, left, right, inner, slope, video, act, masks, spatial, scale, group):
    width, frames, rows, chans = video.shape
    lag = 2 // group
    steps = (width + 2) // group

    def single(place):
        return pl.BlockSpec((1, 2, rows, chans), lambda p, j, m: (place(j), p, 0, 0))

    def pair(back):
        return pl.BlockSpec(
            (group, 2, rows, chans),
            lambda p, j, m: (jnp.maximum(j - lag, 0), jnp.maximum(p - back, 0), 0, 0),
        )

    if group == 1:
        in_specs = [single(lambda j: jnp.clip(j - 1, 0, width - 1)), single(lambda j: width - 1)]
    else:
        in_specs = [single(lambda j: 0), single(lambda j: 1)]
    in_specs += [single(lambda j: 0), single(lambda j: 0)]
    operands = [edges, edges, left, right]
    if inner is not None:
        bands, band = inner.shape[1], inner.shape[4]
        blocks = inner.shape[2] // group
        in_specs.append(
            pl.BlockSpec(
                (1, bands, group, 2, band, chans),
                lambda p, j, m: (p, 0, jnp.clip(j - 1, 0, blocks - 1), 0, 0, 0),
            )
        )
        in_specs += [
            single(functools.partial(lambda e, j: jnp.clip(j * group + e - 1, 0, width - 1), e))
            for e in range(group)
        ]
        operands += [inner] + [slope] * group
    in_specs += [
        pair(0),
        pair(1),
        pair(0),
        pl.BlockSpec(spatial.shape, lambda p, j, m: (0, 0)),
    ]
    operands += [video, video, act, spatial]
    pixels = width * frames * rows
    return pl.pallas_call(
        functools.partial(backward_kernel, group, inner is not None, lag, scale),
        grid_spec=pltpu.PrefetchScalarGridSpec(
            num_scalar_prefetch=1,
            grid=(frames // 2, steps),
            in_specs=in_specs,
            out_specs=[
                pair(0),
                pl.BlockSpec((12, chans, chans), lambda p, j, m: (0, 0, 0)),
            ],
            scratch_shapes=[
                pltpu.VMEM((width + 2, 2, rows, 3 * chans), jnp.bfloat16),
                pltpu.VMEM((group * chans, (group + 2) * 3 * chans), jnp.float32),
                pltpu.VMEM((3, chans, chans), jnp.float32),
            ],
        ),
        out_shape=[
            jax.ShapeDtypeStruct((width, frames, rows, chans), jnp.bfloat16),
            jax.ShapeDtypeStruct((12, chans, chans), jnp.float32),
        ],
        compiler_params=pltpu.CompilerParams(vmem_limit_bytes=VMEM),
        cost_estimate=pl.CostEstimate(
            flops=pixels * chans * chans * 2 * 40,
            bytes_accessed=pixels * chans * 14,
            transcendentals=0,
        ),
    )(masks, *operands)


def video_kernel(now, after, weights, out):
    cols, _, rows, chans = now.shape
    source = jnp.concatenate(
        [
            lanes([ref[e, frame] for ref in (now, after) for frame in range(2)])
            for e in range(cols)
        ],
        axis=0,
    )
    value = jnp.dot(source, weights[0], preferred_element_type=jnp.float32).astype(jnp.bfloat16)
    for e in range(cols):
        for frame in range(2):
            out[e, frame] = value[e * rows : (e + 1) * rows, frame * chans : (frame + 1) * chans]


def video_gradient(grad, weights):
    width, frames, rows, chans = grad.shape
    cols = 4 if width % 4 == 0 else 1
    last = frames // 2 - 1
    pixels = width * frames * rows
    return pl.pallas_call(
        video_kernel,
        grid=(frames // 2, width // cols),
        in_specs=[
            pl.BlockSpec((cols, 2, rows, chans), lambda p, i: (i, p, 0, 0)),
            pl.BlockSpec((cols, 2, rows, chans), lambda p, i: (i, jnp.minimum(p + 1, last), 0, 0)),
            pl.BlockSpec((1, 4 * chans, 2 * chans), lambda p, i: (p, 0, 0)),
        ],
        out_specs=pl.BlockSpec((cols, 2, rows, chans), lambda p, i: (i, p, 0, 0)),
        out_shape=jax.ShapeDtypeStruct(grad.shape, jnp.bfloat16),
        compiler_params=pltpu.CompilerParams(vmem_limit_bytes=VMEM),
        cost_estimate=pl.CostEstimate(
            flops=pixels * chans * chans * 2 * 6,
            bytes_accessed=pixels * chans * 6,
            transcendentals=0,
        ),
    )(grad, grad, weights)


def exchanged(axis, parts):
    count = lax.axis_size(axis)
    return [
        lax.ppermute(parts(s), axis, [(i, i ^ s) for i in range(count)]) for s in range(1, count)
    ]


def sum_over_devices(local):
    def scatter(value, axis):
        me = lax.axis_index(axis)
        blocks = value.reshape(lax.axis_size(axis), -1, value.shape[-1])
        pick = lambda s: lax.dynamic_index_in_dim(blocks, me ^ s, 0, keepdims=False)
        return functools.reduce(jnp.add, exchanged(axis, pick), pick(0))

    def spread(value, axis):
        count = lax.axis_size(axis)
        me = lax.axis_index(axis)
        parts = jnp.stack([value] + exchanged(axis, lambda s: value))
        order = jnp.arange(count, dtype=jnp.int32) ^ me
        return jnp.take(parts, order, axis=0).reshape(-1, value.shape[-1])

    value = scatter(scatter(local, "width"), "height")
    value = functools.reduce(jnp.add, exchanged("tm", lambda s: value), value)
    return spread(spread(value, "height"), "width")


def shards(video, out_grad, lengths, temporal_weight, spatial_weight):
    clip = video[0]
    width, frames, rows, chans = clip.shape
    n_tm = lax.axis_size("tm")
    n_height = lax.axis_size("height")
    frames_dev, rows_dev = out_grad.shape[2], out_grad.shape[3]
    assert frames_dev == 2
    total_cols = out_grad.shape[1] * lax.axis_size("width")
    group = 2 if width % 2 == 0 else 1
    pairs = frames // 2

    left, right = column_neighbours(clip[:1], clip[width - 1 :])
    blocks = out_grad[0].reshape(n_tm * n_height, width, frames_dev, rows_dev, chans)

    def to_columns(part):
        got = lax.all_to_all(part, ("tm", "height"), split_axis=0, concat_axis=0, tiled=True)
        return got.reshape(n_tm, n_height, *part.shape[1:])

    inner = None
    if group == 2 and width > 2:
        outer = to_columns(jnp.stack([blocks[:, 0], blocks[:, width - 1]], axis=1))
        inner = blocks[:, 1 : width - 1]
        inner, outer = lax.optimization_barrier((inner, outer))
        inner = to_columns(inner)
    else:
        outer = to_columns(blocks)

    masks = frame_masks(lengths, frames)
    paired = masks.reshape(3, pairs, 2)
    late = jnp.pad(paired, ((0, 0), (0, 1), (0, 0)))

    def tap_block(i, j):
        k = 2 + j - i
        return paired[k, :, j, None, None] * temporal_weight[k] if 0 <= k < 3 else None

    def back_block(i, j):
        k = i - j
        if not 0 <= k < 3:
            return None
        return late[k, i // 2 : i // 2 + pairs, i % 2, None, None] * temporal_weight[k].T

    temporal_mix = block_table(4, 2, tap_block)
    temporal_back = block_table(4, 2, back_block)

    def pre_block(i, j):
        b = i // 3 - j
        return spatial_weight[i % 3, b] if 0 <= b < 3 else None

    def grad_block(i, j):
        b = j + 2 - i // 3
        return spatial_weight[i % 3, b].T if 0 <= b < 3 else None

    spatial_mix = block_table(3 * (group + 2), group, pre_block)
    spatial_back = block_table(3 * (group + 2), group, grad_block)

    slope, act = forward(clip, left, right, temporal_mix, spatial_mix, group)

    count = outer.shape[2]
    grads = outer.transpose(2, 0, 3, 1, 4, 5).reshape(count, frames, rows, chans)
    slopes = slope if count == width else jnp.stack([slope[0], slope[width - 1]])
    edges = (grads.astype(jnp.float32) * slopes).astype(jnp.bfloat16)
    delta_left, delta_right = column_neighbours(edges[:1], edges[count - 1 :])

    scale = float(frames * rows * total_cols) ** (-0.5)
    grad, local = backward(
        edges,
        delta_left,
        delta_right,
        inner,
        slope,
        clip,
        act,
        masks.astype(jnp.float32),
        spatial_back,
        scale,
        group,
    )
    video_grad = video_gradient(grad, temporal_back)
    sums = sum_over_devices(local.reshape(-1, chans)).reshape(12, chans, chans)
    temporal_grad, spatial_grad = sums[:3], sums[3:].reshape(3, 3, chans, chans)
    return video_grad[None], temporal_grad, spatial_grad


def solution(mesh):
    placed = (
        P("width", ("tm", "height"), None, None, None),
        P("width", None, "tm", "height", None),
        P(),
        P(),
        P(),
    )
    return jax.shard_map(
        shards,
        mesh=mesh,
        in_specs=placed,
        out_specs=(P("width", ("tm", "height"), None, None, None), P(), P()),
        check_vma=False,
    )
```

time: 266 us -> 204 us (0.77)
  starting transfers between devices: 85.9 us -> 44.1 us
  Pallas kernels: 71.4 us -> 55.4 us
    ppermute x22 -> x11, starting transfers between devices: 67.5 us -> 18.4 us  [exchanged(): lax.ppermute(parts(s), axis, [(i, i ^ s) for i in range(count)])]
    ppermute x2, waiting for transfers between devices: 38.8 us -> 1.92 us  [column_neighbours(): right = lax.ppermute(first, MESH_AXES, [(b, a) for a, b in pairs])]
    ppermute x2, waiting for transfers between devices: 9.63 us -> 40.3 us  [column_neighbours(): left = lax.ppermute(last, MESH_AXES, pairs)]
    pallas_call x2 -> x1, Pallas kernels: 45.4 us -> 30.9 us  [backward(): pl.pallas_call(functools.partial(backward_kernel, group, inner is not Non...]
    all_to_all x1 -> x2, waiting for transfers between devices: 2.15 us -> 13.1 us  [to_columns(): lax.all_to_all(part, ('tm', 'height'), split_axis=0, concat_axis=0, tiled...]
    all_to_all x1 -> x2, starting transfers between devices: 8.38 us -> 15.2 us  [to_columns(): lax.all_to_all(part, ('tm', 'height'), split_axis=0, concat_axis=0, tiled...]
    ppermute x22 -> x11, waiting for transfers between devices: 20.1 us -> 14.1 us  [exchanged(): lax.ppermute(parts(s), axis, [(i, i ^ s) for i in range(count)])]
    slice x2 -> x6, local copies, waits for them, and re-layouts: 5.45 us -> 11.1 us  [the longest x1 4.9 us: shards(): inner = blocks[:, 1:width - 1]]
  transfers between devices with their start and end apart: 27 -> 17, of which waited for: 12 -> 11; matrix products, arithmetic and copies ran while one was open for 9% -> 10% of each run, Pallas kernels for 19% -> 12%
where the time goes in v2:
time: 204 us
  waiting for transfers between devices  69.4 us (34%)
  Pallas kernels  55.4 us (27%)
  starting transfers between devices  44.1 us (22%)
  local copies, waits for them, and re-layouts  26.7 us (13%)
  other arithmetic  6.77 us (3%)
    ppermute x2, waiting for transfers between devices, column_neighbours(): left = lax.ppermute(last, MESH_AXES, pairs)  40.3 us
    pallas_call x1, Pallas kernels, backward(): pl.pallas_call(functools.partial(backward_kernel, group, inner is not Non...  30.9 us
    pallas_call x1, Pallas kernels, forward(): pl.pallas_call(functools.partial(forward_kernel, group, width, lag), grid...  18.8 us
    ppermute x11, starting transfers between devices, exchanged(): lax.ppermute(parts(s), axis, [(i, i ^ s) for i in range(count)])  18.4 us
    all_to_all x2, starting transfers between devices, to_columns(): lax.all_to_all(part, ('tm', 'height'), split_axis=0, concat_axis=0, tiled...  15.2 us
    ppermute x11, waiting for transfers between devices, exchanged(): lax.ppermute(parts(s), axis, [(i, i ^ s) for i in range(count)])  14.1 us
    all_to_all x2, waiting for transfers between devices, to_columns(): lax.all_to_all(part, ('tm', 'height'), split_axis=0, concat_axis=0, tiled...  13.1 us
    unnamed x43, local copies, waits for them, and re-layouts  8.38 us
  transfers between devices with their start and end apart: 17, of which 11 were waited for; matrix products, arithmetic and copies ran while one was open for 10% of the time, Pallas kernels for 12%

profile of v2, /device:TPU:0, one launch (start us, length us, event | category | flops | bytes accessed | tf_op | source)
XLA Modules:
  0.0 203.6 jit_solution(10698965259266626913)
XLA Ops:
  3.0 8.3 %all-to-all-start = ((bf16[16,2,2,64,128]{4,3,2,1,0:T(8,128)(2,1)}), bf16[16,2,2,64,128]{4,3,2,1,0:T(8,128)(2,1)S(1)}, u32[]{:S(2)}, u32[]{:S(2)}) async-start(bf16[16,2,2,64,128]{4,3,2,1,0:T(8,128)(2,1)} %pad_maximum_fusion), calls=%async_computation | async-start | bytes 2097152 | tf_op jit(solution)/shard_map/all_to_all | solution.py:410
  11.3 2.3 %slice_bitcast_fusion = (bf16[1,8,256,128]{3,2,1,0:T(8,128)(2,1)}, bf16[1,8,256,128]{3,2,1,0:T(8,128)(2,1)}) fusion(bf16[1,8,8,256,128]{4,3,2,1,0:T(8,128)(2,1)} %param.5), kind=kLoop, calls=%fused_computation.19 | loop fusion | bytes 2097152 | tf_op jit(solution)/shard_map/slice | solution.py:406
  13.6 3.8 %collective-permute-start = (bf16[1,8,256,128]{3,2,1,0:T(8,128)(2,1)}, bf16[1,8,256,128]{3,2,1,0:T(8,128)(2,1)S(1)}, u32[]{:S(2)}, u32[]{:S(2)}) collective-permute-start(bf16[1,8,256,128]{3,2,1,0:T(8,128)(2,1)} %get-tuple-element.27), channel_id=1, source_target_pairs={{0,2},{2,4},{4,6},{6,8},{8,10},{10,12},{12,14},{14,16},{16,18},{18... | collective-permute-start | bytes 1572872 | tf_op jit(solution)/shard_map/ppermute | solution.py:28
  18.9 4.9 %slice.182 = bf16[16,6,2,64,128]{4,3,2,1,0:T(8,128)(2,1)} slice(bf16[16,8,2,64,128]{4,3,2,1,0:T(8,128)(2,1)} %bitcast.106), slice={[0:16], [1:7], [0:2], [0:64], [0:128]} | slice | bytes 6291456 | tf_op jit(solution)/shard_map/slice | solution.py:416
  28.3 13.1 %all-to-all-done = bf16[16,2,2,64,128]{4,3,2,1,0:T(8,128)(2,1)S(1)} async-done(((bf16[16,2,2,64,128]{4,3,2,1,0:T(8,128)(2,1)}), bf16[16,2,2,64,128]{4,3,2,1,0:T(8,128)(2,1)S(1)}, u32[]{:S(2)}, u32[]{:S(2)}) %all-to-all-start) | async-done | bytes 1048608 | tf_op jit(solution)/shard_map/all_to_all | solution.py:410
  42.4 6.9 %all-to-all-start.1 = ((bf16[16,6,2,64,128]{4,3,2,1,0:T(8,128)(2,1)}), bf16[16,6,2,64,128]{4,3,2,1,0:T(8,128)(2,1)}, u32[]{:S(2)}, u32[]{:S(2)}) async-start(bf16[16,6,2,64,128]{4,3,2,1,0:T(8,128)(2,1)} %slice.182), calls=%async_computation.1 | async-start | bytes 6291456 | tf_op jit(solution)/shard_map/all_to_all | solution.py:410
  51.4 1.8 broadcast_multiply_fusion.2
  53.3 18.8 %shard_map.76 = (f32[8,8,256,128]{3,2,1,0:T(8,128)}, bf16[8,8,256,128]{3,2,1,0:T(8,128)(2,1)S(1)}) custom-call(bf16[8,8,256,128]{3,2,1,0:T(8,128)(2,1)S(1)} %bitcast.99, bf16[8,8,256,128]{3,2,1,0:T(8,128)(2,1)S(1)} %bitcast.100, bf16[8,8,256,128]{3,2,1,0:T(8,128)(2,1)S(1)} %bitcast.101, bf16[8,8,256,128]{3,2,1,0:T(8,128)(2,1)S(1)} %bitcast.102, ...), custom_call_target="tpu_custom_call" | custom-call | flops 12884901888 | bytes 29360128 | tf_op jit(solution)/shard_map/pallas_call | solution.py:115
  72.1 3.2 %fusion.21 = (f32[1,8,256,128]{3,2,1,0:T(8,128)S(1)}, f32[1,8,256,128]{3,2,1,0:T(8,128)S(1)}) fusion(f32[8,8,256,128]{3,2,1,0:T(8,128)} %get-tuple-element.10.refs_5_.refs_6_), kind=kLoop, calls=%fused_computation.113 | loop fusion | bytes 4194304 | tf_op jit(solution)/shard_map/slice | solution.py:454
  76.1 3.8 %collective-permute-start.2 = (bf16[1,8,256,128]{3,2,1,0:T(8,128)(2,1)S(1)}, bf16[1,8,256,128]{3,2,1,0:T(8,128)(2,1)S(1)}, u32[]{:S(2)}, u32[]{:S(2)}) collective-permute-start(bf16[1,8,256,128]{3,2,1,0:T(8,128)(2,1)S(1)} %get-tuple-element.31), channel_id=1, source_target_pairs={{0,2},{2,4},{4,6},{6,8},{8,10},{10,12},{12,14},{14,16},{16,18},{18... | collective-permute-start | bytes 1572872 | tf_op jit(solution)/shard_map/ppermute | solution.py:28
  81.3 40.3 %collective-permute-done.2.refs_2_ = bf16[1,8,256,128]{3,2,1,0:T(8,128)(2,1)S(1)} collective-permute-done((bf16[1,8,256,128]{3,2,1,0:T(8,128)(2,1)S(1)}, bf16[1,8,256,128]{3,2,1,0:T(8,128)(2,1)S(1)}, u32[]{:S(2)}, u32[]{:S(2)}) %collective-permute-start.2) | collective-permute-done | bytes 524320 | tf_op jit(solution)/shard_map/ppermute | solution.py:28
  121.6 1.9 collective-permute-done.3.refs_3_
  125.4 30.9 %shard_map.77 = (bf16[8,8,256,128]{3,2,1,0:T(8,128)(2,1)S(1)}, f32[12,128,128]{2,1,0:T(8,128)S(1)}) custom-call(f32[3,8]{1,0:T(4,128)S(1)} %fusion.15.masks, bf16[2,8,256,128]{3,2,1,0:T(8,128)(2,1)S(1)} %fusion.4.refs_0_.refs_1_, bf16[2,8,256,128]{3,2,1,0:T(8,128)(2,1)S(1)} %fusion.4.refs_0_.refs_1_, ...), custom_call_target="tpu_custom_call" | custom-call | flops 21474836480 | bytes 29360128 | tf_op jit(solution)/shard_map/pallas_call | solution.py:301
  156.2 2.0 copy-done
  160.8 2.9 %collective-permute-start.7 = (f32[192,128]{1,0:T(8,128)S(1)}, f32[192,128]{1,0:T(8,128)S(1)}, u32[]{:S(2)}, u32[]{:S(2)}) collective-permute-start(f32[192,128]{1,0:T(8,128)S(1)} %get-tuple-element.33), channel_id=1, source_target_pairs={{0,6},{2,4},{4,2},{6,0},{1,7},{3,5},{5,3},{7,1},{8,14},{10,12},{12... | collective-permute-start | bytes 294920 | tf_op jit(solution)/shard_map/ppermute | solution.py:372
  163.7 2.0 collective-permute-done.5
  165.7 1.7 collective-permute-done.6
  167.5 5.8 %collective-permute-start.10 = (f32[192,128]{1,0:T(8,128)S(1)}, f32[192,128]{1,0:T(8,128)S(1)}, u32[]{:S(2)}, u32[]{:S(2)}) collective-permute-start(f32[192,128]{1,0:T(8,128)S(1)} %fusion.12), channel_id=1, source_target_pairs={{0,24},{8,16},{16,8},{24,0},{1,25},{9,17},{17,9},{25,1},{2,26},{10... | collective-permute-start | bytes 294920 | tf_op jit(solution)/shard_map/ppermute | solution.py:372
  173.3 4.0 %collective-permute-start.8 = (f32[192,128]{1,0:T(8,128)S(1)}, f32[192,128]{1,0:T(8,128)S(1)}, u32[]{:S(2)}, u32[]{:S(2)}) collective-permute-start(f32[192,128]{1,0:T(8,128)S(1)} %fusion.12), channel_id=1, source_target_pairs={{0,8},{8,0},{16,24},{24,16},{1,9},{9,1},{17,25},{25,17},{2,10},{10... | collective-permute-start | bytes 294920 | tf_op jit(solution)/shard_map/ppermute | solution.py:372
  178.7 2.1 %collective-permute-done.8 = f32[192,128]{1,0:T(8,128)S(1)} collective-permute-done((f32[192,128]{1,0:T(8,128)S(1)}, f32[192,128]{1,0:T(8,128)S(1)}, u32[]{:S(2)}, u32[]{:S(2)}) %collective-permute-start.8) | collective-permute-done | bytes 98336 | tf_op jit(solution)/shard_map/ppermute | solution.py:372
  180.7 3.7 %collective-permute-done.9 = f32[192,128]{1,0:T(8,128)S(1)} collective-permute-done((f32[192,128]{1,0:T(8,128)S(1)}, f32[192,128]{1,0:T(8,128)S(1)}, u32[]{:S(2)}, u32[]{:S(2)}) %collective-permute-start.9) | collective-permute-done | bytes 98336 | tf_op jit(solution)/shard_map/ppermute | solution.py:372
  184.4 1.6 collective-permute-start.11
  193.1 2.2 %copy-done.1 = bf16[8,8,256,128]{3,2,1,0:T(8,128)(2,1)S(1)} copy-done((bf16[8,8,256,128]{3,2,1,0:T(8,128)(2,1)S(1)}, bf16[8,8,256,128]{3,2,1,0:T(8,128)(2,1)}, u32[]{:S(2)}) %copy-start.1) | copy-done | bytes 4194328
  195.3 5.8 %shard_map.78 = bf16[8,8,256,128]{3,2,1,0:T(8,128)(2,1)} custom-call(bf16[8,8,256,128]{3,2,1,0:T(8,128)(2,1)S(1)} %copy-done.1, bf16[8,8,256,128]{3,2,1,0:T(8,128)(2,1)S(1)} %copy-done.1, bf16[4,512,256]{2,1,0:T(8,128)(2,1)S(1)} %fusion.10.weights), custom_call_target="tpu_custom_call" | custom-call | flops 3221225472 | bytes 12582912 | tf_op jit(solution)/shard_map/pallas_call | solution.py:350
  (121 shorter events, 28.5 us)
Async XLA Ops:
  3.0 38.4 %all-to-all-start = ((bf16[16,2,2,64,128]{4,3,2,1,0:T(8,128)(2,1)}), bf16[16,2,2,64,128]{4,3,2,1,0:T(8,128)(2,1)S(1)}, u32[]{:S(2)}, u32[]{:S(2)}) async-start(bf16[16,2,2,64,128]{4,3,2,1,0:T(8,128)(2,1)} %pad_maximum_fusion), calls=%async_computation | async-start | bytes 2097152 | tf_op jit(solution)/shard_map/all_to_all | solution.py:410
  13.6 39.7 %collective-permute-start = (bf16[1,8,256,128]{3,2,1,0:T(8,128)(2,1)}, bf16[1,8,256,128]{3,2,1,0:T(8,128)(2,1)S(1)}, u32[]{:S(2)}, u32[]{:S(2)}) collective-permute-start(bf16[1,8,256,128]{3,2,1,0:T(8,128)(2,1)} %get-tuple-element.27), channel_id=1, source_target_pairs={{0,2},{2,4},{4,6},{6,8},{8,10},{10,12},{12,14},{14,16},{16,18},{18... | collective-permute-start | bytes 1572872 | tf_op jit(solution)/shard_map/ppermute | solution.py:28
  17.5 6.4 %copy-start.11 = (s32[4]{0:T(128)S(1)}, s32[4]{0:T(128)}, u32[]{:S(2)}) copy-start(s32[4]{0:T(128)} %param.7) | copy-start | bytes 52
  17.5 6.7 %copy-start.10 = (bf16[3,128,128]{2,1,0:T(8,128)(2,1)S(1)}, bf16[3,128,128]{2,1,0:T(8,128)(2,1)}, u32[]{:S(2)}) copy-start(bf16[3,128,128]{2,1,0:T(8,128)(2,1)} %param.8) | copy-start | bytes 294916
  17.5 9.5 %copy-start.9 = (bf16[3,3,128,128]{3,2,1,0:T(8,128)(2,1)S(1)}, bf16[3,3,128,128]{3,2,1,0:T(8,128)(2,1)}, u32[]{:S(2)}) copy-start(bf16[3,3,128,128]{3,2,1,0:T(8,128)(2,1)} %param.9) | copy-start | bytes 884740
  17.5 35.8 %collective-permute-start.1 = (bf16[1,8,256,128]{3,2,1,0:T(8,128)(2,1)}, bf16[1,8,256,128]{3,2,1,0:T(8,128)(2,1)S(1)}, u32[]{:S(2)}, u32[]{:S(2)}) collective-permute-start(bf16[1,8,256,128]{3,2,1,0:T(8,128)(2,1)} %get-tuple-element.26), channel_id=1, source_target_pairs={{2,0},{4,2},{6,4},{8,6},{10,8},{12,10},{14,12},{16,14},{18,16},{20... | collective-permute-start | bytes 1572872 | tf_op jit(solution)/shard_map/ppermute | solution.py:29
  42.4 81.9 %all-to-all-start.1 = ((bf16[16,6,2,64,128]{4,3,2,1,0:T(8,128)(2,1)}), bf16[16,6,2,64,128]{4,3,2,1,0:T(8,128)(2,1)}, u32[]{:S(2)}, u32[]{:S(2)}) async-start(bf16[16,6,2,64,128]{4,3,2,1,0:T(8,128)(2,1)} %slice.182), calls=%async_computation.1 | async-start | bytes 6291456 | tf_op jit(solution)/shard_map/all_to_all | solution.py:410
  50.2 3.1 %copy-start.2 = (bf16[1,8,8,256,128]{4,3,2,1,0:T(8,128)(2,1)S(1)}, bf16[1,8,8,256,128]{4,3,2,1,0:T(8,128)(2,1)}, u32[]{:S(2)}) copy-start(bf16[1,8,8,256,128]{4,3,2,1,0:T(8,128)(2,1)} %param.5) | copy-start | bytes 12582916
  72.1 3.3 %copy-start.5 = (bf16[8,8,256,128]{3,2,1,0:T(8,128)(2,1)}, bf16[8,8,256,128]{3,2,1,0:T(8,128)(2,1)S(1)}, u32[]{:S(2)}) copy-start(bf16[8,8,256,128]{3,2,1,0:T(8,128)(2,1)S(1)} %get-tuple-element.12.refs_9_) | copy-start | bytes 12582916
  72.1 3.4 %copy-start.7 = (bf16[16,2,2,64,128]{4,3,2,1,0:T(8,128)(2,1)S(1)}, bf16[16,2,2,64,128]{4,3,2,1,0:T(8,128)(2,1)}, u32[]{:S(2)}) copy-start(bf16[16,2,2,64,128]{4,3,2,1,0:T(8,128)(2,1)} %copy-done.6) | copy-start | bytes 3145732
  76.1 45.5 %collective-permute-start.2 = (bf16[1,8,256,128]{3,2,1,0:T(8,128)(2,1)S(1)}, bf16[1,8,256,128]{3,2,1,0:T(8,128)(2,1)S(1)}, u32[]{:S(2)}, u32[]{:S(2)}) collective-permute-start(bf16[1,8,256,128]{3,2,1,0:T(8,128)(2,1)S(1)} %get-tuple-element.31), channel_id=1, source_target_pairs={{0,2},{2,4},{4,6},{6,8},{8,10},{10,12},{12,14},{14,16},{16,18},{18... | collective-permute-start | bytes 1572872 | tf_op jit(solution)/shard_map/ppermute | solution.py:28
  79.9 43.6 %collective-permute-start.3 = (bf16[1,8,256,128]{3,2,1,0:T(8,128)(2,1)S(1)}, bf16[1,8,256,128]{3,2,1,0:T(8,128)(2,1)S(1)}, u32[]{:S(2)}, u32[]{:S(2)}) collective-permute-start(bf16[1,8,256,128]{3,2,1,0:T(8,128)(2,1)S(1)} %get-tuple-element.30), channel_id=1, source_target_pairs={{2,0},{4,2},{6,4},{8,6},{10,8},{12,10},{14,12},{16,14},{18,16},{20... | collective-permute-start | bytes 1572872 | tf_op jit(solution)/shard_map/ppermute | solution.py:29
  125.3 33.2 %copy-start.8 = (bf16[4,128,128]{2,1,0:T(8,128)(2,1)S(1)}, bf16[4,128,128]{2,1,0:T(8,128)(2,1)}, u32[]{:S(2)}) copy-start(bf16[4,128,128]{2,1,0:T(8,128)(2,1)} %get-tuple-element.54) | copy-start | bytes 393220
  158.3 1.8 collective-permute-start.4
  160.2 5.6 %collective-permute-start.5 = (f32[192,128]{1,0:T(8,128)S(1)}, f32[192,128]{1,0:T(8,128)S(1)}, u32[]{:S(2)}, u32[]{:S(2)}) collective-permute-start(f32[192,128]{1,0:T(8,128)S(1)} %get-tuple-element.32), channel_id=1, source_target_pairs={{0,2},{2,0},{4,6},{6,4},{1,3},{3,1},{5,7},{7,5},{8,10},{10,8},{12,... | collective-permute-start | bytes 294920 | tf_op jit(solution)/shard_map/ppermute | solution.py:372
  160.8 6.7 %collective-permute-start.6 = (f32[192,128]{1,0:T(8,128)S(1)}, f32[192,128]{1,0:T(8,128)S(1)}, u32[]{:S(2)}, u32[]{:S(2)}) collective-permute-start(f32[192,128]{1,0:T(8,128)S(1)} %get-tuple-element.34), channel_id=1, source_target_pairs={{0,4},{2,6},{4,0},{6,2},{1,5},{3,7},{5,1},{7,3},{8,12},{10,14},{12... | collective-permute-start | bytes 294920 | tf_op jit(solution)/shard_map/ppermute | solution.py:372
  160.8 6.7 %collective-permute-start.7 = (f32[192,128]{1,0:T(8,128)S(1)}, f32[192,128]{1,0:T(8,128)S(1)}, u32[]{:S(2)}, u32[]{:S(2)}) collective-permute-start(f32[192,128]{1,0:T(8,128)S(1)} %get-tuple-element.33), channel_id=1, source_target_pairs={{0,6},{2,4},{4,2},{6,0},{1,7},{3,5},{5,3},{7,1},{8,14},{10,12},{12... | collective-permute-start | bytes 294920 | tf_op jit(solution)/shard_map/ppermute | solution.py:372
  167.5 11.2 %collective-permute-start.10 = (f32[192,128]{1,0:T(8,128)S(1)}, f32[192,128]{1,0:T(8,128)S(1)}, u32[]{:S(2)}, u32[]{:S(2)}) collective-permute-start(f32[192,128]{1,0:T(8,128)S(1)} %fusion.12), channel_id=1, source_target_pairs={{0,24},{8,16},{16,8},{24,0},{1,25},{9,17},{17,9},{25,1},{2,26},{10... | collective-permute-start | bytes 294920 | tf_op jit(solution)/shard_map/ppermute | solution.py:372
  173.3 7.5 %collective-permute-start.8 = (f32[192,128]{1,0:T(8,128)S(1)}, f32[192,128]{1,0:T(8,128)S(1)}, u32[]{:S(2)}, u32[]{:S(2)}) collective-permute-start(f32[192,128]{1,0:T(8,128)S(1)} %fusion.12), channel_id=1, source_target_pairs={{0,8},{8,0},{16,24},{24,16},{1,9},{9,1},{17,25},{25,17},{2,10},{10... | collective-permute-start | bytes 294920 | tf_op jit(solution)/shard_map/ppermute | solution.py:372
  177.3 7.1 %collective-permute-start.9 = (f32[192,128]{1,0:T(8,128)S(1)}, f32[192,128]{1,0:T(8,128)S(1)}, u32[]{:S(2)}, u32[]{:S(2)}) collective-permute-start(f32[192,128]{1,0:T(8,128)S(1)} %fusion.12), channel_id=1, source_target_pairs={{0,16},{8,24},{16,0},{24,8},{1,17},{9,25},{17,1},{25,9},{2,18},{10... | collective-permute-start | bytes 294920 | tf_op jit(solution)/shard_map/ppermute | solution.py:372
  184.4 4.7 %collective-permute-start.11 = (f32[192,128]{1,0:T(8,128)S(1)}, f32[192,128]{1,0:T(8,128)S(1)}, u32[]{:S(2)}, u32[]{:S(2)}) collective-permute-start(f32[192,128]{1,0:T(8,128)S(1)} %add_add_fusion), channel_id=1, source_target_pairs={{0,2},{2,0},{4,6},{6,4},{1,3},{3,1},{5,7},{7,5},{8,10},{10,8},{12,... | collective-permute-start | bytes 294920 | tf_op jit(solution)/shard_map/ppermute | solution.py:372
  186.0 4.6 %collective-permute-start.12 = (f32[192,128]{1,0:T(8,128)S(1)}, f32[192,128]{1,0:T(8,128)S(1)}, u32[]{:S(2)}, u32[]{:S(2)}) collective-permute-start(f32[192,128]{1,0:T(8,128)S(1)} %add_add_fusion), channel_id=1, source_target_pairs={{0,4},{2,6},{4,0},{6,2},{1,5},{3,7},{5,1},{7,3},{8,12},{10,14},{12... | collective-permute-start | bytes 294920 | tf_op jit(solution)/shard_map/ppermute | solution.py:372
  186.7 5.5 %collective-permute-start.13 = (f32[192,128]{1,0:T(8,128)S(1)}, f32[192,128]{1,0:T(8,128)S(1)}, u32[]{:S(2)}, u32[]{:S(2)}) collective-permute-start(f32[192,128]{1,0:T(8,128)S(1)} %add_add_fusion), channel_id=1, source_target_pairs={{0,6},{2,4},{4,2},{6,0},{1,7},{3,5},{5,3},{7,1},{8,14},{10,12},{12... | collective-permute-start | bytes 294920 | tf_op jit(solution)/shard_map/ppermute | solution.py:372
  193.0 8.2 %collective-permute-start.14 = (f32[768,128]{1,0:T(8,128)S(1)}, f32[768,128]{1,0:T(8,128)S(1)}, u32[]{:S(2)}, u32[]{:S(2)}) collective-permute-start(f32[768,128]{1,0:T(8,128)S(1)} %bitcast_select_fusion), channel_id=1, source_target_pairs={{0,1},{1,0},{2,3},{3,2},{4,5},{5,4},{6,7},{7,6},{8,9},{9,8},{10,11... | collective-permute-start | bytes 1179656 | tf_op jit(solution)/shard_map/ppermute | solution.py:372
  (5 other events, 7.0 us)

commit v3 on v1

v3 whole, which is shorter than its diff:
```python
import functools

import jax
import jax.numpy as jnp
from jax import lax
from jax.experimental import pallas as pl
from jax.experimental.pallas import tpu as pltpu
from jax.sharding import PartitionSpec as P

MESH_AXES = ("tm", "height", "width")
VMEM = 40 * 1024 * 1024


def frame_masks(lengths, frames):
    ends = jnp.cumsum(lengths, dtype=jnp.int32)
    starts = ends - lengths
    frame_index = jnp.arange(frames, dtype=jnp.int32)
    inside = (frame_index[:, None] >= starts[None, :]) & (frame_index[:, None] < ends[None, :])
    first = jnp.sum(jnp.where(inside, starts[None, :], 0), axis=1, dtype=jnp.int32)
    return jnp.stack([frame_index - lag >= first for lag in range(3)]).astype(jnp.bfloat16)


def column_neighbours(first, last):
    n_tm, n_height, n_width = (lax.axis_size(axis) for axis in MESH_AXES)
    blocks = n_tm * n_height
    place = [(pos % blocks) * n_width + pos // blocks for pos in range(blocks * n_width)]
    pairs = list(zip(place[:-1], place[1:]))
    left = lax.ppermute(last, MESH_AXES, pairs)
    right = lax.ppermute(first, MESH_AXES, [(b, a) for a, b in pairs])
    return left, right


def block_table(rows, cols, entry):
    blocks = [[entry(i, j) for j in range(cols)] for i in range(rows)]
    some = next(b for line in blocks for b in line if b is not None)
    zero = jnp.zeros_like(some)
    return jnp.concatenate(
        [jnp.concatenate([zero if b is None else b for b in line], axis=-1) for line in blocks],
        axis=-2,
    )


def row_shifts(block, rows):
    index = lax.broadcasted_iota(jnp.int32, block.shape, 0)
    above = jnp.where(index == 0, 0.0, pltpu.roll(block, 1, 0))
    below = jnp.where(index == rows - 1, 0.0, pltpu.roll(block, rows - 1, 0))
    return above.astype(jnp.bfloat16), below.astype(jnp.bfloat16)


def lanes(parts):
    return parts[0] if len(parts) == 1 else jnp.concatenate(parts, axis=1)


def forward_kernel(group, width, lag, *refs):
    now, before = refs[:group], refs[group : 2 * group]
    left, left_before, right, right_before, temporal, spatial, slope, turned, held = refs[2 * group :]
    step = pl.program_id(1)
    rows, chans = slope.shape[2], slope.shape[3]
    sources = []
    for e in range(group):
        line = []
        for ours, l_ref, r_ref in ((before[e], left_before, right_before), (now[e], left, right)):
            for frame in range(2):
                tile = ours[0, frame]
                if e == 0:
                    tile = jnp.where(step == 0, l_ref[0, frame], tile)
                if e == group - 1:
                    tile = jnp.where(step * group + e == width + 1, r_ref[0, frame], tile)
                line.append(tile)
                if ours is now[e]:
                    turned[e, frame] = tile.T
        sources.append(lanes(line))
    mixed = jnp.dot(
        jnp.concatenate(sources, axis=0), temporal[0], preferred_element_type=jnp.float32
    ).astype(jnp.bfloat16)
    for e in range(group):
        value = mixed[e * rows : (e + 1) * rows]
        above, below = row_shifts(value.astype(jnp.float32), rows)
        for frame in range(2):
            at = slice(frame * chans, (frame + 1) * chans)
            held[step * group + e, frame] = lanes([above[:, at], value[:, at], below[:, at]])

    @pl.when(step >= lag)
    def _():
        base = (step - lag) * group
        source = lanes([held[base + k].reshape(2 * rows, 3 * chans) for k in range(group + 2)])
        pre = jnp.dot(source, spatial[...], preferred_element_type=jnp.float32)
        sig = jax.nn.sigmoid(pre)
        value = sig * (1.0 + pre * (1.0 - sig))
        for e in range(group):
            slope[e] = value[:, e * chans : (e + 1) * chans].reshape(2, rows, chans)


def forward(video, left, right, temporal, spatial, group):
    width, frames, rows, chans = video.shape
    lag = 2 // group
    steps = (width + 2) // group

    def own(e, back):
        return pl.BlockSpec(
            (1, 2, rows, chans),
            lambda p, j: (
                jnp.clip(j * group + e - 1, 0, width - 1),
                jnp.maximum(p - back, 0),
                0,
                0,
            ),
        )

    def edge(back):
        return pl.BlockSpec((1, 2, rows, chans), lambda p, j: (0, jnp.maximum(p - back, 0), 0, 0))

    out = pl.BlockSpec((group, 2, rows, chans), lambda p, j: (jnp.maximum(j - lag, 0), p, 0, 0))
    pixels = width * frames * rows
    return pl.pallas_call(
        functools.partial(forward_kernel, group, width, lag),
        grid=(frames // 2, steps),
        in_specs=[own(e, 0) for e in range(group)]
        + [own(e, 1) for e in range(group)]
        + [
            edge(0),
            edge(1),
            edge(0),
            edge(1),
            pl.BlockSpec((1, 4 * chans, 2 * chans), lambda p, j: (p, 0, 0)),
            pl.BlockSpec(spatial.shape, lambda p, j: (0, 0)),
        ],
        out_specs=[out, pl.BlockSpec((group, 2, chans, rows), lambda p, j: (j, p, 0, 0))],
        out_shape=[
            jax.ShapeDtypeStruct((width, frames, rows, chans), jnp.float32),
            jax.ShapeDtypeStruct((width + 2, frames, chans, rows), jnp.bfloat16),
        ],
        scratch_shapes=[pltpu.VMEM((width + 2, 2, rows, 3 * chans), jnp.bfloat16)],
        compiler_params=pltpu.CompilerParams(vmem_limit_bytes=VMEM),
        cost_estimate=pl.CostEstimate(
            flops=pixels * chans * chans * 2 * 24,
            bytes_accessed=pixels * chans * 14,
            transcendentals=pixels * chans,
        ),
    )(*([video] * (2 * group)), left, left, right, right, temporal, spatial)


def moments_kernel(group, span, extra, scale, masks, *refs):
    grads, slope = refs[:2]
    now, before = refs[2 : 2 + extra], refs[2 + extra : 2 + 2 * extra]
    temporal, spatial, delta, sums, total = refs[2 + 2 * extra :]
    pair, step = pl.program_id(0), pl.program_id(1)
    bands, band = grads.shape[1], grads.shape[4]
    rows, chans = slope.shape[2], slope.shape[3]

    @pl.when((pair == 0) & (step == 0))
    def _():
        total[...] = jnp.zeros_like(total)

    places = [(n, frame) for n in range(span) for frame in range(2)]
    triples = []
    for n, frame in places:
        line = []
        for e in range(n * group, (n + 1) * group):
            for b in range(bands):
                at = slice(b * band, (b + 1) * band)
                value = grads[0, b, e, frame].astype(jnp.float32) * slope[e, frame, at]
                delta[e, frame, at] = value.astype(jnp.bfloat16)
            value = delta[e, frame]
            above, below = row_shifts(value.astype(jnp.float32), rows)
            line += [below, value, above]
        triples.append(lanes(line))
    right = jnp.concatenate(triples, axis=0)

    def add(lag, left):
        total[lag] += jnp.dot(left, right, preferred_element_type=jnp.float32)

    def turned(refs, n, frame):
        cols = range(n * group, (n + 1) * group + 2)
        return jnp.concatenate([refs[c // group][c % group, frame] for c in cols], axis=0)

    add(0, lanes([turned(now, n, frame) for n, frame in places]))
    for lag in (1, 2):
        keep = [masks[lag, 2 * pair + frame] for frame in range(2)]
        source = [(before, 1), (now, 0)] if lag == 1 else [(before, 0), (before, 1)]

        @pl.when(keep[0] + keep[1] > 0)
        def _():
            left = []
            for n, frame in places:
                refs, other = source[frame]
                value = turned(refs, n, other)
                left.append(jnp.where(keep[frame] > 0, value, jnp.zeros_like(value)))
            add(lag, lanes(left))

    @pl.when((pair == pl.num_programs(0) - 1) & (step == pl.num_programs(1) - 1))
    def _():
        lines = []
        for lag in range(3):
            line = []
            for a in range(3):
                for b in range(3):
                    line.append(
                        sum(
                            total[
                                lag,
                                (j + b) * chans : (j + b + 1) * chans,
                                (j * 3 + a) * chans : (j * 3 + a + 1) * chans,
                            ]
                            for j in range(group)
                        )
                    )
            lines.append(lanes(line))
        moments = jnp.concatenate(lines, axis=0)
        high = moments.astype(jnp.bfloat16)
        low = (moments - high.astype(jnp.float32)).astype(jnp.bfloat16)

        def product(left, right):
            return jnp.dot(left, right, preferred_element_type=jnp.float32)

        spatial_sum = product(temporal[...], high) + product(temporal[...], low)
        temporal_sum = product(high, spatial[...]) + product(low, spatial[...])
        for k in range(3):
            sums[k] = temporal_sum[k * chans : (k + 1) * chans] * scale
        for k in range(9):
            sums[3 + k] = spatial_sum[:, k * chans : (k + 1) * chans] * scale


def moments(received, slope, turned, masks, temporal, spatial, scale, group):
    width, frames, rows, chans = slope.shape
    bands, band = received.shape[1], received.shape[4]
    span = 2 if width % (2 * group) == 0 else 1
    cols = span * group
    extra = span + 2 // group
    pixels = width * frames * rows

    def columns(k, back):
        return pl.BlockSpec(
            (group, 2, chans, rows),
            lambda p, i, m: (i * span + k, jnp.maximum(p - back, 0), 0, 0),
        )

    own = pl.BlockSpec((cols, 2, rows, chans), lambda p, i, m: (i, p, 0, 0))
    return pl.pallas_call(
        functools.partial(moments_kernel, group, span, extra, scale),
        grid_spec=pltpu.PrefetchScalarGridSpec(
            num_scalar_prefetch=1,
            grid=(frames // 2, width // cols),
            in_specs=[
                pl.BlockSpec((1, bands, cols, 2, band, chans), lambda p, i, m: (p, 0, i, 0, 0, 0)),
                own,
            ]
            + [columns(k, 0) for k in range(extra)]
            + [columns(k, 1) for k in range(extra)]
            + [
                pl.BlockSpec(temporal.shape, lambda p, i, m: (0, 0)),
                pl.BlockSpec(spatial.shape, lambda p, i, m: (0, 0)),
            ],
            out_specs=[own, pl.BlockSpec((12, chans, chans), lambda p, i, m: (0, 0, 0))],
            scratch_shapes=[
                pltpu.VMEM((3, (group + 2) * chans, group * 3 * chans), jnp.float32),
            ],
        ),
        out_shape=[
            jax.ShapeDtypeStruct((width, frames, rows, chans), jnp.bfloat16),
            jax.ShapeDtypeStruct((12, chans, chans), jnp.float32),
        ],
        compiler_params=pltpu.CompilerParams(vmem_limit_bytes=VMEM),
        cost_estimate=pl.CostEstimate(
            flops=pixels * chans * chans * 2 * 30,
            bytes_accessed=pixels * chans * 20,
            transcendentals=0,
        ),
    )(masks, received, slope, *([turned] * (2 * extra)), temporal, spatial)


def backward_kernel(group, *refs):
    delta, left, right, spatial = refs[:4]
    grad = refs[-1]
    width, rows, chans = grad.shape[0], grad.shape[2], grad.shape[3]
    triples = []
    for col in [left.at[0]] + [delta.at[c] for c in range(width)] + [right.at[0]]:
        lines = []
        for frame in range(2):
            value = col[frame]
            above, below = row_shifts(value.astype(jnp.float32), rows)
            lines.append(lanes([below, value, above]))
        triples.append(jnp.concatenate(lines, axis=0))
    for base in range(0, width, group):
        source = lanes(triples[base : base + group + 2])
        back = jnp.dot(source, spatial[...], preferred_element_type=jnp.float32)
        back = back.astype(jnp.bfloat16)
        for e in range(group):
            grad[base + e] = back[:, e * chans : (e + 1) * chans].reshape(2, rows, chans)


def backward(delta, left, right, spatial, filled, pairs, group):
    width, _, rows, chans = delta.shape
    start = pairs[0]
    filled = [] if filled is None else [filled]
    block = pl.BlockSpec((width, 2, rows, chans), lambda p: (0, start + p, 0, 0))
    edge = pl.BlockSpec((1, 2, rows, chans), lambda p: (0, start + p, 0, 0))
    pixels = width * 2 * len(pairs) * rows
    return pl.pallas_call(
        functools.partial(backward_kernel, group),
        grid=(len(pairs),),
        in_specs=[block, edge, edge, pl.BlockSpec(spatial.shape, lambda p: (0, 0))]
        + [pl.BlockSpec(memory_space=pl.ANY)] * len(filled),
        out_specs=block,
        out_shape=jax.ShapeDtypeStruct(delta.shape, jnp.bfloat16),
        input_output_aliases={4: 0} if filled else {},
        compiler_params=pltpu.CompilerParams(vmem_limit_bytes=VMEM),
        cost_estimate=pl.CostEstimate(
            flops=pixels * chans * chans * 2 * 18,
            bytes_accessed=pixels * chans * 6,
            transcendentals=0,
        ),
    )(delta, left, right, spatial, *filled)


def video_kernel(now, after, weights, out):
    cols, _, rows, chans = now.shape
    source = jnp.concatenate(
        [
            lanes([ref[e, frame] for ref in (now, after) for frame in range(2)])
            for e in range(cols)
        ],
        axis=0,
    )
    value = jnp.dot(source, weights[0], preferred_element_type=jnp.float32).astype(jnp.bfloat16)
    for e in range(cols):
        for frame in range(2):
            out[e, frame] = value[e * rows : (e + 1) * rows, frame * chans : (frame + 1) * chans]


def video_gradient(grad, weights):
    width, frames, rows, chans = grad.shape
    cols = 4 if width % 4 == 0 else 1
    last = frames // 2 - 1
    pixels = width * frames * rows
    return pl.pallas_call(
        video_kernel,
        grid=(frames // 2, width // cols),
        in_specs=[
            pl.BlockSpec((cols, 2, rows, chans), lambda p, i: (i, p, 0, 0)),
            pl.BlockSpec((cols, 2, rows, chans), lambda p, i: (i, jnp.minimum(p + 1, last), 0, 0)),
            pl.BlockSpec((1, 4 * chans, 2 * chans), lambda p, i: (p, 0, 0)),
        ],
        out_specs=pl.BlockSpec((cols, 2, rows, chans), lambda p, i: (i, p, 0, 0)),
        out_shape=jax.ShapeDtypeStruct(grad.shape, jnp.bfloat16),
        compiler_params=pltpu.CompilerParams(vmem_limit_bytes=VMEM),
        cost_estimate=pl.CostEstimate(
            flops=pixels * chans * chans * 2 * 6,
            bytes_accessed=pixels * chans * 6,
            transcendentals=0,
        ),
    )(grad, grad, weights)


def exchanged(axis, parts):
    count = lax.axis_size(axis)
    return [
        lax.ppermute(parts(s), axis, [(i, i ^ s) for i in range(count)]) for s in range(1, count)
    ]


def sum_over_devices(local, works, state):
    def pieces(value, axis):
        me = lax.axis_index(axis)
        blocks = value.reshape(lax.axis_size(axis), -1, value.shape[-1])
        return lambda s: lax.dynamic_index_in_dim(blocks, me ^ s, 0, keepdims=False)

    def spread(parts, axis):
        order = jnp.arange(len(parts), dtype=jnp.int32) ^ lax.axis_index(axis)
        return jnp.take(jnp.stack(parts), order, axis=0).reshape(-1, parts[0].shape[-1])

    def beside(value, got, work, state):
        value, state = lax.optimization_barrier((value, state))
        got = got(value)
        state = work(state)
        got, state = lax.optimization_barrier((got, state))
        return value, got, state

    pick = pieces(local, "width")
    value = functools.reduce(jnp.add, exchanged("width", pick), pick(0))
    value, got, state = beside(
        value, lambda v: exchanged("height", pieces(v, "height")), works[0], state
    )
    value = functools.reduce(jnp.add, got, pieces(value, "height")(0))
    value, got, state = beside(
        value, lambda v: exchanged("tm", lambda s: v), works[1], state
    )
    value = functools.reduce(jnp.add, got, value)
    value, got, state = beside(
        value, lambda v: exchanged("height", lambda s: v), works[2], state
    )
    value = spread([value] + got, "height")
    return spread([value] + exchanged("width", lambda s: value), "width"), state


def shards(video, out_grad, lengths, temporal_weight, spatial_weight):
    clip = video[0]
    width, frames, rows, chans = clip.shape
    n_tm = lax.axis_size("tm")
    n_height = lax.axis_size("height")
    frames_dev, rows_dev = out_grad.shape[2], out_grad.shape[3]
    assert frames_dev == 2
    total_cols = out_grad.shape[1] * lax.axis_size("width")
    group = 2 if width % 2 == 0 else 1
    pairs = frames // 2

    left, right = column_neighbours(clip[:1], clip[width - 1 :])
    received = lax.all_to_all(out_grad[0], ("tm", "height"), split_axis=0, concat_axis=0, tiled=True)
    received = received.reshape(n_tm, n_height, width, frames_dev, rows_dev, chans)

    masks = frame_masks(lengths, frames)
    paired = masks.reshape(3, pairs, 2)
    late = jnp.pad(paired, ((0, 0), (0, 1), (0, 0)))

    def tap_block(i, j):
        k = 2 + j - i
        return paired[k, :, j, None, None] * temporal_weight[k] if 0 <= k < 3 else None

    def back_block(i, j):
        k = i - j
        if not 0 <= k < 3:
            return None
        return late[k, i // 2 : i // 2 + pairs, i % 2, None, None] * temporal_weight[k].T

    temporal_mix = block_table(4, 2, tap_block)
    temporal_back = block_table(4, 2, back_block)

    def pre_block(i, j):
        b = i // 3 - j
        return spatial_weight[i % 3, b] if 0 <= b < 3 else None

    def grad_block(i, j):
        b = j + 2 - i // 3
        return spatial_weight[i % 3, b].T if 0 <= b < 3 else None

    spatial_mix = block_table(3 * (group + 2), group, pre_block)
    spatial_back = block_table(3 * (group + 2), group, grad_block)

    slope, turned = forward(clip, left, right, temporal_mix, spatial_mix, group)

    def edge_delta(col):
        grads = received[:, :, col].transpose(0, 2, 1, 3, 4).reshape(1, frames, rows, chans)
        return (grads.astype(jnp.float32) * slope[col][None]).astype(jnp.bfloat16)

    first, last = edge_delta(0), edge_delta(width - 1)
    received, first, last = lax.optimization_barrier((received, first, last))
    delta_left, delta_right = column_neighbours(first, last)

    scale = float(frames * rows * total_cols) ** (-0.5)
    delta, local = moments(
        received,
        slope,
        turned,
        masks.astype(jnp.float32),
        jnp.concatenate([temporal_weight[k].T for k in range(3)], axis=1),
        jnp.concatenate([spatial_weight[k // 3, k % 3].T for k in range(9)], axis=0),
        scale,
        group,
    )
    local, delta, delta_left, delta_right = lax.optimization_barrier(
        (local, delta, delta_left, delta_right)
    )

    half = pairs // 2

    def first_half(state):
        grad = backward(*state, spatial_back, None, range(half), group)
        return grad, state

    def second_half(both):
        grad, state = both
        return backward(*state, spatial_back, grad, range(half, pairs), group)

    sums, video_grad = sum_over_devices(
        local.reshape(-1, chans),
        [first_half, second_half, lambda grad: video_gradient(grad, temporal_back)],
        (delta, delta_left, delta_right),
    )
    sums = sums.reshape(12, chans, chans)
    temporal_grad, spatial_grad = sums[:3], sums[3:].reshape(3, 3, chans, chans)
    return video_grad[None], temporal_grad, spatial_grad


def solution(mesh):
    placed = (
        P("width", ("tm", "height"), None, None, None),
        P("width", None, "tm", "height", None),
        P(),
        P(),
        P(),
    )
    return jax.shard_map(
        shards,
        mesh=mesh,
        in_specs=placed,
        out_specs=(P("width", ("tm", "height"), None, None, None), P(), P()),
        check_vma=False,
    )
```

time: 266 us -> 188 us (0.71)
  starting transfers between devices: 85.9 us -> 49.4 us
  Pallas kernels: 71.4 us -> 54.8 us
  local copies, waits for them, and re-layouts: 27.1 us -> 10.9 us
  waiting for transfers between devices: 70.6 us -> 62.9 us
    ppermute x22 -> x11, starting transfers between devices: 67.5 us -> 23.4 us  [exchanged(): lax.ppermute(parts(s), axis, [(i, i ^ s) for i in range(count)])]
    all_to_all x1, waiting for transfers between devices: 2.15 us -> 43.4 us  [shards(): lax.all_to_all(out_grad[0], ('tm', 'height'), split_axis=0, concat_axis=0...]
    ppermute x2, waiting for transfers between devices: 38.8 us -> 6.51 us  [column_neighbours(): right = lax.ppermute(first, MESH_AXES, [(b, a) for a, b in pairs])]
    pallas_call x2 -> x3, Pallas kernels: 45.4 us -> 30.3 us  [the longest x1 22.6 us: moments(): pl.pallas_call(functools.partial(moments_kernel, group, span, extra, scal...]
    ppermute x22 -> x11, waiting for transfers between devices: 20.1 us -> 6.44 us  [exchanged(): lax.ppermute(parts(s), axis, [(i, i ^ s) for i in range(count)])]
    ppermute x2, starting transfers between devices: 7.32 us -> 15 us  [column_neighbours(): left = lax.ppermute(last, MESH_AXES, pairs)]
    unnamed x53 -> x50, local copies, waits for them, and re-layouts: 7.95 us -> 4.09 us
    reshape x2 -> x0, local copies, waits for them, and re-layouts: 3.81 us -> none  [the longest x1 2.05 us: shards(): blocks = spatial_terms.reshape(group, chans, group + 2, 3, chans)]
  transfers between devices with their start and end apart: 27 -> 16, of which waited for: 12 -> 7; matrix products, arithmetic and copies ran while one was open for 9% -> 4% of each run, Pallas kernels for 19% -> 29%
where the time goes in v3:
time: 188 us; the launch traced here: 187 us
  waiting for transfers between devices  62.9 us (33%)
  Pallas kernels  54.8 us (29%)
  starting transfers between devices  49.4 us (26%)
  local copies, waits for them, and re-layouts  10.9 us (6%)
  other arithmetic  7.94 us (4%)
    all_to_all x1, waiting for transfers between devices, shards(): lax.all_to_all(out_grad[0], ('tm', 'height'), split_axis=0, concat_axis=0...  43.4 us
    ppermute x11, starting transfers between devices, exchanged(): lax.ppermute(parts(s), axis, [(i, i ^ s) for i in range(count)])  23.4 us
    pallas_call x1, Pallas kernels, moments(): pl.pallas_call(functools.partial(moments_kernel, group, span, extra, scal...  22.6 us
    pallas_call x1, Pallas kernels, forward(): pl.pallas_call(functools.partial(forward_kernel, group, width, lag), grid...  18.7 us
    ppermute x2, starting transfers between devices, column_neighbours(): left = lax.ppermute(last, MESH_AXES, pairs)  15 us
    all_to_all x1, starting transfers between devices, shards(): lax.all_to_all(out_grad[0], ('tm', 'height'), split_axis=0, concat_axis=0...  8.18 us
    pallas_call x2, Pallas kernels, backward(): pl.pallas_call(functools.partial(backward_kernel, group), grid=(len(pairs...  7.75 us
    ppermute x2, waiting for transfers between devices, column_neighbours(): left = lax.ppermute(last, MESH_AXES, pairs)  6.57 us
  transfers between devices with their start and end apart: 16, of which 7 were waited for; matrix products, arithmetic and copies ran while one was open for 4% of the time, Pallas kernels for 29%

profile of v3, /device:TPU:0, one launch (start us, length us, event | category | flops | bytes accessed | tf_op | source)
XLA Modules:
  0.0 187.2 jit_solution(695670956440814459)
XLA Ops:
  0.6 2.3 %slice_bitcast_fusion.2 = (bf16[1,8,256,128]{3,2,1,0:T(8,128)(2,1)}, bf16[1,8,256,128]{3,2,1,0:T(8,128)(2,1)}) fusion(bf16[1,8,8,256,128]{4,3,2,1,0:T(8,128)(2,1)} %param.5), kind=kLoop, calls=%fused_computation.21 | loop fusion | bytes 2097152 | tf_op jit(solution)/shard_map/slice | solution.py:407
  2.9 4.9 %collective-permute-start = (bf16[1,8,256,128]{3,2,1,0:T(8,128)(2,1)}, bf16[1,8,256,128]{3,2,1,0:T(8,128)(2,1)S(1)}, u32[]{:S(2)}, u32[]{:S(2)}) collective-permute-start(bf16[1,8,256,128]{3,2,1,0:T(8,128)(2,1)} %get-tuple-element.91), channel_id=1, source_target_pairs={{0,2},{2,4},{4,6},{6,8},{8,10},{10,12},{12,14},{14,16},{16,18},{18... | collective-permute-start | bytes 1572872 | tf_op jit(solution)/shard_map/ppermute | solution.py:28
  9.1 8.2 %all-to-all-start = ((bf16[128,2,64,128]{3,2,1,0:T(8,128)(2,1)}), bf16[128,2,64,128]{3,2,1,0:T(8,128)(2,1)}, u32[]{:S(2)}, u32[]{:S(2)}) async-start(bf16[128,2,64,128]{3,2,1,0:T(8,128)(2,1)} %bitcast.124), calls=%async_computation | async-start | bytes 8388608 | tf_op jit(solution)/shard_map/all_to_all | solution.py:408
  21.1 1.7 broadcast_multiply_fusion.8
  22.8 1.7 broadcast_multiply_fusion.2
  24.7 6.6 %collective-permute-done.refs_4_.refs_5_ = bf16[1,8,256,128]{3,2,1,0:T(8,128)(2,1)S(1)} collective-permute-done((bf16[1,8,256,128]{3,2,1,0:T(8,128)(2,1)}, bf16[1,8,256,128]{3,2,1,0:T(8,128)(2,1)S(1)}, u32[]{:S(2)}, u32[]{:S(2)}) %collective-permute-start) | collective-permute-done | bytes 524320 | tf_op jit(solution)/shard_map/ppermute | solution.py:28
  31.3 2.1 %collective-permute-done.1.refs_6_.refs_7_ = bf16[1,8,256,128]{3,2,1,0:T(8,128)(2,1)S(1)} collective-permute-done((bf16[1,8,256,128]{3,2,1,0:T(8,128)(2,1)}, bf16[1,8,256,128]{3,2,1,0:T(8,128)(2,1)S(1)}, u32[]{:S(2)}, u32[]{:S(2)}) %collective-permute-start.1) | collective-permute-done | bytes 524320 | tf_op jit(solution)/shard_map/ppermute | solution.py:29
  33.4 18.7 %shard_map.76 = (f32[8,8,256,128]{3,2,1,0:T(8,128)}, bf16[10,8,128,256]{3,2,1,0:T(8,128)(2,1)S(1)}) custom-call(bf16[8,8,256,128]{3,2,1,0:T(8,128)(2,1)S(1)} %bitcast.118, bf16[8,8,256,128]{3,2,1,0:T(8,128)(2,1)S(1)} %bitcast.119, bf16[8,8,256,128]{3,2,1,0:T(8,128)(2,1)S(1)} %bitcast.120, bf16[8,8,256,128]{3,2,1,0:T(8,128)(2,1)S(1)} %bitcast.121, ...), custom_call_target="tpu_custom_call" | custom-call | flops 12884901888 | bytes 29360128 | tf_op jit(solution)/shard_map/pallas_call | solution.py:115
  52.1 2.4 %copy-done.1 = bf16[10,8,128,256]{3,2,1,0:T(8,128)(2,1)} copy-done((bf16[10,8,128,256]{3,2,1,0:T(8,128)(2,1)}, bf16[10,8,128,256]{3,2,1,0:T(8,128)(2,1)S(1)}, u32[]{:S(2)}) %copy-start.1) | copy-done | bytes 5242904
  54.5 43.4 %all-to-all-done = bf16[128,2,64,128]{3,2,1,0:T(8,128)(2,1)} async-done(((bf16[128,2,64,128]{3,2,1,0:T(8,128)(2,1)}), bf16[128,2,64,128]{3,2,1,0:T(8,128)(2,1)}, u32[]{:S(2)}, u32[]{:S(2)}) %all-to-all-start) | async-done | bytes 4194336 | tf_op jit(solution)/shard_map/all_to_all | solution.py:408
  99.5 1.8 multiply_convert_fusion
  101.3 10.1 %collective-permute-start.2 = (bf16[1,8,256,128]{3,2,1,0:T(8,128)(2,1)S(1)}, bf16[1,8,256,128]{3,2,1,0:T(8,128)(2,1)S(1)}, u32[]{:S(2)}, u32[]{:S(2)}) collective-permute-start(bf16[1,8,256,128]{3,2,1,0:T(8,128)(2,1)S(1)} %get-tuple-element.45), channel_id=1, source_target_pairs={{0,2},{2,4},{4,6},{6,8},{8,10},{10,12},{12,14},{14,16},{16,18},{18... | collective-permute-start | bytes 1572872 | tf_op jit(solution)/shard_map/ppermute | solution.py:28
  111.4 1.5 collective-permute-start.3
  112.9 22.6 %shard_map.77 = (bf16[8,8,256,128]{3,2,1,0:T(8,128)(2,1)S(1)}, f32[12,128,128]{2,1,0:T(8,128)S(1)}) custom-call(f32[3,8]{1,0:T(4,128)S(1)} %fusion.14.masks, bf16[4,4,8,2,64,128]{5,4,3,2,1,0:T(8,128)(2,1)} %bitcast.4.refs_0_, f32[8,8,256,128]{3,2,1,0:T(8,128)} %get-tuple-element.40.refs_1_, bf16[10,8,128,256]{3,2,1,0:T(8,128)(2,1)} %copy-done.1, ...), custom_call_target="tpu_custom_call" | custom-call | flops 16106127360 | bytes 41943040 | tf_op jit(solution)/shard_map/pallas_call | solution.py:239
  135.5 4.4 %collective-permute-done.3.refs_2_ = bf16[1,8,256,128]{3,2,1,0:T(8,128)(2,1)S(1)} collective-permute-done((bf16[1,8,256,128]{3,2,1,0:T(8,128)(2,1)S(1)}, bf16[1,8,256,128]{3,2,1,0:T(8,128)(2,1)S(1)}, u32[]{:S(2)}, u32[]{:S(2)}) %collective-permute-start.3) | collective-permute-done | bytes 524320 | tf_op jit(solution)/shard_map/ppermute | solution.py:29
  140.0 11.8 %collective-permute-start.4 = (f32[768,128]{1,0:T(8,128)S(1)}, f32[768,128]{1,0:T(8,128)S(1)}, u32[]{:S(2)}, u32[]{:S(2)}) collective-permute-start(f32[768,128]{1,0:T(8,128)S(1)} %dynamic-slice_bitcast_fusion), channel_id=1, source_target_pairs={{0,1},{1,0},{2,3},{3,2},{4,5},{5,4},{6,7},{7,6},{8,9},{9,8},{10,11... | collective-permute-start | bytes 1179656 | tf_op jit(solution)/shard_map/ppermute | solution.py:358
  153.4 3.4 %collective-permute-start.7 = (f32[192,128]{1,0:T(8,128)S(1)}, f32[192,128]{1,0:T(8,128)S(1)}, u32[]{:S(2)}, u32[]{:S(2)}) collective-permute-start(f32[192,128]{1,0:T(8,128)S(1)} %get-tuple-element.92), channel_id=1, source_target_pairs={{0,6},{2,4},{4,2},{6,0},{1,7},{3,5},{5,3},{7,1},{8,14},{10,12},{12... | collective-permute-start | bytes 294920 | tf_op jit(solution)/shard_map/ppermute | solution.py:358
  156.8 3.9 %shard_map.78.refs_4_ = bf16[8,8,256,128]{3,2,1,0:T(8,128)(2,1)S(1)} custom-call(bf16[8,8,256,128]{3,2,1,0:T(8,128)(2,1)S(1)} %get-tuple-element.63.refs_0_, bf16[1,8,256,128]{3,2,1,0:T(8,128)(2,1)S(1)} %collective-permute-done.2.refs_1_, bf16[1,8,256,128]{3,2,1,0:T(8,128)(2,1)S(1)} %collective-permute-done.3.refs_2_, ...), custom_call_target="tpu_custom_call" | custom-call | flops 4831838208 | bytes 6291456 | tf_op jit(solution)/shard_map/pallas_call | solution.py:299
  160.7 1.6 collective-permute-start.10
  163.6 1.5 collective-permute-start.9
  165.2 3.9 %shard_map.79.now.after = bf16[8,8,256,128]{3,2,1,0:T(8,128)(2,1)S(1)} custom-call(bf16[8,8,256,128]{3,2,1,0:T(8,128)(2,1)S(1)} %get-tuple-element.63.refs_0_, bf16[1,8,256,128]{3,2,1,0:T(8,128)(2,1)S(1)} %collective-permute-done.2.refs_1_, bf16[1,8,256,128]{3,2,1,0:T(8,128)(2,1)S(1)} %collective-permute-done.3.refs_2_, ...), custom_call_target="tpu_custom_call", output_to_operand_aliasing={{}: (4, {})} | custom-call | flops 4831838208 | bytes 6291456 | tf_op jit(solution)/shard_map/pallas_call | solution.py:299
  169.1 3.9 %collective-permute-done.9 = f32[192,128]{1,0:T(8,128)S(1)} collective-permute-done((f32[192,128]{1,0:T(8,128)S(1)}, f32[192,128]{1,0:T(8,128)S(1)}, u32[]{:S(2)}, u32[]{:S(2)}) %collective-permute-start.9) | collective-permute-done | bytes 98336 | tf_op jit(solution)/shard_map/ppermute | solution.py:358
  174.5 2.0 %collective-permute-start.13 = (f32[192,128]{1,0:T(8,128)S(1)}, f32[192,128]{1,0:T(8,128)S(1)}, u32[]{:S(2)}, u32[]{:S(2)}) collective-permute-start(f32[192,128]{1,0:T(8,128)S(1)} %add_add_fusion), channel_id=1, source_target_pairs={{0,6},{2,4},{4,2},{6,0},{1,7},{3,5},{5,3},{7,1},{8,14},{10,12},{12... | collective-permute-start | bytes 294920 | tf_op jit(solution)/shard_map/ppermute | solution.py:358
  176.5 5.8 %shard_map.80 = bf16[8,8,256,128]{3,2,1,0:T(8,128)(2,1)} custom-call(bf16[8,8,256,128]{3,2,1,0:T(8,128)(2,1)S(1)} %shard_map.79.now.after, bf16[8,8,256,128]{3,2,1,0:T(8,128)(2,1)S(1)} %shard_map.79.now.after, bf16[4,512,256]{2,1,0:T(8,128)(2,1)S(1)} %fusion.9.weights), custom_call_target="tpu_custom_call" | custom-call | flops 3221225472 | bytes 12582912 | tf_op jit(solution)/shard_map/pallas_call | solution.py:336
  (124 shorter events, 16.0 us)
Async XLA Ops:
  2.9 28.4 %collective-permute-start = (bf16[1,8,256,128]{3,2,1,0:T(8,128)(2,1)}, bf16[1,8,256,128]{3,2,1,0:T(8,128)(2,1)S(1)}, u32[]{:S(2)}, u32[]{:S(2)}) collective-permute-start(bf16[1,8,256,128]{3,2,1,0:T(8,128)(2,1)} %get-tuple-element.91), channel_id=1, source_target_pairs={{0,2},{2,4},{4,6},{6,8},{8,10},{10,12},{12,14},{14,16},{16,18},{18... | collective-permute-start | bytes 1572872 | tf_op jit(solution)/shard_map/ppermute | solution.py:28
  7.8 25.7 %collective-permute-start.1 = (bf16[1,8,256,128]{3,2,1,0:T(8,128)(2,1)}, bf16[1,8,256,128]{3,2,1,0:T(8,128)(2,1)S(1)}, u32[]{:S(2)}, u32[]{:S(2)}) collective-permute-start(bf16[1,8,256,128]{3,2,1,0:T(8,128)(2,1)} %get-tuple-element.90), channel_id=1, source_target_pairs={{2,0},{4,2},{6,4},{8,6},{10,8},{12,10},{14,12},{16,14},{18,16},{20... | collective-permute-start | bytes 1572872 | tf_op jit(solution)/shard_map/ppermute | solution.py:29
  9.1 8.4 %copy-start.8 = (bf16[3,128,128]{2,1,0:T(8,128)(2,1)S(1)}, bf16[3,128,128]{2,1,0:T(8,128)(2,1)}, u32[]{:S(2)}) copy-start(bf16[3,128,128]{2,1,0:T(8,128)(2,1)} %param.8) | copy-start | bytes 294916
  9.1 9.1 %copy-start.7 = (bf16[3,3,128,128]{3,2,1,0:T(8,128)(2,1)S(1)}, bf16[3,3,128,128]{3,2,1,0:T(8,128)(2,1)}, u32[]{:S(2)}) copy-start(bf16[3,3,128,128]{3,2,1,0:T(8,128)(2,1)} %param.9) | copy-start | bytes 884740
  9.1 88.8 %all-to-all-start = ((bf16[128,2,64,128]{3,2,1,0:T(8,128)(2,1)}), bf16[128,2,64,128]{3,2,1,0:T(8,128)(2,1)}, u32[]{:S(2)}, u32[]{:S(2)}) async-start(bf16[128,2,64,128]{3,2,1,0:T(8,128)(2,1)} %bitcast.124), calls=%async_computation | async-start | bytes 8388608 | tf_op jit(solution)/shard_map/all_to_all | solution.py:408
  21.1 12.3 %copy-start = (bf16[1,8,8,256,128]{4,3,2,1,0:T(8,128)(2,1)S(1)}, bf16[1,8,8,256,128]{4,3,2,1,0:T(8,128)(2,1)}, u32[]{:S(2)}) copy-start(bf16[1,8,8,256,128]{4,3,2,1,0:T(8,128)(2,1)} %param.5) | copy-start | bytes 12582916
  101.3 34.3 %collective-permute-start.2 = (bf16[1,8,256,128]{3,2,1,0:T(8,128)(2,1)S(1)}, bf16[1,8,256,128]{3,2,1,0:T(8,128)(2,1)S(1)}, u32[]{:S(2)}, u32[]{:S(2)}) collective-permute-start(bf16[1,8,256,128]{3,2,1,0:T(8,128)(2,1)S(1)} %get-tuple-element.45), channel_id=1, source_target_pairs={{0,2},{2,4},{4,6},{6,8},{8,10},{10,12},{12,14},{14,16},{16,18},{18... | collective-permute-start | bytes 1572872 | tf_op jit(solution)/shard_map/ppermute | solution.py:28
  111.4 28.5 %collective-permute-start.3 = (bf16[1,8,256,128]{3,2,1,0:T(8,128)(2,1)S(1)}, bf16[1,8,256,128]{3,2,1,0:T(8,128)(2,1)S(1)}, u32[]{:S(2)}, u32[]{:S(2)}) collective-permute-start(bf16[1,8,256,128]{3,2,1,0:T(8,128)(2,1)S(1)} %get-tuple-element.46), channel_id=1, source_target_pairs={{2,0},{4,2},{6,4},{8,6},{10,8},{12,10},{14,12},{16,14},{18,16},{20... | collective-permute-start | bytes 1572872 | tf_op jit(solution)/shard_map/ppermute | solution.py:29
  112.9 38.9 %copy-start.2 = (bf16[4,128,128]{2,1,0:T(8,128)(2,1)S(1)}, bf16[4,128,128]{2,1,0:T(8,128)(2,1)}, u32[]{:S(2)}) copy-start(bf16[4,128,128]{2,1,0:T(8,128)(2,1)} %get-tuple-element.126) | copy-start | bytes 393220
  112.9 38.9 %copy-start.3 = (bf16[4,128,128]{2,1,0:T(8,128)(2,1)S(1)}, bf16[4,128,128]{2,1,0:T(8,128)(2,1)}, u32[]{:S(2)}) copy-start(bf16[4,128,128]{2,1,0:T(8,128)(2,1)} %get-tuple-element.114) | copy-start | bytes 393220
  112.9 38.9 %copy-start.4 = (bf16[4,128,128]{2,1,0:T(8,128)(2,1)S(1)}, bf16[4,128,128]{2,1,0:T(8,128)(2,1)}, u32[]{:S(2)}) copy-start(bf16[4,128,128]{2,1,0:T(8,128)(2,1)} %get-tuple-element.115) | copy-start | bytes 393220
  112.9 38.9 %copy-start.5 = (bf16[4,128,128]{2,1,0:T(8,128)(2,1)S(1)}, bf16[4,128,128]{2,1,0:T(8,128)(2,1)}, u32[]{:S(2)}) copy-start(bf16[4,128,128]{2,1,0:T(8,128)(2,1)} %get-tuple-element.134) | copy-start | bytes 393220
  112.9 38.9 %copy-start.6 = (bf16[4,128,128]{2,1,0:T(8,128)(2,1)S(1)}, bf16[4,128,128]{2,1,0:T(8,128)(2,1)}, u32[]{:S(2)}) copy-start(bf16[4,128,128]{2,1,0:T(8,128)(2,1)} %get-tuple-element.135) | copy-start | bytes 393220
  140.0 13.2 %collective-permute-start.4 = (f32[768,128]{1,0:T(8,128)S(1)}, f32[768,128]{1,0:T(8,128)S(1)}, u32[]{:S(2)}, u32[]{:S(2)}) collective-permute-start(f32[768,128]{1,0:T(8,128)S(1)} %dynamic-slice_bitcast_fusion), channel_id=1, source_target_pairs={{0,1},{1,0},{2,3},{3,2},{4,5},{5,4},{6,7},{7,6},{8,9},{9,8},{10,11... | collective-permute-start | bytes 1179656 | tf_op jit(solution)/shard_map/ppermute | solution.py:358
  153.2 7.5 %collective-permute-start.5 = (f32[192,128]{1,0:T(8,128)S(1)}, f32[192,128]{1,0:T(8,128)S(1)}, u32[]{:S(2)}, u32[]{:S(2)}) collective-permute-start(f32[192,128]{1,0:T(8,128)S(1)} %get-tuple-element.94), channel_id=1, source_target_pairs={{0,2},{2,0},{4,6},{6,4},{1,3},{3,1},{5,7},{7,5},{8,10},{10,8},{12,... | collective-permute-start | bytes 294920 | tf_op jit(solution)/shard_map/ppermute | solution.py:358
  153.3 7.4 %collective-permute-start.6 = (f32[192,128]{1,0:T(8,128)S(1)}, f32[192,128]{1,0:T(8,128)S(1)}, u32[]{:S(2)}, u32[]{:S(2)}) collective-permute-start(f32[192,128]{1,0:T(8,128)S(1)} %get-tuple-element.93), channel_id=1, source_target_pairs={{0,4},{2,6},{4,0},{6,2},{1,5},{3,7},{5,1},{7,3},{8,12},{10,14},{12... | collective-permute-start | bytes 294920 | tf_op jit(solution)/shard_map/ppermute | solution.py:358
  153.4 7.3 %collective-permute-start.7 = (f32[192,128]{1,0:T(8,128)S(1)}, f32[192,128]{1,0:T(8,128)S(1)}, u32[]{:S(2)}, u32[]{:S(2)}) collective-permute-start(f32[192,128]{1,0:T(8,128)S(1)} %get-tuple-element.92), channel_id=1, source_target_pairs={{0,6},{2,4},{4,2},{6,0},{1,7},{3,5},{5,3},{7,1},{8,14},{10,12},{12... | collective-permute-start | bytes 294920 | tf_op jit(solution)/shard_map/ppermute | solution.py:358
  160.7 8.3 %collective-permute-start.10 = (f32[192,128]{1,0:T(8,128)S(1)}, f32[192,128]{1,0:T(8,128)S(1)}, u32[]{:S(2)}, u32[]{:S(2)}) collective-permute-start(f32[192,128]{1,0:T(8,128)S(1)} %fusion.11), channel_id=1, source_target_pairs={{0,24},{8,16},{16,8},{24,0},{1,25},{9,17},{17,9},{25,1},{2,26},{10... | collective-permute-start | bytes 294920 | tf_op jit(solution)/shard_map/ppermute | solution.py:358
  162.3 6.8 %collective-permute-start.8 = (f32[192,128]{1,0:T(8,128)S(1)}, f32[192,128]{1,0:T(8,128)S(1)}, u32[]{:S(2)}, u32[]{:S(2)}) collective-permute-start(f32[192,128]{1,0:T(8,128)S(1)} %fusion.11), channel_id=1, source_target_pairs={{0,8},{8,0},{16,24},{24,16},{1,9},{9,1},{17,25},{25,17},{2,10},{10... | collective-permute-start | bytes 294920 | tf_op jit(solution)/shard_map/ppermute | solution.py:358
  163.6 9.3 %collective-permute-start.9 = (f32[192,128]{1,0:T(8,128)S(1)}, f32[192,128]{1,0:T(8,128)S(1)}, u32[]{:S(2)}, u32[]{:S(2)}) collective-permute-start(f32[192,128]{1,0:T(8,128)S(1)} %fusion.11), channel_id=1, source_target_pairs={{0,16},{8,24},{16,0},{24,8},{1,17},{9,25},{17,1},{25,9},{2,18},{10... | collective-permute-start | bytes 294920 | tf_op jit(solution)/shard_map/ppermute | solution.py:358
  173.0 9.3 %collective-permute-start.11 = (f32[192,128]{1,0:T(8,128)S(1)}, f32[192,128]{1,0:T(8,128)S(1)}, u32[]{:S(2)}, u32[]{:S(2)}) collective-permute-start(f32[192,128]{1,0:T(8,128)S(1)} %add_add_fusion), channel_id=1, source_target_pairs={{0,2},{2,0},{4,6},{6,4},{1,3},{3,1},{5,7},{7,5},{8,10},{10,8},{12,... | collective-permute-start | bytes 294920 | tf_op jit(solution)/shard_map/ppermute | solution.py:358
  173.4 8.9 %collective-permute-start.12 = (f32[192,128]{1,0:T(8,128)S(1)}, f32[192,128]{1,0:T(8,128)S(1)}, u32[]{:S(2)}, u32[]{:S(2)}) collective-permute-start(f32[192,128]{1,0:T(8,128)S(1)} %add_add_fusion), channel_id=1, source_target_pairs={{0,4},{2,6},{4,0},{6,2},{1,5},{3,7},{5,1},{7,3},{8,12},{10,14},{12... | collective-permute-start | bytes 294920 | tf_op jit(solution)/shard_map/ppermute | solution.py:358
  174.5 7.8 %collective-permute-start.13 = (f32[192,128]{1,0:T(8,128)S(1)}, f32[192,128]{1,0:T(8,128)S(1)}, u32[]{:S(2)}, u32[]{:S(2)}) collective-permute-start(f32[192,128]{1,0:T(8,128)S(1)} %add_add_fusion), channel_id=1, source_target_pairs={{0,6},{2,4},{4,2},{6,0},{1,7},{3,5},{5,3},{7,1},{8,14},{10,12},{12... | collective-permute-start | bytes 294920 | tf_op jit(solution)/shard_map/ppermute | solution.py:358
  183.1 1.8 collective-permute-start.14
  (2 other events, 10.6 us)

commit v4 on v3

v4 whole, which is shorter than its diff:
```python
import functools

import jax
import jax.numpy as jnp
from jax import lax
from jax.experimental import pallas as pl
from jax.experimental.pallas import tpu as pltpu
from jax.sharding import PartitionSpec as P

MESH_AXES = ("tm", "height", "width")
MIB = 1024 * 1024


def column_neighbours(first, last):
    n_tm, n_height, n_width = (lax.axis_size(axis) for axis in MESH_AXES)
    blocks = n_tm * n_height
    place = [(pos % blocks) * n_width + pos // blocks for pos in range(blocks * n_width)]
    pairs = list(zip(place[:-1], place[1:]))
    left = lax.ppermute(last, MESH_AXES, pairs)
    right = lax.ppermute(first, MESH_AXES, [(b, a) for a, b in pairs])
    return left, right


def prepare_kernel(group, lengths, temporal, spatial, *outs):
    mix, back, pre, grad, temporal_turned, spatial_turned, masks = outs
    frames, chans = masks.shape[1], temporal.shape[1]
    end, spans = jnp.int32(0), []
    for n in range(lengths.shape[0]):
        spans.append((end, end + lengths[n]))
        end = end + lengths[n]
    keep = []
    for frame in range(frames):
        first = jnp.int32(0)
        for start, stop in spans:
            first = first + jnp.where((frame >= start) & (frame < stop), start, 0)
        keep.append([jnp.where(frame - lag >= first, 1.0, 0.0) for lag in range(3)])
    for lag in range(3):
        for frame in range(frames):
            masks[lag, frame] = keep[frame][lag]

    zero = jnp.zeros((chans, chans), jnp.bfloat16)
    turned = [temporal[k].T for k in range(3)]
    for i in range(4):
        for j in range(2):
            at = (slice(i * chans, (i + 1) * chans), slice(j * chans, (j + 1) * chans))
            for p in range(frames // 2):
                k, frame = 2 + j - i, 2 * p + j
                value = zero
                if 0 <= k < 3:
                    value = jnp.where(keep[frame][k] > 0, temporal[k], zero)
                mix[(p, *at)] = value
                k, frame = i - j, 2 * p + i
                value = zero
                if 0 <= k < 3 and frame < frames:
                    value = jnp.where(keep[frame][k] > 0, turned[k], zero)
                back[(p, *at)] = value
    for k in range(3):
        temporal_turned[:, k * chans : (k + 1) * chans] = turned[k]
    for a in range(3):
        for b in range(3):
            value = spatial[a, b].T
            n = 3 * a + b
            spatial_turned[n * chans : (n + 1) * chans] = value
            for j in range(group):
                at = slice(j * chans, (j + 1) * chans)
                i = 3 * (b + j) + a
                pre[i * chans : (i + 1) * chans, at] = spatial[a, b]
                i = 3 * (j + 2 - b) + a
                grad[i * chans : (i + 1) * chans, at] = value
    for j in range(group):
        for i in range(group + 2):
            if not 0 <= i - j < 3:
                at = (slice(3 * i * chans, 3 * (i + 1) * chans), slice(j * chans, (j + 1) * chans))
                pre[at] = jnp.zeros((3 * chans, chans), jnp.bfloat16)
                grad[at] = jnp.zeros((3 * chans, chans), jnp.bfloat16)


def prepare(lengths, temporal, spatial, frames, group):
    chans = temporal.shape[1]

    def wide(*shape):
        return jax.ShapeDtypeStruct(shape, jnp.bfloat16)

    vmem, smem = pl.BlockSpec(memory_space=pltpu.VMEM), pl.BlockSpec(memory_space=pltpu.SMEM)
    return pl.pallas_call(
        functools.partial(prepare_kernel, group),
        in_specs=[smem, vmem, vmem],
        out_specs=[vmem] * 6 + [smem],
        out_shape=[
            wide(frames // 2, 4 * chans, 2 * chans),
            wide(frames // 2, 4 * chans, 2 * chans),
            wide(3 * (group + 2) * chans, group * chans),
            wide(3 * (group + 2) * chans, group * chans),
            wide(chans, 3 * chans),
            wide(9 * chans, chans),
            jax.ShapeDtypeStruct((3, frames), jnp.float32),
        ],
        compiler_params=pltpu.CompilerParams(vmem_limit_bytes=24 * MIB),
        cost_estimate=pl.CostEstimate(flops=0, bytes_accessed=4 << 20, transcendentals=0),
    )(lengths, temporal, spatial)


def row_shifts(block, rows):
    index = lax.broadcasted_iota(jnp.int32, block.shape, 0)
    above = jnp.where(index == 0, 0.0, pltpu.roll(block, 1, 0))
    below = jnp.where(index == rows - 1, 0.0, pltpu.roll(block, rows - 1, 0))
    return above.astype(jnp.bfloat16), below.astype(jnp.bfloat16)


def lanes(parts):
    return parts[0] if len(parts) == 1 else jnp.concatenate(parts, axis=1)


def forward_kernel(group, width, lag, *refs):
    now, before = refs[:group], refs[group : 2 * group]
    left, left_before, right, right_before, temporal, spatial, slope, turned, held = refs[2 * group :]
    step = pl.program_id(1)
    rows, chans = slope.shape[2], slope.shape[3]
    sources = []
    for e in range(group):
        line = []
        for ours, l_ref, r_ref in ((before[e], left_before, right_before), (now[e], left, right)):
            for frame in range(2):
                tile = ours[0, frame]
                if e == 0:
                    tile = jnp.where(step == 0, l_ref[0, frame], tile)
                if e == group - 1:
                    tile = jnp.where(step * group + e == width + 1, r_ref[0, frame], tile)
                line.append(tile)
                if ours is now[e]:
                    turned[e, frame] = tile.T
        sources.append(lanes(line))
    mixed = jnp.dot(
        jnp.concatenate(sources, axis=0), temporal[0], preferred_element_type=jnp.float32
    ).astype(jnp.bfloat16)
    for e in range(group):
        value = mixed[e * rows : (e + 1) * rows]
        above, below = row_shifts(value.astype(jnp.float32), rows)
        for frame in range(2):
            at = slice(frame * chans, (frame + 1) * chans)
            held[step * group + e, frame] = lanes([above[:, at], value[:, at], below[:, at]])

    @pl.when(step >= lag)
    def _():
        base = (step - lag) * group
        source = lanes([held[base + k].reshape(2 * rows, 3 * chans) for k in range(group + 2)])
        pre = jnp.dot(source, spatial[...], preferred_element_type=jnp.float32)
        sig = jax.nn.sigmoid(pre)
        value = sig * (1.0 + pre * (1.0 - sig))
        for e in range(group):
            slope[e] = value[:, e * chans : (e + 1) * chans].reshape(2, rows, chans)


def forward(video, left, right, temporal, spatial, group):
    width, frames, rows, chans = video.shape
    lag = 2 // group
    steps = (width + 2) // group

    def own(e, back):
        return pl.BlockSpec(
            (1, 2, rows, chans),
            lambda p, j: (
                jnp.clip(j * group + e - 1, 0, width - 1),
                jnp.maximum(p - back, 0),
                0,
                0,
            ),
        )

    def edge(back):
        return pl.BlockSpec((1, 2, rows, chans), lambda p, j: (0, jnp.maximum(p - back, 0), 0, 0))

    out = pl.BlockSpec((group, 2, rows, chans), lambda p, j: (jnp.maximum(j - lag, 0), p, 0, 0))
    pixels = width * frames * rows
    return pl.pallas_call(
        functools.partial(forward_kernel, group, width, lag),
        grid=(frames // 2, steps),
        in_specs=[own(e, 0) for e in range(group)]
        + [own(e, 1) for e in range(group)]
        + [
            edge(0),
            edge(1),
            edge(0),
            edge(1),
            pl.BlockSpec((1, 4 * chans, 2 * chans), lambda p, j: (p, 0, 0)),
            pl.BlockSpec(spatial.shape, lambda p, j: (0, 0)),
        ],
        out_specs=[out, pl.BlockSpec((group, 2, chans, rows), lambda p, j: (j, p, 0, 0))],
        out_shape=[
            jax.ShapeDtypeStruct((width, frames, rows, chans), jnp.float32),
            jax.ShapeDtypeStruct((width + 2, frames, chans, rows), jnp.bfloat16),
        ],
        scratch_shapes=[pltpu.VMEM((width + 2, 2, rows, 3 * chans), jnp.bfloat16)],
        compiler_params=pltpu.CompilerParams(vmem_limit_bytes=60 * MIB),
        cost_estimate=pl.CostEstimate(
            flops=pixels * chans * chans * 2 * 24 * 5,
            bytes_accessed=pixels * chans * 14,
            transcendentals=pixels * chans,
        ),
    )(*([video] * (2 * group)), left, left, right, right, temporal, spatial)


def moments_kernel(group, groups, places, edges, scale, masks, *refs):
    count = len(groups)
    grads, refs = refs[0], refs[1:]
    slopes, refs = refs[:count], refs[count:]
    now, before, refs = refs[: len(places)], refs[len(places) : 2 * len(places)], refs[2 * len(places) :]
    temporal, spatial, refs = refs[0], refs[1], refs[2:]
    total, refs = refs[-1], refs[:-1]
    if edges:
        head, tail, refs, earlier = refs[-2], refs[-1], refs[:-2], None
    else:
        earlier, refs = refs[0], refs[1:]
    deltas, sums = refs[:count], refs[count]
    pair = pl.program_id(0)
    bands, band = grads.shape[1], grads.shape[4]
    rows, chans = slopes[0].shape[2], slopes[0].shape[3]

    @pl.when(pair == 0)
    def _():
        total[...] = jnp.zeros_like(total)

    parts = [(n, frame) for frame in range(2) for n in range(count)]
    triples = []
    for n, frame in parts:
        line = []
        for e in range(group):
            for b in range(bands):
                at = slice(b * band, (b + 1) * band)
                value = grads[0, b, n * group + e, frame].astype(jnp.float32)
                deltas[n][e, frame, at] = (value * slopes[n][e, frame, at]).astype(jnp.bfloat16)
            value = deltas[n][e, frame]
            above, below = row_shifts(value.astype(jnp.float32), rows)
            line += [below, value, above]
        triples.append(lanes(line))
    right = jnp.concatenate(triples, axis=0)
    if edges:
        head[0] = deltas[0][0]
        tail[0] = deltas[-1][group - 1]

    def add(lag, left, right):
        total[lag] += jnp.dot(left, right, preferred_element_type=jnp.float32)

    def turned(refs, n, frame):
        first = groups[n] * group
        return jnp.concatenate(
            [
                refs[places.index(c // group)][c % group, frame]
                for c in range(first, first + group + 2)
            ],
            axis=0,
        )

    add(0, lanes([turned(now, n, frame) for n, frame in parts]), right)
    rest = count * rows
    for lag, frame, source, other in (
        (1, 0, before, 1),
        (1, 1, now, 0),
        (2, 0, before, 0),
        (2, 1, before, 1),
    ):

        @pl.when(masks[lag, 2 * pair + frame] > 0)
        def _():
            left = lanes([turned(source, n, other) for n in range(count)])
            add(lag, left, right[frame * rest : (frame + 1) * rest])

    @pl.when(pair == pl.num_programs(0) - 1)
    def _():
        lines = []
        for lag in range(3):
            line = []
            for a in range(3):
                for b in range(3):
                    line.append(
                        sum(
                            total[
                                lag,
                                (j + b) * chans : (j + b + 1) * chans,
                                (j * 3 + a) * chans : (j * 3 + a + 1) * chans,
                            ]
                            for j in range(group)
                        )
                    )
            lines.append(lanes(line))
        moments = jnp.concatenate(lines, axis=0)
        high = moments.astype(jnp.bfloat16)
        low = (moments - high.astype(jnp.float32)).astype(jnp.bfloat16)

        def product(left, right):
            return jnp.dot(left, right, preferred_element_type=jnp.float32)

        spatial_sum = product(temporal[...], high) + product(temporal[...], low)
        temporal_sum = product(high, spatial[...]) + product(low, spatial[...])
        for k in range(3):
            value = temporal_sum[k * chans : (k + 1) * chans] * scale
            sums[k] = value if earlier is None else earlier[k] + value
        for k in range(9):
            value = spatial_sum[:, k * chans : (k + 1) * chans] * scale
            sums[3 + k] = value if earlier is None else earlier[3 + k] + value


def moments(received, slope, turned, masks, temporal, spatial, earlier, groups, group):
    edges = earlier is None
    frames, rows, chans = slope.shape[1:]
    bands, band = received.shape[1], received.shape[4]
    count = len(groups)
    places = sorted({n + k for n in groups for k in range(2 // group + 1)})
    pixels = count * group * frames * rows
    scale = float(frames * rows * slope.shape[0] * lax.axis_size(MESH_AXES)) ** (-0.5)

    def own(n):
        return pl.BlockSpec((group, 2, rows, chans), lambda p, m: (n, p, 0, 0))

    def columns(n, back):
        return pl.BlockSpec(
            (group, 2, chans, rows), lambda p, m: (n, jnp.maximum(p - back, 0), 0, 0)
        )

    def whole(shape):
        return pl.BlockSpec(shape, lambda p, m: (0,) * len(shape))

    edge = pl.BlockSpec((1, 2, rows, chans), lambda p, m: (0, p, 0, 0))
    edge_shape = jax.ShapeDtypeStruct((1, frames, rows, chans), jnp.bfloat16)
    sums_shape = (12, chans, chans)
    outs = pl.pallas_call(
        functools.partial(moments_kernel, group, groups, places, edges, scale),
        grid_spec=pltpu.PrefetchScalarGridSpec(
            num_scalar_prefetch=1,
            grid=(frames // 2,),
            in_specs=[
                pl.BlockSpec(
                    (1, bands, count * group, 2, band, chans), lambda p, m: (p, 0, 0, 0, 0, 0)
                )
            ]
            + [own(n) for n in groups]
            + [columns(n, 0) for n in places]
            + [columns(n, 1) for n in places]
            + [whole(temporal.shape), whole(spatial.shape)]
            + ([] if edges else [whole(sums_shape)]),
            out_specs=[own(0) for _ in groups]
            + [whole(sums_shape)]
            + ([edge, edge] if edges else []),
            scratch_shapes=[
                pltpu.VMEM((3, (group + 2) * chans, group * 3 * chans), jnp.float32),
            ],
        ),
        out_shape=[jax.ShapeDtypeStruct((group, frames, rows, chans), jnp.bfloat16)] * count
        + [jax.ShapeDtypeStruct(sums_shape, jnp.float32)]
        + ([edge_shape, edge_shape] if edges else []),
        compiler_params=pltpu.CompilerParams(vmem_limit_bytes=60 * MIB),
        cost_estimate=pl.CostEstimate(
            flops=pixels * chans * chans * 2 * 30,
            bytes_accessed=pixels * chans * 20,
            transcendentals=0,
        ),
    )(
        masks,
        received,
        *([slope] * count),
        *([turned] * (2 * len(places))),
        temporal,
        spatial,
        *([] if edges else [earlier]),
    )
    return outs[:count], outs[count], outs[count + 1 :]


def backward_kernel(group, sources, *refs):
    spatial, temporal = refs[len(sources) : len(sources) + 2]
    out, later = refs[-2:]
    cols, rows, chans = out.shape[0], out.shape[2], out.shape[3]

    @pl.when(pl.program_id(0) == 0)
    def _():
        later[...] = jnp.zeros_like(later)

    triples = []
    for ref, col in zip(refs, sources):
        lines = []
        for frame in range(2):
            value = ref[col, frame]
            above, below = row_shifts(value.astype(jnp.float32), rows)
            lines.append(lanes([below, value, above]))
        triples.append(jnp.concatenate(lines, axis=0))
    grad = []
    for base in range(0, cols, group):
        source = lanes(triples[base : base + group + 2])
        back = jnp.dot(source, spatial[...], preferred_element_type=jnp.float32)
        back = back.astype(jnp.bfloat16)
        for e in range(group):
            at = slice(e * chans, (e + 1) * chans)
            grad.append(lanes([back[f * rows : (f + 1) * rows, at] for f in range(2)]))
    grad = jnp.concatenate(grad, axis=0)
    value = jnp.dot(
        lanes([grad, later[...]]), temporal[0], preferred_element_type=jnp.float32
    ).astype(jnp.bfloat16)
    later[...] = grad
    for col in range(cols):
        for frame in range(2):
            out[col, frame] = value[
                col * rows : (col + 1) * rows, frame * chans : (frame + 1) * chans
            ]


def backward(deltas, left, right, spatial, temporal, filled, first, cols):
    group, frames, rows, chans = deltas[0].shape
    width = group * len(deltas)
    filled = [] if filled is None else [filled]
    ext = [(left, 0)] + [(d, e) for d in deltas for e in range(group)] + [(right, 0)]
    ext = ext[first : first + cols + 2]
    part = first // cols
    last = frames // 2 - 1
    pixels = cols * frames * rows
    block = pl.BlockSpec((cols, 2, rows, chans), lambda p: (part, last - p, 0, 0))
    return pl.pallas_call(
        functools.partial(backward_kernel, group, [0] * len(ext)),
        grid=(frames // 2,),
        in_specs=[
            pl.BlockSpec(
                (1, 2, rows, chans), functools.partial(lambda e, p: (e, last - p, 0, 0), e)
            )
            for _, e in ext
        ]
        + [
            pl.BlockSpec(spatial.shape, lambda p: (0, 0)),
            pl.BlockSpec((1, 4 * chans, 2 * chans), lambda p: (last - p, 0, 0)),
        ]
        + [pl.BlockSpec(memory_space=pl.ANY)] * len(filled),
        out_specs=block,
        out_shape=jax.ShapeDtypeStruct((width, frames, rows, chans), jnp.bfloat16),
        input_output_aliases={len(ext) + 2: 0} if filled else {},
        scratch_shapes=[pltpu.VMEM((cols * rows, 2 * chans), jnp.bfloat16)],
        compiler_params=pltpu.CompilerParams(vmem_limit_bytes=60 * MIB),
        cost_estimate=pl.CostEstimate(
            flops=pixels * chans * chans * 2 * 24,
            bytes_accessed=pixels * chans * 6,
            transcendentals=0,
        ),
    )(*[array for array, _ in ext], spatial, temporal, *filled)


def exchanged(axis, parts):
    count = lax.axis_size(axis)
    return [
        lax.ppermute(parts(s), axis, [(i, i ^ s) for i in range(count)]) for s in range(1, count)
    ]


def sum_over_devices(local, works, state):
    def pieces(value, axis):
        me = lax.axis_index(axis)
        blocks = value.reshape(lax.axis_size(axis), -1, value.shape[-1])
        return lambda s: lax.dynamic_index_in_dim(blocks, me ^ s, 0, keepdims=False)

    def spread(parts, axis):
        order = jnp.arange(len(parts), dtype=jnp.int32) ^ lax.axis_index(axis)
        return jnp.take(jnp.stack(parts), order, axis=0).reshape(-1, parts[0].shape[-1])

    def beside(value, got, work, state):
        value, state = lax.optimization_barrier((value, state))
        got = got(value)
        state = work(state)
        got, state = lax.optimization_barrier((got, state))
        return value, got, state

    pick = pieces(local, "width")
    value = functools.reduce(jnp.add, exchanged("width", pick), pick(0))
    value, got, state = beside(
        value, lambda v: exchanged("height", pieces(v, "height")), works[0], state
    )
    value = functools.reduce(jnp.add, got, pieces(value, "height")(0))
    value, got, state = beside(value, lambda v: exchanged("tm", lambda s: v), works[1], state)
    value = functools.reduce(jnp.add, got, value)
    value, got, state = beside(value, lambda v: exchanged("height", lambda s: v), works[2], state)
    value = spread([value] + got, "height")
    return spread([value] + exchanged("width", lambda s: value), "width"), state


def shards(video, out_grad, lengths, temporal_weight, spatial_weight):
    clip = video[0]
    width, frames, rows, chans = clip.shape
    n_tm = lax.axis_size("tm")
    n_height = lax.axis_size("height")
    frames_dev, rows_dev = out_grad.shape[2], out_grad.shape[3]
    assert frames_dev == 2
    group = 2 if width % 2 == 0 else 1
    pairs = frames // 2

    left, right = column_neighbours(clip[:1], clip[width - 1 :])
    blocks = out_grad[0].reshape(n_tm * n_height, width, frames_dev, rows_dev, chans)

    def to_columns(part):
        got = lax.all_to_all(part, ("tm", "height"), split_axis=0, concat_axis=0, tiled=True)
        return got.reshape(n_tm, n_height, *part.shape[1:])

    early, later = list(range(width // group)), []
    if len(early) >= 4:
        later = [early.pop(-2)]
        cut = later[0] * group
        first = jnp.concatenate([blocks[:, :cut], blocks[:, cut + group :]], axis=1)
    else:
        first = blocks
    received = to_columns(first)

    temporal_mix, temporal_back, spatial_mix, spatial_back, *weights, masks = prepare(
        lengths, temporal_weight, spatial_weight, frames, group
    )
    slope, turned = forward(clip, left, right, temporal_mix, spatial_mix, group)
    if later:
        blocks, slope, turned = lax.optimization_barrier((blocks, slope, turned))
        second = blocks[:, cut : cut + group]
        second, received, slope, turned = lax.optimization_barrier(
            (second, received, slope, turned)
        )
        second = to_columns(second)

    weights = (slope, turned, masks, *weights)
    def edge_delta(col, place):
        grads = received[:, :, place].transpose(0, 2, 1, 3, 4).reshape(1, frames, rows, chans)
        return (grads.astype(jnp.float32) * slope[col][None]).astype(jnp.bfloat16)

    head, tail = edge_delta(0, 0), edge_delta(width - 1, received.shape[2] - 1)
    received, head, tail = lax.optimization_barrier((received, head, tail))
    delta_left, delta_right = column_neighbours(head, tail)
    deltas, local, _ = moments(received, *weights, None, early, group)
    if later:
        more, local, _ = moments(second, *weights, local, later, group)
        deltas = deltas[: later[0]] + more + deltas[later[0] :]
    local, deltas, delta_left, delta_right = lax.optimization_barrier(
        (local, deltas, delta_left, delta_right)
    )

    parts = [(0, width), None, None]
    if len(deltas) >= 4:
        half = width // 2
        parts = [(0, half), (half, half), None]

    def one_part(part, state):
        if part is None:
            return state
        operands, filled = state
        return operands, backward(*operands, spatial_back, temporal_back, filled, *part)

    sums, (_, video_grad) = sum_over_devices(
        local.reshape(-1, chans),
        [functools.partial(one_part, part) for part in parts],
        ((deltas, delta_left, delta_right), None),
    )
    sums = sums.reshape(12, chans, chans)
    temporal_grad, spatial_grad = sums[:3], sums[3:].reshape(3, 3, chans, chans)
    return video_grad[None], temporal_grad, spatial_grad


def solution(mesh):
    placed = (
        P("width", ("tm", "height"), None, None, None),
        P("width", None, "tm", "height", None),
        P(),
        P(),
        P(),
    )
    return jax.shard_map(
        shards,
        mesh=mesh,
        in_specs=placed,
        out_specs=(P("width", ("tm", "height"), None, None, None), P(), P()),
        check_vma=False,
    )
```

time: 188 us -> 187 us (level)
  waiting for transfers between devices: 62.9 us -> 43.3 us
  Pallas kernels: 54.8 us -> 71.1 us
  local copies, waits for them, and re-layouts: 10.9 us -> 16.6 us
  other arithmetic: 7.94 us -> 5.66 us
    all_to_all x1 -> x2, starting transfers between devices: 8.18 us -> 21.5 us  [to_columns(): lax.all_to_all(part, ('tm', 'height'), split_axis=0, concat_axis=0, tiled...]
    all_to_all x1 -> x2, waiting for transfers between devices: 43.4 us -> 31.5 us  [to_columns(): lax.all_to_all(part, ('tm', 'height'), split_axis=0, concat_axis=0, tiled...]
    pallas_call x4 -> x5, Pallas kernels: 36.1 us -> 46.7 us  [the longest x2 29.3 us: moments(): pl.pallas_call(functools.partial(moments_kernel, group, groups, places, e...]
    ppermute x11, starting transfers between devices: 23.4 us -> 14.9 us  [exchanged(): lax.ppermute(parts(s), axis, [(i, i ^ s) for i in range(count)])]
    pallas_call x1, Pallas kernels: 18.7 us -> 24.4 us  [forward(): pl.pallas_call(functools.partial(forward_kernel, group, width, lag), grid...]
    ppermute x2, starting transfers between devices: 15 us -> 9.46 us  [column_neighbours(): left = lax.ppermute(last, MESH_AXES, pairs)]
    ppermute x2, waiting for transfers between devices: 6.51 us -> 2.13 us  [column_neighbours(): right = lax.ppermute(first, MESH_AXES, [(b, a) for a, b in pairs])]
    mul x2 -> x0, other arithmetic: 3.34 us -> none  [the longest x1 1.69 us: tap_block(): paired[k, :, j, None, None] * temporal_weight[k]]
  transfers between devices with their start and end apart: 16 -> 17, of which waited for: 7 -> 9; matrix products, arithmetic and copies ran while one was open for 4% -> 5% of each run, Pallas kernels for 29% -> 38%
where the time goes in v4:
time: 187 us; the launch traced here: 186 us
  Pallas kernels  71.1 us (38%)
  starting transfers between devices  48.5 us (26%)
  waiting for transfers between devices  43.3 us (23%)
  local copies, waits for them, and re-layouts  16.6 us (9%)
  other arithmetic  5.66 us (3%)
    all_to_all x2, waiting for transfers between devices, to_columns(): lax.all_to_all(part, ('tm', 'height'), split_axis=0, concat_axis=0, tiled...  31.5 us
    pallas_call x2, Pallas kernels, moments(): pl.pallas_call(functools.partial(moments_kernel, group, groups, places, e...  29.3 us
    pallas_call x1, Pallas kernels, forward(): pl.pallas_call(functools.partial(forward_kernel, group, width, lag), grid...  24.4 us
    all_to_all x2, starting transfers between devices, to_columns(): lax.all_to_all(part, ('tm', 'height'), split_axis=0, concat_axis=0, tiled...  21.5 us
    pallas_call x2, Pallas kernels, backward(): pl.pallas_call(functools.partial(backward_kernel, group, [0] * len(ext)),...  16.1 us
    ppermute x11, starting transfers between devices, exchanged(): lax.ppermute(parts(s), axis, [(i, i ^ s) for i in range(count)])  14.9 us
    ppermute x2, starting transfers between devices, column_neighbours(): left = lax.ppermute(last, MESH_AXES, pairs)  9.46 us
    ppermute x11, waiting for transfers between devices, exchanged(): lax.ppermute(parts(s), axis, [(i, i ^ s) for i in range(count)])  6.04 us
  transfers between devices with their start and end apart: 17, of which 9 were waited for; matrix products, arithmetic and copies ran while one was open for 5% of the time, Pallas kernels for 38%

profile of v4, /device:TPU:0, one launch (start us, length us, event | category | flops | bytes accessed | tf_op | source)
XLA Modules:
  0.0 186.1 jit_solution(2874996036803273341)
XLA Ops:
  0.6 2.4 %slice_bitcast_fusion = (bf16[1,8,256,128]{3,2,1,0:T(8,128)(2,1)}, bf16[1,8,256,128]{3,2,1,0:T(8,128)(2,1)}) fusion(bf16[1,8,8,256,128]{4,3,2,1,0:T(8,128)(2,1)} %param.5), kind=kLoop, calls=%fused_computation.8 | loop fusion | bytes 2097152 | tf_op jit(solution)/shard_map/slice | solution.py:490
  3.1 5.7 %collective-permute-start = (bf16[1,8,256,128]{3,2,1,0:T(8,128)(2,1)}, bf16[1,8,256,128]{3,2,1,0:T(8,128)(2,1)}, u32[]{:S(2)}, u32[]{:S(2)}) collective-permute-start(bf16[1,8,256,128]{3,2,1,0:T(8,128)(2,1)} %get-tuple-element.132), channel_id=1, source_target_pairs={{0,2},{2,4},{4,6},{6,8},{8,10},{10,12},{12,14},{14,16},{16,18},{18... | collective-permute-start | bytes 1572872 | tf_op jit(solution)/shard_map/ppermute | solution.py:19
  11.6 1.9 %pad_maximum_fusion = bf16[16,6,2,64,128]{4,3,2,1,0:T(8,128)(2,1)} fusion(bf16[16,2,2,64,128]{4,3,2,1,0:T(8,128)(2,1)S(1)} %slice.57, bf16[16,4,2,64,128]{4,3,2,1,0:T(8,128)(2,1)S(1)} %slice.56), kind=kLoop, calls=%fused_computation.2 | loop fusion | flops 1572864 | bytes 6291456 | tf_op jit(solution)/shard_map/concatenate | solution.py:501
  13.6 7.3 %all-to-all-start = ((bf16[16,6,2,64,128]{4,3,2,1,0:T(8,128)(2,1)}), bf16[16,6,2,64,128]{4,3,2,1,0:T(8,128)(2,1)S(1)}, u32[]{:S(2)}, u32[]{:S(2)}) async-start(bf16[16,6,2,64,128]{4,3,2,1,0:T(8,128)(2,1)} %pad_maximum_fusion), calls=%async_computation | async-start | bytes 6291456 | tf_op jit(solution)/shard_map/all_to_all | solution.py:494
  28.0 3.6 %collective-permute-done.refs_4_.refs_5_ = bf16[1,8,256,128]{3,2,1,0:T(8,128)(2,1)} collective-permute-done((bf16[1,8,256,128]{3,2,1,0:T(8,128)(2,1)}, bf16[1,8,256,128]{3,2,1,0:T(8,128)(2,1)}, u32[]{:S(2)}, u32[]{:S(2)}) %collective-permute-start) | collective-permute-done | bytes 524320 | tf_op jit(solution)/shard_map/ppermute | solution.py:19
  31.6 2.1 %collective-permute-done.1.refs_6_.refs_7_ = bf16[1,8,256,128]{3,2,1,0:T(8,128)(2,1)} collective-permute-done((bf16[1,8,256,128]{3,2,1,0:T(8,128)(2,1)}, bf16[1,8,256,128]{3,2,1,0:T(8,128)(2,1)}, u32[]{:S(2)}, u32[]{:S(2)}) %collective-permute-start.1) | collective-permute-done | bytes 524320 | tf_op jit(solution)/shard_map/ppermute | solution.py:20
  33.7 24.4 %shard_map.77 = (f32[8,8,256,128]{3,2,1,0:T(8,128)}, bf16[10,8,128,256]{3,2,1,0:T(8,128)(2,1)}) custom-call(bf16[8,8,256,128]{3,2,1,0:T(8,128)(2,1)} %bitcast.71, bf16[8,8,256,128]{3,2,1,0:T(8,128)(2,1)} %bitcast.72, bf16[8,8,256,128]{3,2,1,0:T(8,128)(2,1)} %bitcast.73, bf16[8,8,256,128]{3,2,1,0:T(8,128)(2,1)} %bitcast.74, ...), custom_call_target="tpu_custom_call" | custom-call | flops 64424509440 | bytes 29360128 | tf_op jit(solution)/shard_map/pallas_call | solution.py:175
  58.1 2.3 %slice.43 = bf16[16,2,2,64,128]{4,3,2,1,0:T(8,128)(2,1)} slice(bf16[16,8,2,64,128]{4,3,2,1,0:T(8,128)(2,1)} %bitcast.60), slice={[0:16], [4:6], [0:2], [0:64], [0:128]} | slice | bytes 2097152 | tf_op jit(solution)/shard_map/slice | solution.py:512
  60.4 27.7 %all-to-all-done = bf16[16,6,2,64,128]{4,3,2,1,0:T(8,128)(2,1)S(1)} async-done(((bf16[16,6,2,64,128]{4,3,2,1,0:T(8,128)(2,1)}), bf16[16,6,2,64,128]{4,3,2,1,0:T(8,128)(2,1)S(1)}, u32[]{:S(2)}, u32[]{:S(2)}) %all-to-all-start) | async-done | bytes 3145760 | tf_op jit(solution)/shard_map/all_to_all | solution.py:494
  88.1 14.1 %all-to-all-start.1 = ((bf16[16,2,2,64,128]{4,3,2,1,0:T(8,128)(2,1)}), bf16[16,2,2,64,128]{4,3,2,1,0:T(8,128)(2,1)}, u32[]{:S(2)}, u32[]{:S(2)}) async-start(bf16[16,2,2,64,128]{4,3,2,1,0:T(8,128)(2,1)} %slice.43), calls=%async_computation.1 | async-start | bytes 2097152 | tf_op jit(solution)/shard_map/all_to_all | solution.py:494
  102.6 1.8 multiply_convert_fusion
  104.5 3.8 %collective-permute-start.2 = (bf16[1,8,256,128]{3,2,1,0:T(8,128)(2,1)S(1)}, bf16[1,8,256,128]{3,2,1,0:T(8,128)(2,1)S(1)}, u32[]{:S(2)}, u32[]{:S(2)}) collective-permute-start(bf16[1,8,256,128]{3,2,1,0:T(8,128)(2,1)S(1)} %get-tuple-element.87), channel_id=1, source_target_pairs={{0,2},{2,4},{4,6},{6,8},{8,10},{10,12},{12,14},{14,16},{16,18},{18... | collective-permute-start | bytes 1572872 | tf_op jit(solution)/shard_map/ppermute | solution.py:19
  108.3 1.5 collective-permute-start.3
  109.7 18.5 %shard_map.78 = (bf16[2,8,256,128]{3,2,1,0:T(8,128)(2,1)}, bf16[2,8,256,128]{3,2,1,0:T(8,128)(2,1)}, bf16[2,8,256,128]{3,2,1,0:T(8,128)(2,1)}, f32[12,128,128]{2...) custom-call(f32[3,8]{1,0:T(4,128)} %copy-done.4, ...), custom_call_target="tpu_custom_call" | custom-call | flops 12079595520 | bytes 31457280 | tf_op jit(solution)/shard_map/pallas_call | solution.py:326
  128.3 3.9 %all-to-all-done.1 = bf16[16,2,2,64,128]{4,3,2,1,0:T(8,128)(2,1)} async-done(((bf16[16,2,2,64,128]{4,3,2,1,0:T(8,128)(2,1)}), bf16[16,2,2,64,128]{4,3,2,1,0:T(8,128)(2,1)}, u32[]{:S(2)}, u32[]{:S(2)}) %all-to-all-start.1) | async-done | bytes 1048608 | tf_op jit(solution)/shard_map/all_to_all | solution.py:494
  132.1 10.8 %shard_map.79 = (bf16[2,8,256,128]{3,2,1,0:T(8,128)(2,1)}, f32[12,128,128]{2,1,0:T(8,128)}) custom-call(f32[3,8]{1,0:T(4,128)} %copy-done.4, bf16[4,4,2,2,64,128]{5,4,3,2,1,0:T(8,128)(2,1)} %bitcast.5.refs_0_, f32[8,8,256,128]{3,2,1,0:T(8,128)} %get-tuple-element.75.refs_1_.refs_2_.refs_3_, ...), custom_call_target="tpu_custom_call" | custom-call | flops 4026531840 | bytes 10485760 | tf_op jit(solution)/shard_map/pallas_call | solution.py:326
  147.3 1.9 %collective-permute-start.6 = (f32[192,128]{1,0:T(8,128)S(1)}, f32[192,128]{1,0:T(8,128)S(1)}, u32[]{:S(2)}, u32[]{:S(2)}) collective-permute-start(f32[192,128]{1,0:T(8,128)S(1)} %get-tuple-element.136), channel_id=1, source_target_pairs={{0,4},{2,6},{4,0},{6,2},{1,5},{3,7},{5,1},{7,3},{8,12},{10,14},{12... | collective-permute-start | bytes 294920 | tf_op jit(solution)/shard_map/ppermute | solution.py:446
  149.3 1.5 collective-permute-start.7
  150.8 8.0 %shard_map.80.refs_8_ = bf16[8,8,256,128]{3,2,1,0:T(8,128)(2,1)} custom-call(bf16[1,8,256,128]{3,2,1,0:T(8,128)(2,1)} %copy-done.13, bf16[2,8,256,128]{3,2,1,0:T(8,128)(2,1)} %get-tuple-element.97.refs_1_.refs_2_, bf16[2,8,256,128]{3,2,1,0:T(8,128)(2,1)} %get-tuple-element.97.refs_1_.refs_2_, ...), custom_call_target="tpu_custom_call" | custom-call | flops 6442450944 | bytes 6291456 | tf_op jit(solution)/shard_map/pallas_call | solution.py:416
  158.9 4.7 %collective-permute-start.8 = (f32[192,128]{1,0:T(8,128)S(1)}, f32[192,128]{1,0:T(8,128)S(1)}, u32[]{:S(2)}, u32[]{:S(2)}) collective-permute-start(f32[192,128]{1,0:T(8,128)S(1)} %fusion.1), channel_id=1, source_target_pairs={{0,8},{8,0},{16,24},{24,16},{1,9},{9,1},{17,25},{25,17},{2,10},{10... | collective-permute-start | bytes 294920 | tf_op jit(solution)/shard_map/ppermute | solution.py:446
  163.6 2.4 %collective-permute-start.10 = (f32[192,128]{1,0:T(8,128)S(1)}, f32[192,128]{1,0:T(8,128)S(1)}, u32[]{:S(2)}, u32[]{:S(2)}) collective-permute-start(f32[192,128]{1,0:T(8,128)S(1)} %fusion.1), channel_id=1, source_target_pairs={{0,24},{8,16},{16,8},{24,0},{1,25},{9,17},{17,9},{25,1},{2,26},{10... | collective-permute-start | bytes 294920 | tf_op jit(solution)/shard_map/ppermute | solution.py:446
  166.1 8.0 %shard_map.81 = bf16[8,8,256,128]{3,2,1,0:T(8,128)(2,1)} custom-call(bf16[2,8,256,128]{3,2,1,0:T(8,128)(2,1)} %get-tuple-element.114.refs_3_.refs_4_.refs_0_, bf16[2,8,256,128]{3,2,1,0:T(8,128)(2,1)} %get-tuple-element.115.refs_5_.refs_1_.refs_2_, ...), custom_call_target="tpu_custom_call", output_to_operand_aliasing={{}: (8, {})} | custom-call | flops 6442450944 | bytes 6291456 | tf_op jit(solution)/shard_map/pallas_call | solution.py:416
  175.7 2.0 %collective-permute-start.13 = (f32[192,128]{1,0:T(8,128)S(1)}, f32[192,128]{1,0:T(8,128)S(1)}, u32[]{:S(2)}, u32[]{:S(2)}) collective-permute-start(f32[192,128]{1,0:T(8,128)S(1)} %add_add_fusion), channel_id=1, source_target_pairs={{0,6},{2,4},{4,2},{6,0},{1,7},{3,5},{5,3},{7,1},{8,14},{10,12},{12... | collective-permute-start | bytes 294920 | tf_op jit(solution)/shard_map/ppermute | solution.py:446
  179.8 1.5 collective-permute-done.13
  (77 shorter events, 23.2 us)
Async XLA Ops:
  0.6 10.7 %copy-start.11 = (bf16[1,128,2,64,128]{4,3,2,1,0:T(8,128)(2,1)S(1)}, bf16[1,128,2,64,128]{4,3,2,1,0:T(8,128)(2,1)}, u32[]{:S(2)}) copy-start(bf16[1,128,2,64,128]{4,3,2,1,0:T(8,128)(2,1)} %param.6) | copy-start | bytes 12582916
  3.1 28.5 %collective-permute-start = (bf16[1,8,256,128]{3,2,1,0:T(8,128)(2,1)}, bf16[1,8,256,128]{3,2,1,0:T(8,128)(2,1)}, u32[]{:S(2)}, u32[]{:S(2)}) collective-permute-start(bf16[1,8,256,128]{3,2,1,0:T(8,128)(2,1)} %get-tuple-element.132), channel_id=1, source_target_pairs={{0,2},{2,4},{4,6},{6,8},{8,10},{10,12},{12,14},{14,16},{16,18},{18... | collective-permute-start | bytes 1572872 | tf_op jit(solution)/shard_map/ppermute | solution.py:19
  8.7 25.0 %collective-permute-start.1 = (bf16[1,8,256,128]{3,2,1,0:T(8,128)(2,1)}, bf16[1,8,256,128]{3,2,1,0:T(8,128)(2,1)}, u32[]{:S(2)}, u32[]{:S(2)}) collective-permute-start(bf16[1,8,256,128]{3,2,1,0:T(8,128)(2,1)} %get-tuple-element.131), channel_id=1, source_target_pairs={{2,0},{4,2},{6,4},{8,6},{10,8},{12,10},{14,12},{16,14},{18,16},{20... | collective-permute-start | bytes 1572872 | tf_op jit(solution)/shard_map/ppermute | solution.py:20
  13.6 7.4 %copy-start.2 = (bf16[3,3,128,128]{3,2,1,0:T(8,128)(2,1)S(1)}, bf16[3,3,128,128]{3,2,1,0:T(8,128)(2,1)}, u32[]{:S(2)}) copy-start(bf16[3,3,128,128]{3,2,1,0:T(8,128)(2,1)} %spatial.1) | copy-start | bytes 884740
  13.6 7.4 %copy-start.3 = (bf16[3,128,128]{2,1,0:T(8,128)(2,1)S(1)}, bf16[3,128,128]{2,1,0:T(8,128)(2,1)}, u32[]{:S(2)}) copy-start(bf16[3,128,128]{2,1,0:T(8,128)(2,1)} %temporal.1) | copy-start | bytes 294916
  13.6 7.4 %copy-start.5 = (s32[4]{0:T(128)S(1)}, s32[4]{0:T(128)}, u32[]{:S(2)}) copy-start(s32[4]{0:T(128)} %lengths.1) | copy-start | bytes 52
  13.6 74.5 %all-to-all-start = ((bf16[16,6,2,64,128]{4,3,2,1,0:T(8,128)(2,1)}), bf16[16,6,2,64,128]{4,3,2,1,0:T(8,128)(2,1)S(1)}, u32[]{:S(2)}, u32[]{:S(2)}) async-start(bf16[16,6,2,64,128]{4,3,2,1,0:T(8,128)(2,1)} %pad_maximum_fusion), calls=%async_computation | async-start | bytes 6291456 | tf_op jit(solution)/shard_map/all_to_all | solution.py:494
  88.1 14.5 %copy-start.10 = (bf16[16,6,2,64,128]{4,3,2,1,0:T(8,128)(2,1)}, bf16[16,6,2,64,128]{4,3,2,1,0:T(8,128)(2,1)S(1)}, u32[]{:S(2)}) copy-start(bf16[16,6,2,64,128]{4,3,2,1,0:T(8,128)(2,1)S(1)} %all-to-all-done) | copy-start | bytes 9437188
  88.1 44.0 %all-to-all-start.1 = ((bf16[16,2,2,64,128]{4,3,2,1,0:T(8,128)(2,1)}), bf16[16,2,2,64,128]{4,3,2,1,0:T(8,128)(2,1)}, u32[]{:S(2)}, u32[]{:S(2)}) async-start(bf16[16,2,2,64,128]{4,3,2,1,0:T(8,128)(2,1)} %slice.43), calls=%async_computation.1 | async-start | bytes 2097152 | tf_op jit(solution)/shard_map/all_to_all | solution.py:494
  104.5 38.5 %collective-permute-start.2 = (bf16[1,8,256,128]{3,2,1,0:T(8,128)(2,1)S(1)}, bf16[1,8,256,128]{3,2,1,0:T(8,128)(2,1)S(1)}, u32[]{:S(2)}, u32[]{:S(2)}) collective-permute-start(bf16[1,8,256,128]{3,2,1,0:T(8,128)(2,1)S(1)} %get-tuple-element.87), channel_id=1, source_target_pairs={{0,2},{2,4},{4,6},{6,8},{8,10},{10,12},{12,14},{14,16},{16,18},{18... | collective-permute-start | bytes 1572872 | tf_op jit(solution)/shard_map/ppermute | solution.py:19
  108.3 34.7 %collective-permute-start.3 = (bf16[1,8,256,128]{3,2,1,0:T(8,128)(2,1)S(1)}, bf16[1,8,256,128]{3,2,1,0:T(8,128)(2,1)S(1)}, u32[]{:S(2)}, u32[]{:S(2)}) collective-permute-start(bf16[1,8,256,128]{3,2,1,0:T(8,128)(2,1)S(1)} %get-tuple-element.88), channel_id=1, source_target_pairs={{2,0},{4,2},{6,4},{8,6},{10,8},{12,10},{14,12},{16,14},{18,16},{20... | collective-permute-start | bytes 1572872 | tf_op jit(solution)/shard_map/ppermute | solution.py:20
  142.9 7.9 %copy-start.13 = (bf16[1,8,256,128]{3,2,1,0:T(8,128)(2,1)}, bf16[1,8,256,128]{3,2,1,0:T(8,128)(2,1)S(1)}, u32[]{:S(2)}) copy-start(bf16[1,8,256,128]{3,2,1,0:T(8,128)(2,1)S(1)} %collective-permute-done.2.refs_0_) | copy-start | bytes 1572868
  142.9 15.9 %copy-start.12 = (bf16[1,8,256,128]{3,2,1,0:T(8,128)(2,1)}, bf16[1,8,256,128]{3,2,1,0:T(8,128)(2,1)S(1)}, u32[]{:S(2)}) copy-start(bf16[1,8,256,128]{3,2,1,0:T(8,128)(2,1)S(1)} %collective-permute-done.3.refs_5_) | copy-start | bytes 1572868
  144.3 1.9 %collective-permute-start.4 = (f32[768,128]{1,0:T(8,128)S(1)}, f32[768,128]{1,0:T(8,128)S(1)}, u32[]{:S(2)}, u32[]{:S(2)}) collective-permute-start(f32[768,128]{1,0:T(8,128)S(1)} %dynamic-slice_bitcast_fusion), channel_id=1, source_target_pairs={{0,1},{1,0},{2,3},{3,2},{4,5},{5,4},{6,7},{7,6},{8,9},{9,8},{10,11... | collective-permute-start | bytes 1179656 | tf_op jit(solution)/shard_map/ppermute | solution.py:446
  147.2 11.6 %collective-permute-start.5 = (f32[192,128]{1,0:T(8,128)S(1)}, f32[192,128]{1,0:T(8,128)S(1)}, u32[]{:S(2)}, u32[]{:S(2)}) collective-permute-start(f32[192,128]{1,0:T(8,128)S(1)} %get-tuple-element.137), channel_id=1, source_target_pairs={{0,2},{2,0},{4,6},{6,4},{1,3},{3,1},{5,7},{7,5},{8,10},{10,8},{12,... | collective-permute-start | bytes 294920 | tf_op jit(solution)/shard_map/ppermute | solution.py:446
  147.3 11.5 %collective-permute-start.6 = (f32[192,128]{1,0:T(8,128)S(1)}, f32[192,128]{1,0:T(8,128)S(1)}, u32[]{:S(2)}, u32[]{:S(2)}) collective-permute-start(f32[192,128]{1,0:T(8,128)S(1)} %get-tuple-element.136), channel_id=1, source_target_pairs={{0,4},{2,6},{4,0},{6,2},{1,5},{3,7},{5,1},{7,3},{8,12},{10,14},{12... | collective-permute-start | bytes 294920 | tf_op jit(solution)/shard_map/ppermute | solution.py:446
  149.3 9.6 %collective-permute-start.7 = (f32[192,128]{1,0:T(8,128)S(1)}, f32[192,128]{1,0:T(8,128)S(1)}, u32[]{:S(2)}, u32[]{:S(2)}) collective-permute-start(f32[192,128]{1,0:T(8,128)S(1)} %get-tuple-element.135), channel_id=1, source_target_pairs={{0,6},{2,4},{4,2},{6,0},{1,7},{3,5},{5,3},{7,1},{8,14},{10,12},{12... | collective-permute-start | bytes 294920 | tf_op jit(solution)/shard_map/ppermute | solution.py:446
  158.9 15.2 %collective-permute-start.8 = (f32[192,128]{1,0:T(8,128)S(1)}, f32[192,128]{1,0:T(8,128)S(1)}, u32[]{:S(2)}, u32[]{:S(2)}) collective-permute-start(f32[192,128]{1,0:T(8,128)S(1)} %fusion.1), channel_id=1, source_target_pairs={{0,8},{8,0},{16,24},{24,16},{1,9},{9,1},{17,25},{25,17},{2,10},{10... | collective-permute-start | bytes 294920 | tf_op jit(solution)/shard_map/ppermute | solution.py:446
  163.6 10.5 %collective-permute-start.9 = (f32[192,128]{1,0:T(8,128)S(1)}, f32[192,128]{1,0:T(8,128)S(1)}, u32[]{:S(2)}, u32[]{:S(2)}) collective-permute-start(f32[192,128]{1,0:T(8,128)S(1)} %fusion.1), channel_id=1, source_target_pairs={{0,16},{8,24},{16,0},{24,8},{1,17},{9,25},{17,1},{25,9},{2,18},{10... | collective-permute-start | bytes 294920 | tf_op jit(solution)/shard_map/ppermute | solution.py:446
  163.6 10.5 %collective-permute-start.10 = (f32[192,128]{1,0:T(8,128)S(1)}, f32[192,128]{1,0:T(8,128)S(1)}, u32[]{:S(2)}, u32[]{:S(2)}) collective-permute-start(f32[192,128]{1,0:T(8,128)S(1)} %fusion.1), channel_id=1, source_target_pairs={{0,24},{8,16},{16,8},{24,0},{1,25},{9,17},{17,9},{25,1},{2,26},{10... | collective-permute-start | bytes 294920 | tf_op jit(solution)/shard_map/ppermute | solution.py:446
  174.1 4.8 %collective-permute-start.11 = (f32[192,128]{1,0:T(8,128)S(1)}, f32[192,128]{1,0:T(8,128)S(1)}, u32[]{:S(2)}, u32[]{:S(2)}) collective-permute-start(f32[192,128]{1,0:T(8,128)S(1)} %add_add_fusion), channel_id=1, source_target_pairs={{0,2},{2,0},{4,6},{6,4},{1,3},{3,1},{5,7},{7,5},{8,10},{10,8},{12,... | collective-permute-start | bytes 294920 | tf_op jit(solution)/shard_map/ppermute | solution.py:446
  174.3 5.4 %collective-permute-start.12 = (f32[192,128]{1,0:T(8,128)S(1)}, f32[192,128]{1,0:T(8,128)S(1)}, u32[]{:S(2)}, u32[]{:S(2)}) collective-permute-start(f32[192,128]{1,0:T(8,128)S(1)} %add_add_fusion), channel_id=1, source_target_pairs={{0,4},{2,6},{4,0},{6,2},{1,5},{3,7},{5,1},{7,3},{8,12},{10,14},{12... | collective-permute-start | bytes 294920 | tf_op jit(solution)/shard_map/ppermute | solution.py:446
  175.7 5.5 %collective-permute-start.13 = (f32[192,128]{1,0:T(8,128)S(1)}, f32[192,128]{1,0:T(8,128)S(1)}, u32[]{:S(2)}, u32[]{:S(2)}) collective-permute-start(f32[192,128]{1,0:T(8,128)S(1)} %add_add_fusion), channel_id=1, source_target_pairs={{0,6},{2,4},{4,2},{6,0},{1,7},{3,5},{5,3},{7,1},{8,14},{10,12},{12... | collective-permute-start | bytes 294920 | tf_op jit(solution)/shard_map/ppermute | solution.py:446
  182.0 1.8 collective-permute-start.14
  (7 other events, 5.7 us)

commit v5 on v4

--- a/solution.py
+++ b/solution.py
@@ -200,17 +200,14 @@
     )(*([video] * (2 * group)), left, left, right, right, temporal, spatial)
 
 
-def moments_kernel(group, groups, places, edges, scale, masks, *refs):
+def moments_kernel(group, groups, places, fresh, scale, masks, *refs):
     count = len(groups)
     grads, refs = refs[0], refs[1:]
     slopes, refs = refs[:count], refs[count:]
     now, before, refs = refs[: len(places)], refs[len(places) : 2 * len(places)], refs[2 * len(places) :]
     temporal, spatial, refs = refs[0], refs[1], refs[2:]
     total, refs = refs[-1], refs[:-1]
-    if edges:
-        head, tail, refs, earlier = refs[-2], refs[-1], refs[:-2], None
-    else:
-        earlier, refs = refs[0], refs[1:]
+    earlier, refs = (None, refs) if fresh else (refs[0], refs[1:])
     deltas, sums = refs[:count], refs[count]
     pair = pl.program_id(0)
     bands, band = grads.shape[1], grads.shape[4]
@@ -234,9 +231,6 @@
             line += [below, value, above]
         triples.append(lanes(line))
     right = jnp.concatenate(triples, axis=0)
-    if edges:
-        head[0] = deltas[0][0]
-        tail[0] = deltas[-1][group - 1]
 
     def add(lag, left, right):
         total[lag] += jnp.dot(left, right, preferred_element_type=jnp.float32)
@@ -301,7 +295,7 @@
 
 
 def moments(received, slope, turned, masks, temporal, spatial, earlier, groups, group):
-    edges = earlier is None
+    fresh = earlier is None
     frames, rows, chans = slope.shape[1:]
     bands, band = received.shape[1], received.shape[4]
     count = len(groups)
@@ -320,11 +314,9 @@
     def whole(shape):
         return pl.BlockSpec(shape, lambda p, m: (0,) * len(shape))
 
-    edge = pl.BlockSpec((1, 2, rows, chans), lambda p, m: (0, p, 0, 0))
-    edge_shape = jax.ShapeDtypeStruct((1, frames, rows, chans), jnp.bfloat16)
     sums_shape = (12, chans, chans)
-    outs = pl.pallas_call(
-        functools.partial(moments_kernel, group, groups, places, edges, scale),
+    *deltas, sums = pl.pallas_call(
+        functools.partial(moments_kernel, group, groups, places, fresh, scale),
         grid_spec=pltpu.PrefetchScalarGridSpec(
             num_scalar_prefetch=1,
             grid=(frames // 2,),
@@ -337,17 +329,14 @@
             + [columns(n, 0) for n in places]
             + [columns(n, 1) for n in places]
             + [whole(temporal.shape), whole(spatial.shape)]
-            + ([] if edges else [whole(sums_shape)]),
-            out_specs=[own(0) for _ in groups]
-            + [whole(sums_shape)]
-            + ([edge, edge] if edges else []),
+            + ([] if fresh else [whole(sums_shape)]),
+            out_specs=[own(0) for _ in groups] + [whole(sums_shape)],
             scratch_shapes=[
                 pltpu.VMEM((3, (group + 2) * chans, group * 3 * chans), jnp.float32),
             ],
         ),
         out_shape=[jax.ShapeDtypeStruct((group, frames, rows, chans), jnp.bfloat16)] * count
-        + [jax.ShapeDtypeStruct(sums_shape, jnp.float32)]
-        + ([edge_shape, edge_shape] if edges else []),
+        + [jax.ShapeDtypeStruct(sums_shape, jnp.float32)],
         compiler_params=pltpu.CompilerParams(vmem_limit_bytes=60 * MIB),
         cost_estimate=pl.CostEstimate(
             flops=pixels * chans * chans * 2 * 30,
@@ -361,9 +350,9 @@
         *([turned] * (2 * len(places))),
         temporal,
         spatial,
-        *([] if edges else [earlier]),
-    )
-    return outs[:count], outs[count], outs[count + 1 :]
+        *([] if fresh else [earlier]),
+    )
+    return deltas, sums
 
 
 def backward_kernel(group, sources, *refs):
@@ -494,39 +483,48 @@
         got = lax.all_to_all(part, ("tm", "height"), split_axis=0, concat_axis=0, tiled=True)
         return got.reshape(n_tm, n_height, *part.shape[1:])
 
-    early, later = list(range(width // group)), []
-    if len(early) >= 4:
-        later = [early.pop(-2)]
-        cut = later[0] * group
-        first = jnp.concatenate([blocks[:, :cut], blocks[:, cut + group :]], axis=1)
-    else:
-        first = blocks
-    received = to_columns(first)
+    count = width // group
+    chunks = [list(range(count))]
+    if count >= 4:
+        chunks = [[0, count - 1], list(range(1, count - 1))]
+
+    def outgoing(blocks, groups):
+        if len(groups) == count:
+            return blocks
+        runs = [blocks[:, n * group : (n + 1) * group] for n in groups]
+        return runs[0] if len(runs) == 1 else jnp.concatenate(runs, axis=1)
+
+    received = to_columns(outgoing(blocks, chunks[0]))
 
     temporal_mix, temporal_back, spatial_mix, spatial_back, *weights, masks = prepare(
         lengths, temporal_weight, spatial_weight, frames, group
     )
     slope, turned = forward(clip, left, right, temporal_mix, spatial_mix, group)
-    if later:
-        blocks, slope, turned = lax.optimization_barrier((blocks, slope, turned))
-        second = blocks[:, cut : cut + group]
-        second, received, slope, turned = lax.optimization_barrier(
-            (second, received, slope, turned)
-        )
+    second = None
+    if len(chunks) > 1:
+        second = outgoing(blocks, chunks[1])
+        second, received = lax.optimization_barrier((second, received))
         second = to_columns(second)
-
     weights = (slope, turned, masks, *weights)
-    def edge_delta(col, place):
+    deltas, local = [None] * count, None
+
+    def add(received, groups):
+        some, total = moments(received, *weights, local, groups, group)
+        for n, delta in zip(groups, some):
+            deltas[n] = delta
+        return total
+
+    def edge_delta(received, col, place):
         grads = received[:, :, place].transpose(0, 2, 1, 3, 4).reshape(1, frames, rows, chans)
         return (grads.astype(jnp.float32) * slope[col][None]).astype(jnp.bfloat16)
 
-    head, tail = edge_delta(0, 0), edge_delta(width - 1, received.shape[2] - 1)
+    head = edge_delta(received, 0, 0)
+    tail = edge_delta(received, width - 1, received.shape[2] - 1)
     received, head, tail = lax.optimization_barrier((received, head, tail))
     delta_left, delta_right = column_neighbours(head, tail)
-    deltas, local, _ = moments(received, *weights, None, early, group)
-    if later:
-        more, local, _ = moments(second, *weights, local, later, group)
-        deltas = deltas[: later[0]] + more + deltas[later[0] :]
+    local = add(received, chunks[0])
+    if second is not None:
+        local = add(second, chunks[1])
     local, deltas, delta_left, delta_right = lax.optimization_barrier(
         (local, deltas, delta_left, delta_right)
     )

time: 187 us -> 181 us (0.968)
  Pallas kernels: 71.1 us -> 68.5 us
  waiting for transfers between devices: 43.3 us -> 41 us
    ppermute x2, waiting for transfers between devices: 3.58 us -> 0.01 us  [column_neighbours(): left = lax.ppermute(last, MESH_AXES, pairs)]
    concatenate x0 -> x1, local copies, waits for them, and re-layouts: none -> 3.23 us  [outgoing(): return runs[0] if len(runs) == 1 else jnp.concatenate(runs, axis=1)]
    pallas_call x2, Pallas kernels: 29.3 us -> 26.6 us  [moments(): pl.pallas_call(functools.partial(moments_kernel, group, groups, places, f...]
    all_to_all x2, waiting for transfers between devices: 31.5 us -> 34.2 us  [to_columns(): lax.all_to_all(part, ('tm', 'height'), split_axis=0, concat_axis=0, tiled...]
    slice x3 -> x1, local copies, waits for them, and re-layouts: 3.91 us -> 1.73 us  [outgoing(): runs = [blocks[:, n * group:(n + 1) * group] for n in groups]]
    ppermute x2, waiting for transfers between devices: 2.13 us -> 0.01 us  [column_neighbours(): right = lax.ppermute(first, MESH_AXES, [(b, a) for a, b in pairs])]
    unnamed x28 -> x26, local copies, waits for them, and re-layouts: 5.7 us -> 5.72 us
  transfers between devices with their start and end apart: 17 -> 17, of which waited for: 9 -> 7; matrix products, arithmetic and copies ran while one was open for 5% -> 4% of each run, Pallas kernels for 38% -> 38%
where the time goes in v5:
time: 181 us; the launch traced here: 179 us
  Pallas kernels  68.5 us (38%)
  starting transfers between devices  46.8 us (26%)
  waiting for transfers between devices  41 us (23%)
  local copies, waits for them, and re-layouts  16.5 us (9%)
  other arithmetic  5.21 us (3%)
    all_to_all x2, waiting for transfers between devices, to_columns(): lax.all_to_all(part, ('tm', 'height'), split_axis=0, concat_axis=0, tiled...  34.2 us
    pallas_call x2, Pallas kernels, moments(): pl.pallas_call(functools.partial(moments_kernel, group, groups, places, f...  26.6 us
    pallas_call x1, Pallas kernels, forward(): pl.pallas_call(functools.partial(forward_kernel, group, width, lag), grid...  24.5 us
    all_to_all x2, starting transfers between devices, to_columns(): lax.all_to_all(part, ('tm', 'height'), split_axis=0, concat_axis=0, tiled...  20 us
    pallas_call x2, Pallas kernels, backward(): pl.pallas_call(functools.partial(backward_kernel, group, [0] * len(ext)),...  16.1 us
    ppermute x11, starting transfers between devices, exchanged(): lax.ppermute(parts(s), axis, [(i, i ^ s) for i in range(count)])  15.6 us
    ppermute x2, starting transfers between devices, column_neighbours(): left = lax.ppermute(last, MESH_AXES, pairs)  8.43 us
    ppermute x11, waiting for transfers between devices, exchanged(): lax.ppermute(parts(s), axis, [(i, i ^ s) for i in range(count)])  6.86 us
  transfers between devices with their start and end apart: 17, of which 7 were waited for; matrix products, arithmetic and copies ran while one was open for 4% of the time, Pallas kernels for 38%

profile of v5, /device:TPU:0, one launch (start us, length us, event | category | flops | bytes accessed | tf_op | source)
XLA Modules:
  0.0 179.1 jit_solution(17444064175147618865)
XLA Ops:
  0.6 1.7 fusion.4
  2.4 1.5 pad_maximum_fusion
  3.9 8.3 %all-to-all-start = ((bf16[16,4,2,64,128]{4,3,2,1,0:T(8,128)(2,1)}), bf16[16,4,2,64,128]{4,3,2,1,0:T(8,128)(2,1)S(1)}, u32[]{:S(2)}, u32[]{:S(2)}) async-start(bf16[16,4,2,64,128]{4,3,2,1,0:T(8,128)(2,1)} %pad_maximum_fusion), calls=%async_computation | async-start | bytes 4194304 | tf_op jit(solution)/shard_map/all_to_all | solution.py:483
  13.5 4.6 %collective-permute-start = (bf16[1,8,256,128]{3,2,1,0:T(8,128)(2,1)S(1)}, bf16[1,8,256,128]{3,2,1,0:T(8,128)(2,1)}, u32[]{:S(2)}, u32[]{:S(2)}) collective-permute-start(bf16[1,8,256,128]{3,2,1,0:T(8,128)(2,1)S(1)} %get-tuple-element.122), channel_id=1, source_target_pairs={{0,2},{2,4},{4,6},{6,8},{8,10},{10,12},{12,14},{14,16},{16,18},{18... | collective-permute-start | bytes 1572872 | tf_op jit(solution)/shard_map/ppermute | solution.py:19
  19.5 3.2 %concatenate.8 = bf16[16,4,2,64,128]{4,3,2,1,0:T(8,128)(2,1)} slice(bf16[16,8,2,64,128]{4,3,2,1,0:T(8,128)(2,1)} %bitcast.60), slice={[0:16], [2:6], [0:2], [0:64], [0:128]} | slice | bytes 4194304 | tf_op jit(solution)/shard_map/concatenate | solution.py:495
  29.8 32.0 %all-to-all-done = bf16[16,4,2,64,128]{4,3,2,1,0:T(8,128)(2,1)S(1)} async-done(((bf16[16,4,2,64,128]{4,3,2,1,0:T(8,128)(2,1)}), bf16[16,4,2,64,128]{4,3,2,1,0:T(8,128)(2,1)S(1)}, u32[]{:S(2)}, u32[]{:S(2)}) %all-to-all-start) | async-done | bytes 2097184 | tf_op jit(solution)/shard_map/all_to_all | solution.py:483
  61.7 11.7 %all-to-all-start.1 = ((bf16[16,4,2,64,128]{4,3,2,1,0:T(8,128)(2,1)}), bf16[16,4,2,64,128]{4,3,2,1,0:T(8,128)(2,1)}, u32[]{:S(2)}, u32[]{:S(2)}) async-start(bf16[16,4,2,64,128]{4,3,2,1,0:T(8,128)(2,1)} %concatenate.8), calls=%async_computation.1 | async-start | bytes 4194304 | tf_op jit(solution)/shard_map/all_to_all | solution.py:483
  73.5 24.5 %shard_map.77 = (f32[8,8,256,128]{3,2,1,0:T(8,128)}, bf16[10,8,128,256]{3,2,1,0:T(8,128)(2,1)}) custom-call(bf16[8,8,256,128]{3,2,1,0:T(8,128)(2,1)} %bitcast.70, bf16[8,8,256,128]{3,2,1,0:T(8,128)(2,1)} %bitcast.71, bf16[8,8,256,128]{3,2,1,0:T(8,128)(2,1)} %bitcast.72, bf16[8,8,256,128]{3,2,1,0:T(8,128)(2,1)} %bitcast.73, ...), custom_call_target="tpu_custom_call" | custom-call | flops 64424509440 | bytes 29360128 | tf_op jit(solution)/shard_map/pallas_call | solution.py:175
  98.4 1.8 %multiply_convert_fusion = (bf16[1,8,256,128]{3,2,1,0:T(8,128)(2,1)S(1)}, bf16[1,8,256,128]{3,2,1,0:T(8,128)(2,1)S(1)}) fusion(f32[1,8,256,128]{3,2,1,0:T(8,128)S(1)} %bitcast.57, f32[8,8,256,128]{3,2,1,0:T(8,128)} %get-tuple-element.65.refs_1_.refs_2_, f32[1,8,256,128]{3,2,1,0:T(8,128)S(1)} %bitcast.58), kind=kLoop, calls=%fused_computation.5 | loop fusion | flops 1048576 | bytes 5242880 | tf_op jit(solution)/shard_map/convert_element_type | solution.py:519
  100.2 3.8 %collective-permute-start.2 = (bf16[1,8,256,128]{3,2,1,0:T(8,128)(2,1)S(1)}, bf16[1,8,256,128]{3,2,1,0:T(8,128)(2,1)S(1)}, u32[]{:S(2)}, u32[]{:S(2)}) collective-permute-start(bf16[1,8,256,128]{3,2,1,0:T(8,128)(2,1)S(1)} %get-tuple-element.77), channel_id=1, source_target_pairs={{0,2},{2,4},{4,6},{6,8},{8,10},{10,12},{12,14},{14,16},{16,18},{18... | collective-permute-start | bytes 1572872 | tf_op jit(solution)/shard_map/ppermute | solution.py:19
  104.0 1.5 collective-permute-start.3
  105.5 13.4 %shard_map.78 = (bf16[2,8,256,128]{3,2,1,0:T(8,128)(2,1)}, bf16[2,8,256,128]{3,2,1,0:T(8,128)(2,1)}, f32[12,128,128]{2,1,0:T(8,128)}) custom-call(f32[3,8]{1,0:T(4,128)} %copy-done.4, bf16[4,4,4,2,64,128]{5,4,3,2,1,0:T(8,128)(2,1)} %bitcast.56, f32[8,8,256,128]{3,2,1,0:T(8,128)} %get-tuple-element.65.refs_1_.refs_2_, ...), custom_call_target="tpu_custom_call" | custom-call | flops 8053063680 | bytes 20971520 | tf_op jit(solution)/shard_map/pallas_call | solution.py:318
  118.9 2.2 %all-to-all-done.1 = bf16[16,4,2,64,128]{4,3,2,1,0:T(8,128)(2,1)} async-done(((bf16[16,4,2,64,128]{4,3,2,1,0:T(8,128)(2,1)}), bf16[16,4,2,64,128]{4,3,2,1,0:T(8,128)(2,1)}, u32[]{:S(2)}, u32[]{:S(2)}) %all-to-all-start.1) | async-done | bytes 2097184 | tf_op jit(solution)/shard_map/all_to_all | solution.py:483
  121.1 13.2 %shard_map.79 = (bf16[2,8,256,128]{3,2,1,0:T(8,128)(2,1)}, bf16[2,8,256,128]{3,2,1,0:T(8,128)(2,1)}, f32[12,128,128]{2,1,0:T(8,128)}) custom-call(f32[3,8]{1,0:T(4,128)} %copy-done.4, bf16[4,4,4,2,64,128]{5,4,3,2,1,0:T(8,128)(2,1)} %bitcast.2.refs_0_, f32[8,8,256,128]{3,2,1,0:T(8,128)} %get-tuple-element.65.refs_1_.refs_2_, ...), custom_call_target="tpu_custom_call" | custom-call | flops 8053063680 | bytes 20971520 | tf_op jit(solution)/shard_map/pallas_call | solution.py:318
  135.7 2.2 %collective-permute-start.4 = (f32[768,128]{1,0:T(8,128)S(1)}, f32[768,128]{1,0:T(8,128)S(1)}, u32[]{:S(2)}, u32[]{:S(2)}) collective-permute-start(f32[768,128]{1,0:T(8,128)S(1)} %dynamic-slice_bitcast_fusion), channel_id=1, source_target_pairs={{0,1},{1,0},{2,3},{3,2},{4,5},{5,4},{6,7},{7,6},{8,9},{9,8},{10,11... | collective-permute-start | bytes 1179656 | tf_op jit(solution)/shard_map/ppermute | solution.py:435
  140.4 1.5 collective-permute-start.6
  141.9 1.9 %collective-permute-start.7 = (f32[192,128]{1,0:T(8,128)S(1)}, f32[192,128]{1,0:T(8,128)S(1)}, u32[]{:S(2)}, u32[]{:S(2)}) collective-permute-start(f32[192,128]{1,0:T(8,128)S(1)} %get-tuple-element.127), channel_id=1, source_target_pairs={{0,6},{2,4},{4,2},{6,0},{1,7},{3,5},{5,3},{7,1},{8,14},{10,12},{12... | collective-permute-start | bytes 294920 | tf_op jit(solution)/shard_map/ppermute | solution.py:435
  143.9 8.0 %shard_map.80.refs_8_ = bf16[8,8,256,128]{3,2,1,0:T(8,128)(2,1)} custom-call(bf16[1,8,256,128]{3,2,1,0:T(8,128)(2,1)} %copy-done.12, bf16[2,8,256,128]{3,2,1,0:T(8,128)(2,1)} %get-tuple-element.87.refs_1_.refs_2_, bf16[2,8,256,128]{3,2,1,0:T(8,128)(2,1)} %get-tuple-element.87.refs_1_.refs_2_, ...), custom_call_target="tpu_custom_call" | custom-call | flops 6442450944 | bytes 6291456 | tf_op jit(solution)/shard_map/pallas_call | solution.py:405
  152.0 4.3 %collective-permute-start.10 = (f32[192,128]{1,0:T(8,128)S(1)}, f32[192,128]{1,0:T(8,128)S(1)}, u32[]{:S(2)}, u32[]{:S(2)}) collective-permute-start(f32[192,128]{1,0:T(8,128)S(1)} %fusion.1), channel_id=1, source_target_pairs={{0,24},{8,16},{16,8},{24,0},{1,25},{9,17},{17,9},{25,1},{2,26},{10... | collective-permute-start | bytes 294920 | tf_op jit(solution)/shard_map/ppermute | solution.py:435
  156.8 1.4 collective-permute-start.9
  158.2 8.0 %shard_map.81 = bf16[8,8,256,128]{3,2,1,0:T(8,128)(2,1)} custom-call(bf16[2,8,256,128]{3,2,1,0:T(8,128)(2,1)} %get-tuple-element.104.refs_3_.refs_4_.refs_0_, bf16[2,8,256,128]{3,2,1,0:T(8,128)(2,1)} %get-tuple-element.105.refs_5_.refs_1_.refs_2_, ...), custom_call_target="tpu_custom_call", output_to_operand_aliasing={{}: (8, {})} | custom-call | flops 6442450944 | bytes 6291456 | tf_op jit(solution)/shard_map/pallas_call | solution.py:405
  166.9 1.6 collective-permute-start.12
  169.8 1.9 %collective-permute-done.11 = f32[192,128]{1,0:T(8,128)S(1)} collective-permute-done((f32[192,128]{1,0:T(8,128)S(1)}, f32[192,128]{1,0:T(8,128)S(1)}, u32[]{:S(2)}, u32[]{:S(2)}) %collective-permute-start.11) | collective-permute-done | bytes 98336 | tf_op jit(solution)/shard_map/ppermute | solution.py:435
  172.6 1.6 collective-permute-done.13
  (74 shorter events, 22.0 us)
Async XLA Ops:
  3.9 57.9 %all-to-all-start = ((bf16[16,4,2,64,128]{4,3,2,1,0:T(8,128)(2,1)}), bf16[16,4,2,64,128]{4,3,2,1,0:T(8,128)(2,1)S(1)}, u32[]{:S(2)}, u32[]{:S(2)}) async-start(bf16[16,4,2,64,128]{4,3,2,1,0:T(8,128)(2,1)} %pad_maximum_fusion), calls=%async_computation | async-start | bytes 4194304 | tf_op jit(solution)/shard_map/all_to_all | solution.py:483
  12.2 10.5 %copy-start.2 = (bf16[3,3,128,128]{3,2,1,0:T(8,128)(2,1)S(1)}, bf16[3,3,128,128]{3,2,1,0:T(8,128)(2,1)}, u32[]{:S(2)}) copy-start(bf16[3,3,128,128]{3,2,1,0:T(8,128)(2,1)} %spatial.1) | copy-start | bytes 884740
  12.2 10.5 %copy-start.3 = (bf16[3,128,128]{2,1,0:T(8,128)(2,1)S(1)}, bf16[3,128,128]{2,1,0:T(8,128)(2,1)}, u32[]{:S(2)}) copy-start(bf16[3,128,128]{2,1,0:T(8,128)(2,1)} %temporal.1) | copy-start | bytes 294916
  12.2 10.5 %copy-start.5 = (s32[4]{0:T(128)S(1)}, s32[4]{0:T(128)}, u32[]{:S(2)}) copy-start(s32[4]{0:T(128)} %lengths.1) | copy-start | bytes 52
  13.5 59.9 %collective-permute-start = (bf16[1,8,256,128]{3,2,1,0:T(8,128)(2,1)S(1)}, bf16[1,8,256,128]{3,2,1,0:T(8,128)(2,1)}, u32[]{:S(2)}, u32[]{:S(2)}) collective-permute-start(bf16[1,8,256,128]{3,2,1,0:T(8,128)(2,1)S(1)} %get-tuple-element.122), channel_id=1, source_target_pairs={{0,2},{2,4},{4,6},{6,8},{8,10},{10,12},{12,14},{14,16},{16,18},{18... | collective-permute-start | bytes 1572872 | tf_op jit(solution)/shard_map/ppermute | solution.py:19
  18.2 55.3 %collective-permute-start.1 = (bf16[1,8,256,128]{3,2,1,0:T(8,128)(2,1)S(1)}, bf16[1,8,256,128]{3,2,1,0:T(8,128)(2,1)}, u32[]{:S(2)}, u32[]{:S(2)}) collective-permute-start(bf16[1,8,256,128]{3,2,1,0:T(8,128)(2,1)S(1)} %get-tuple-element.121), channel_id=1, source_target_pairs={{2,0},{4,2},{6,4},{8,6},{10,8},{12,10},{14,12},{16,14},{18,16},{20... | collective-permute-start | bytes 1572872 | tf_op jit(solution)/shard_map/ppermute | solution.py:20
  27.0 1.0 copy-start.7
  61.7 36.3 %copy-start.10 = (bf16[16,4,2,64,128]{4,3,2,1,0:T(8,128)(2,1)}, bf16[16,4,2,64,128]{4,3,2,1,0:T(8,128)(2,1)S(1)}, u32[]{:S(2)}) copy-start(bf16[16,4,2,64,128]{4,3,2,1,0:T(8,128)(2,1)S(1)} %all-to-all-done) | copy-start | bytes 6291460
  61.7 59.3 %all-to-all-start.1 = ((bf16[16,4,2,64,128]{4,3,2,1,0:T(8,128)(2,1)}), bf16[16,4,2,64,128]{4,3,2,1,0:T(8,128)(2,1)}, u32[]{:S(2)}, u32[]{:S(2)}) async-start(bf16[16,4,2,64,128]{4,3,2,1,0:T(8,128)(2,1)} %concatenate.8), calls=%async_computation.1 | async-start | bytes 4194304 | tf_op jit(solution)/shard_map/all_to_all | solution.py:483
  100.2 34.1 %collective-permute-start.2 = (bf16[1,8,256,128]{3,2,1,0:T(8,128)(2,1)S(1)}, bf16[1,8,256,128]{3,2,1,0:T(8,128)(2,1)S(1)}, u32[]{:S(2)}, u32[]{:S(2)}) collective-permute-start(bf16[1,8,256,128]{3,2,1,0:T(8,128)(2,1)S(1)} %get-tuple-element.77), channel_id=1, source_target_pairs={{0,2},{2,4},{4,6},{6,8},{8,10},{10,12},{12,14},{14,16},{16,18},{18... | collective-permute-start | bytes 1572872 | tf_op jit(solution)/shard_map/ppermute | solution.py:19
  104.0 30.3 %collective-permute-start.3 = (bf16[1,8,256,128]{3,2,1,0:T(8,128)(2,1)S(1)}, bf16[1,8,256,128]{3,2,1,0:T(8,128)(2,1)S(1)}, u32[]{:S(2)}, u32[]{:S(2)}) collective-permute-start(bf16[1,8,256,128]{3,2,1,0:T(8,128)(2,1)S(1)} %get-tuple-element.78), channel_id=1, source_target_pairs={{2,0},{4,2},{6,4},{8,6},{10,8},{12,10},{14,12},{16,14},{18,16},{20... | collective-permute-start | bytes 1572872 | tf_op jit(solution)/shard_map/ppermute | solution.py:20
  134.3 9.6 %copy-start.12 = (bf16[1,8,256,128]{3,2,1,0:T(8,128)(2,1)}, bf16[1,8,256,128]{3,2,1,0:T(8,128)(2,1)S(1)}, u32[]{:S(2)}) copy-start(bf16[1,8,256,128]{3,2,1,0:T(8,128)(2,1)S(1)} %collective-permute-done.2.refs_0_) | copy-start | bytes 1572868
  134.3 17.6 %copy-start.11 = (bf16[1,8,256,128]{3,2,1,0:T(8,128)(2,1)}, bf16[1,8,256,128]{3,2,1,0:T(8,128)(2,1)S(1)}, u32[]{:S(2)}) copy-start(bf16[1,8,256,128]{3,2,1,0:T(8,128)(2,1)S(1)} %collective-permute-done.3.refs_5_) | copy-start | bytes 1572868
  135.7 3.6 %collective-permute-start.4 = (f32[768,128]{1,0:T(8,128)S(1)}, f32[768,128]{1,0:T(8,128)S(1)}, u32[]{:S(2)}, u32[]{:S(2)}) collective-permute-start(f32[768,128]{1,0:T(8,128)S(1)} %dynamic-slice_bitcast_fusion), channel_id=1, source_target_pairs={{0,1},{1,0},{2,3},{3,2},{4,5},{5,4},{6,7},{7,6},{8,9},{9,8},{10,11... | collective-permute-start | bytes 1179656 | tf_op jit(solution)/shard_map/ppermute | solution.py:435
  140.3 11.6 %collective-permute-start.5 = (f32[192,128]{1,0:T(8,128)S(1)}, f32[192,128]{1,0:T(8,128)S(1)}, u32[]{:S(2)}, u32[]{:S(2)}) collective-permute-start(f32[192,128]{1,0:T(8,128)S(1)} %get-tuple-element.129), channel_id=1, source_target_pairs={{0,2},{2,0},{4,6},{6,4},{1,3},{3,1},{5,7},{7,5},{8,10},{10,8},{12,... | collective-permute-start | bytes 294920 | tf_op jit(solution)/shard_map/ppermute | solution.py:435
  140.4 11.5 %collective-permute-start.6 = (f32[192,128]{1,0:T(8,128)S(1)}, f32[192,128]{1,0:T(8,128)S(1)}, u32[]{:S(2)}, u32[]{:S(2)}) collective-permute-start(f32[192,128]{1,0:T(8,128)S(1)} %get-tuple-element.128), channel_id=1, source_target_pairs={{0,4},{2,6},{4,0},{6,2},{1,5},{3,7},{5,1},{7,3},{8,12},{10,14},{12... | collective-permute-start | bytes 294920 | tf_op jit(solution)/shard_map/ppermute | solution.py:435
  141.9 10.0 %collective-permute-start.7 = (f32[192,128]{1,0:T(8,128)S(1)}, f32[192,128]{1,0:T(8,128)S(1)}, u32[]{:S(2)}, u32[]{:S(2)}) collective-permute-start(f32[192,128]{1,0:T(8,128)S(1)} %get-tuple-element.127), channel_id=1, source_target_pairs={{0,6},{2,4},{4,2},{6,0},{1,7},{3,5},{5,3},{7,1},{8,14},{10,12},{12... | collective-permute-start | bytes 294920 | tf_op jit(solution)/shard_map/ppermute | solution.py:435
  152.0 14.2 %collective-permute-start.10 = (f32[192,128]{1,0:T(8,128)S(1)}, f32[192,128]{1,0:T(8,128)S(1)}, u32[]{:S(2)}, u32[]{:S(2)}) collective-permute-start(f32[192,128]{1,0:T(8,128)S(1)} %fusion.1), channel_id=1, source_target_pairs={{0,24},{8,16},{16,8},{24,0},{1,25},{9,17},{17,9},{25,1},{2,26},{10... | collective-permute-start | bytes 294920 | tf_op jit(solution)/shard_map/ppermute | solution.py:435
  156.3 9.9 %collective-permute-start.8 = (f32[192,128]{1,0:T(8,128)S(1)}, f32[192,128]{1,0:T(8,128)S(1)}, u32[]{:S(2)}, u32[]{:S(2)}) collective-permute-start(f32[192,128]{1,0:T(8,128)S(1)} %fusion.1), channel_id=1, source_target_pairs={{0,8},{8,0},{16,24},{24,16},{1,9},{9,1},{17,25},{25,17},{2,10},{10... | collective-permute-start | bytes 294920 | tf_op jit(solution)/shard_map/ppermute | solution.py:435
  156.8 9.4 %collective-permute-start.9 = (f32[192,128]{1,0:T(8,128)S(1)}, f32[192,128]{1,0:T(8,128)S(1)}, u32[]{:S(2)}, u32[]{:S(2)}) collective-permute-start(f32[192,128]{1,0:T(8,128)S(1)} %fusion.1), channel_id=1, source_target_pairs={{0,16},{8,24},{16,0},{24,8},{1,17},{9,25},{17,1},{25,9},{2,18},{10... | collective-permute-start | bytes 294920 | tf_op jit(solution)/shard_map/ppermute | solution.py:435
  166.3 5.5 %collective-permute-start.11 = (f32[192,128]{1,0:T(8,128)S(1)}, f32[192,128]{1,0:T(8,128)S(1)}, u32[]{:S(2)}, u32[]{:S(2)}) collective-permute-start(f32[192,128]{1,0:T(8,128)S(1)} %add_add_fusion), channel_id=1, source_target_pairs={{0,2},{2,0},{4,6},{6,4},{1,3},{3,1},{5,7},{7,5},{8,10},{10,8},{12,... | collective-permute-start | bytes 294920 | tf_op jit(solution)/shard_map/ppermute | solution.py:435
  166.9 5.7 %collective-permute-start.12 = (f32[192,128]{1,0:T(8,128)S(1)}, f32[192,128]{1,0:T(8,128)S(1)}, u32[]{:S(2)}, u32[]{:S(2)}) collective-permute-start(f32[192,128]{1,0:T(8,128)S(1)} %add_add_fusion), channel_id=1, source_target_pairs={{0,4},{2,6},{4,0},{6,2},{1,5},{3,7},{5,1},{7,3},{8,12},{10,14},{12... | collective-permute-start | bytes 294920 | tf_op jit(solution)/shard_map/ppermute | solution.py:435
  168.6 5.6 %collective-permute-start.13 = (f32[192,128]{1,0:T(8,128)S(1)}, f32[192,128]{1,0:T(8,128)S(1)}, u32[]{:S(2)}, u32[]{:S(2)}) collective-permute-start(f32[192,128]{1,0:T(8,128)S(1)} %add_add_fusion), channel_id=1, source_target_pairs={{0,6},{2,4},{4,2},{6,0},{1,7},{3,5},{5,3},{7,1},{8,14},{10,12},{12... | collective-permute-start | bytes 294920 | tf_op jit(solution)/shard_map/ppermute | solution.py:435
  175.0 1.8 collective-permute-start.14
  (6 other events, 4.7 us)

commit v6 on v5

--- a/solution.py
+++ b/solution.py
@@ -111,104 +111,85 @@
     return parts[0] if len(parts) == 1 else jnp.concatenate(parts, axis=1)
 
 
-def forward_kernel(group, width, lag, *refs):
-    now, before = refs[:group], refs[group : 2 * group]
-    left, left_before, right, right_before, temporal, spatial, slope, turned, held = refs[2 * group :]
-    step = pl.program_id(1)
-    rows, chans = slope.shape[2], slope.shape[3]
-    sources = []
-    for e in range(group):
-        line = []
-        for ours, l_ref, r_ref in ((before[e], left_before, right_before), (now[e], left, right)):
+def forward_kernel(group, now, before, left, left_before, right, right_before, *refs):
+    temporal, spatial, slope, turned = refs
+    width, rows, chans = slope.shape[0], slope.shape[2], slope.shape[3]
+    columns = [(left_before.at[0], left.at[0])]
+    columns += [(before.at[c], now.at[c]) for c in range(width)]
+    columns += [(right_before.at[0], right.at[0])]
+    triples = []
+    for base in range(0, width + 2, group):
+        sources = []
+        for e in range(group):
+            older, newer = columns[base + e]
             for frame in range(2):
-                tile = ours[0, frame]
-                if e == 0:
-                    tile = jnp.where(step == 0, l_ref[0, frame], tile)
-                if e == group - 1:
-                    tile = jnp.where(step * group + e == width + 1, r_ref[0, frame], tile)
-                line.append(tile)
-                if ours is now[e]:
-                    turned[e, frame] = tile.T
-        sources.append(lanes(line))
-    mixed = jnp.dot(
-        jnp.concatenate(sources, axis=0), temporal[0], preferred_element_type=jnp.float32
-    ).astype(jnp.bfloat16)
-    for e in range(group):
-        value = mixed[e * rows : (e + 1) * rows]
-        above, below = row_shifts(value.astype(jnp.float32), rows)
-        for frame in range(2):
-            at = slice(frame * chans, (frame + 1) * chans)
-            held[step * group + e, frame] = lanes([above[:, at], value[:, at], below[:, at]])
-
-    @pl.when(step >= lag)
-    def _():
-        base = (step - lag) * group
-        source = lanes([held[base + k].reshape(2 * rows, 3 * chans) for k in range(group + 2)])
+                turned[base + e, frame] = newer[frame].T
+            sources.append(lanes([ref[frame] for ref in (older, newer) for frame in range(2)]))
+        mixed = jnp.dot(
+            jnp.concatenate(sources, axis=0), temporal[0], preferred_element_type=jnp.float32
+        ).astype(jnp.bfloat16)
+        for e in range(group):
+            lines = []
+            for frame in range(2):
+                value = mixed[e * rows : (e + 1) * rows, frame * chans : (frame + 1) * chans]
+                above, below = row_shifts(value.astype(jnp.float32), rows)
+                lines.append(lanes([above, value, below]))
+            triples.append(jnp.concatenate(lines, axis=0))
+    for base in range(0, width, group):
+        source = lanes(triples[base : base + group + 2])
         pre = jnp.dot(source, spatial[...], preferred_element_type=jnp.float32)
         sig = jax.nn.sigmoid(pre)
         value = sig * (1.0 + pre * (1.0 - sig))
         for e in range(group):
-            slope[e] = value[:, e * chans : (e + 1) * chans].reshape(2, rows, chans)
+            slope[base + e] = value[:, e * chans : (e + 1) * chans].reshape(2, rows, chans)
 
 
 def forward(video, left, right, temporal, spatial, group):
     width, frames, rows, chans = video.shape
-    lag = 2 // group
-    steps = (width + 2) // group
-
-    def own(e, back):
-        return pl.BlockSpec(
-            (1, 2, rows, chans),
-            lambda p, j: (
-                jnp.clip(j * group + e - 1, 0, width - 1),
-                jnp.maximum(p - back, 0),
-                0,
-                0,
-            ),
-        )
-
-    def edge(back):
-        return pl.BlockSpec((1, 2, rows, chans), lambda p, j: (0, jnp.maximum(p - back, 0), 0, 0))
-
-    out = pl.BlockSpec((group, 2, rows, chans), lambda p, j: (jnp.maximum(j - lag, 0), p, 0, 0))
+
+    def pair(cols, back):
+        return pl.BlockSpec((cols, 2, rows, chans), lambda p: (0, jnp.maximum(p - back, 0), 0, 0))
+
     pixels = width * frames * rows
     return pl.pallas_call(
-        functools.partial(forward_kernel, group, width, lag),
-        grid=(frames // 2, steps),
-        in_specs=[own(e, 0) for e in range(group)]
-        + [own(e, 1) for e in range(group)]
-        + [
-            edge(0),
-            edge(1),
-            edge(0),
-            edge(1),
-            pl.BlockSpec((1, 4 * chans, 2 * chans), lambda p, j: (p, 0, 0)),
-            pl.BlockSpec(spatial.shape, lambda p, j: (0, 0)),
+        functools.partial(forward_kernel, group),
+        grid=(frames // 2,),
+        in_specs=[
+            pair(width, 0),
+            pair(width, 1),
+            pair(1, 0),
+            pair(1, 1),
+            pair(1, 0),
+            pair(1, 1),
+            pl.BlockSpec((1, 4 * chans, 2 * chans), lambda p: (p, 0, 0)),
+            pl.BlockSpec(spatial.shape, lambda p: (0, 0)),
         ],
-        out_specs=[out, pl.BlockSpec((group, 2, chans, rows), lambda p, j: (j, p, 0, 0))],
+        out_specs=[
+            pair(width, 0),
+            pl.BlockSpec((width + 2, 2, chans, rows), lambda p: (0, p, 0, 0)),
+        ],
         out_shape=[
             jax.ShapeDtypeStruct((width, frames, rows, chans), jnp.float32),
             jax.ShapeDtypeStruct((width + 2, frames, chans, rows), jnp.bfloat16),
         ],
-        scratch_shapes=[pltpu.VMEM((width + 2, 2, rows, 3 * chans), jnp.bfloat16)],
         compiler_params=pltpu.CompilerParams(vmem_limit_bytes=60 * MIB),
         cost_estimate=pl.CostEstimate(
             flops=pixels * chans * chans * 2 * 24 * 5,
             bytes_accessed=pixels * chans * 14,
             transcendentals=pixels * chans,
         ),
-    )(*([video] * (2 * group)), left, left, right, right, temporal, spatial)
-
-
-def moments_kernel(group, groups, places, fresh, scale, masks, *refs):
+    )(video, video, left, left, right, right, temporal, spatial)
+
+
+def moments_kernel(group, groups, places, fresh, final, scale, masks, side, *refs):
     count = len(groups)
     grads, refs = refs[0], refs[1:]
     slopes, refs = refs[:count], refs[count:]
     now, before, refs = refs[: len(places)], refs[len(places) : 2 * len(places)], refs[2 * len(places) :]
     temporal, spatial, refs = refs[0], refs[1], refs[2:]
-    total, refs = refs[-1], refs[:-1]
+    total, ordered, refs = refs[-2], refs[-1], refs[:-2]
     earlier, refs = (None, refs) if fresh else (refs[0], refs[1:])
-    deltas, sums = refs[:count], refs[count]
+    deltas, sums = refs[:count], ordered if final else refs[count]
     pair = pl.program_id(0)
     bands, band = grads.shape[1], grads.shape[4]
     rows, chans = slopes[0].shape[2], slopes[0].shape[3]
@@ -292,9 +273,13 @@
         for k in range(9):
             value = spatial_sum[:, k * chans : (k + 1) * chans] * scale
             sums[3 + k] = value if earlier is None else earlier[3 + k] + value
-
-
-def moments(received, slope, turned, masks, temporal, spatial, earlier, groups, group):
+        if final:
+            half = ordered.shape[0] // 2
+            refs[count][...] = ordered[pl.ds(half * side[0], half)]
+            refs[count + 1][...] = ordered[pl.ds(half * (1 - side[0]), half)]
+
+
+def moments(received, slope, turned, masks, temporal, spatial, earlier, groups, group, final):
     fresh = earlier is None
     frames, rows, chans = slope.shape[1:]
     bands, band = received.shape[1], received.shape[4]
@@ -304,25 +289,27 @@
     scale = float(frames * rows * slope.shape[0] * lax.axis_size(MESH_AXES)) ** (-0.5)
 
     def own(n):
-        return pl.BlockSpec((group, 2, rows, chans), lambda p, m: (n, p, 0, 0))
+        return pl.BlockSpec((group, 2, rows, chans), lambda p, *m: (n, p, 0, 0))
 
     def columns(n, back):
         return pl.BlockSpec(
-            (group, 2, chans, rows), lambda p, m: (n, jnp.maximum(p - back, 0), 0, 0)
+            (group, 2, chans, rows), lambda p, *m: (n, jnp.maximum(p - back, 0), 0, 0)
         )
 
     def whole(shape):
-        return pl.BlockSpec(shape, lambda p, m: (0,) * len(shape))
+        return pl.BlockSpec(shape, lambda p, *m: (0,) * len(shape))
 
     sums_shape = (12, chans, chans)
-    *deltas, sums = pl.pallas_call(
-        functools.partial(moments_kernel, group, groups, places, fresh, scale),
+    outs = [(6, chans, chans)] * 2 if final else [sums_shape]
+    side = lax.axis_index("width").astype(jnp.int32).reshape(1)
+    results = pl.pallas_call(
+        functools.partial(moments_kernel, group, groups, places, fresh, final, scale),
         grid_spec=pltpu.PrefetchScalarGridSpec(
-            num_scalar_prefetch=1,
+            num_scalar_prefetch=2,
             grid=(frames // 2,),
             in_specs=[
                 pl.BlockSpec(
-                    (1, bands, count * group, 2, band, chans), lambda p, m: (p, 0, 0, 0, 0, 0)
+                    (1, bands, count * group, 2, band, chans), lambda p, *m: (p, 0, 0, 0, 0, 0)
                 )
             ]
             + [own(n) for n in groups]
@@ -330,13 +317,14 @@
             + [columns(n, 1) for n in places]
             + [whole(temporal.shape), whole(spatial.shape)]
             + ([] if fresh else [whole(sums_shape)]),
-            out_specs=[own(0) for _ in groups] + [whole(sums_shape)],
+            out_specs=[own(0) for _ in groups] + [whole(shape) for shape in outs],
             scratch_shapes=[
                 pltpu.VMEM((3, (group + 2) * chans, group * 3 * chans), jnp.float32),
+                pltpu.VMEM(sums_shape, jnp.float32),
             ],
         ),
         out_shape=[jax.ShapeDtypeStruct((group, frames, rows, chans), jnp.bfloat16)] * count
-        + [jax.ShapeDtypeStruct(sums_shape, jnp.float32)],
+        + [jax.ShapeDtypeStruct(shape, jnp.float32) for shape in outs],
         compiler_params=pltpu.CompilerParams(vmem_limit_bytes=60 * MIB),
         cost_estimate=pl.CostEstimate(
             flops=pixels * chans * chans * 2 * 30,
@@ -345,6 +333,7 @@
         ),
     )(
         masks,
+        side,
         received,
         *([slope] * count),
         *([turned] * (2 * len(places))),
@@ -352,7 +341,7 @@
         spatial,
         *([] if fresh else [earlier]),
     )
-    return deltas, sums
+    return results[:count], results[count:] if final else results[count]
 
 
 def backward_kernel(group, sources, *refs):
@@ -453,8 +442,8 @@
         got, state = lax.optimization_barrier((got, state))
         return value, got, state
 
-    pick = pieces(local, "width")
-    value = functools.reduce(jnp.add, exchanged("width", pick), pick(0))
+    keep, send = local
+    value = keep + exchanged("width", lambda s: send)[0]
     value, got, state = beside(
         value, lambda v: exchanged("height", pieces(v, "height")), works[0], state
     )
@@ -463,7 +452,9 @@
     value = functools.reduce(jnp.add, got, value)
     value, got, state = beside(value, lambda v: exchanged("height", lambda s: v), works[2], state)
     value = spread([value] + got, "height")
-    return spread([value] + exchanged("width", lambda s: value), "width"), state
+    (other,) = exchanged("width", lambda s: value)
+    swap = lax.axis_index("width") == 1
+    return [jnp.where(swap, other, value), jnp.where(swap, value, other)], state
 
 
 def shards(video, out_grad, lengths, temporal_weight, spatial_weight):
@@ -491,8 +482,10 @@
     def outgoing(blocks, groups):
         if len(groups) == count:
             return blocks
-        runs = [blocks[:, n * group : (n + 1) * group] for n in groups]
-        return runs[0] if len(runs) == 1 else jnp.concatenate(runs, axis=1)
+        first, step = groups[0], groups[1] - groups[0]
+        some = blocks.reshape(blocks.shape[0], count, group, *blocks.shape[2:])
+        some = some[:, first : groups[-1] + 1 : step]
+        return some.reshape(blocks.shape[0], len(groups) * group, *blocks.shape[2:])
 
     received = to_columns(outgoing(blocks, chunks[0]))
 
@@ -502,14 +495,15 @@
     slope, turned = forward(clip, left, right, temporal_mix, spatial_mix, group)
     second = None
     if len(chunks) > 1:
+        blocks, spatial_back = lax.optimization_barrier((blocks, spatial_back))
         second = outgoing(blocks, chunks[1])
         second, received = lax.optimization_barrier((second, received))
         second = to_columns(second)
     weights = (slope, turned, masks, *weights)
     deltas, local = [None] * count, None
 
-    def add(received, groups):
-        some, total = moments(received, *weights, local, groups, group)
+    def add(received, groups, final):
+        some, total = moments(received, *weights, local, groups, group, final)
         for n, delta in zip(groups, some):
             deltas[n] = delta
         return total
@@ -522,9 +516,9 @@
     tail = edge_delta(received, width - 1, received.shape[2] - 1)
     received, head, tail = lax.optimization_barrier((received, head, tail))
     delta_left, delta_right = column_neighbours(head, tail)
-    local = add(received, chunks[0])
+    local = add(received, chunks[0], second is None)
     if second is not None:
-        local = add(second, chunks[1])
+        local = add(second, chunks[1], True)
     local, deltas, delta_left, delta_right = lax.optimization_barrier(
         (local, deltas, delta_left, delta_right)
     )
@@ -541,12 +535,13 @@
         return operands, backward(*operands, spatial_back, temporal_back, filled, *part)
 
     sums, (_, video_grad) = sum_over_devices(
-        local.reshape(-1, chans),
+        [half.reshape(-1, chans) for half in local],
         [functools.partial(one_part, part) for part in parts],
         ((deltas, delta_left, delta_right), None),
     )
-    sums = sums.reshape(12, chans, chans)
-    temporal_grad, spatial_grad = sums[:3], sums[3:].reshape(3, 3, chans, chans)
+    low, high = (half.reshape(6, chans, chans) for half in sums)
+    temporal_grad = low[:3]
+    spatial_grad = jnp.concatenate([low[3:], high]).reshape(3, 3, chans, chans)
     return video_grad[None], temporal_grad, spatial_grad
 
 

time: 181 us -> 180 us (level)
  waiting for transfers between devices: 41 us -> 52.2 us
  Pallas kernels: 68.5 us -> 59.5 us
    all_to_all x2, waiting for transfers between devices: 34.2 us -> 43.3 us  [to_columns(): lax.all_to_all(part, ('tm', 'height'), split_axis=0, concat_axis=0, tiled...]
    pallas_call x1, Pallas kernels: 24.5 us -> 15.5 us  [forward(): pl.pallas_call(functools.partial(forward_kernel, group), grid=(frames //...]
    slice x3, local copies, waits for them, and re-layouts: 3.28 us -> 7.19 us  [the longest x2 6.49 us: outgoing(): some = some[:, first:groups[-1] + 1:step]]
    concatenate x1 -> x0, local copies, waits for them, and re-layouts: 3.23 us -> none  [outgoing(): return runs[0] if len(runs) == 1 else jnp.concatenate(runs, axis=1)]
    ppermute x11, waiting for transfers between devices: 6.86 us -> 8.96 us  [exchanged(): lax.ppermute(parts(s), axis, [(i, i ^ s) for i in range(count)])]
  transfers between devices with their start and end apart: 17 -> 17, of which waited for: 7 -> 8; matrix products, arithmetic and copies ran while one was open for 4% -> 4% of each run, Pallas kernels for 38% -> 33%
where the time goes in v6:
time: 180 us; the launch traced here: 179 us
  Pallas kernels  59.5 us (33%)
  waiting for transfers between devices  52.2 us (29%)
  starting transfers between devices  46.6 us (26%)
  local copies, waits for them, and re-layouts  15.1 us (8%)
  other arithmetic  4.38 us (2%)
    all_to_all x2, waiting for transfers between devices, to_columns(): lax.all_to_all(part, ('tm', 'height'), split_axis=0, concat_axis=0, tiled...  43.3 us
    pallas_call x2, Pallas kernels, moments(): pl.pallas_call(functools.partial(moments_kernel, group, groups, places, f...  26.5 us
    all_to_all x2, starting transfers between devices, to_columns(): lax.all_to_all(part, ('tm', 'height'), split_axis=0, concat_axis=0, tiled...  20.2 us
    pallas_call x2, Pallas kernels, backward(): pl.pallas_call(functools.partial(backward_kernel, group, [0] * len(ext)),...  16.1 us
    pallas_call x1, Pallas kernels, forward(): pl.pallas_call(functools.partial(forward_kernel, group), grid=(frames //...  15.5 us
    ppermute x11, starting transfers between devices, exchanged(): lax.ppermute(parts(s), axis, [(i, i ^ s) for i in range(count)])  15.2 us
    ppermute x11, waiting for transfers between devices, exchanged(): lax.ppermute(parts(s), axis, [(i, i ^ s) for i in range(count)])  8.96 us
    ppermute x2, starting transfers between devices, column_neighbours(): left = lax.ppermute(last, MESH_AXES, pairs)  8.43 us
  transfers between devices with their start and end apart: 17, of which 8 were waited for; matrix products, arithmetic and copies ran while one was open for 4% of the time, Pallas kernels for 33%

profile of v6, /device:TPU:0, one launch (start us, length us, event | category | flops | bytes accessed | tf_op | source)
XLA Modules:
  0.0 178.8 jit_solution(15402968876673783730)
XLA Ops:
  0.6 3.3 %slice.43 = bf16[16,2,2,2,64,128]{5,4,3,2,1,0:T(8,128)(2,1)} slice(bf16[16,4,2,2,64,128]{5,4,3,2,1,0:T(8,128)(2,1)} %bitcast.62), slice={[0:16:1], [0:4:3], [0:2:1], [0:2:1], [0:64:1], [0:128:1]} | slice | bytes 4194304 | tf_op jit(solution)/shard_map/slice | solution.py:487
  3.9 8.4 %all-to-all-start = ((bf16[16,4,2,64,128]{4,3,2,1,0:T(8,128)(2,1)}), bf16[16,4,2,64,128]{4,3,2,1,0:T(8,128)(2,1)S(1)}, u32[]{:S(2)}, u32[]{:S(2)}) async-start(bf16[16,4,2,64,128]{4,3,2,1,0:T(8,128)(2,1)} %bitcast.59), calls=%async_computation | async-start | bytes 4194304 | tf_op jit(solution)/shard_map/all_to_all | solution.py:474
  13.6 4.6 %collective-permute-start = (bf16[1,8,256,128]{3,2,1,0:T(8,128)(2,1)S(1)}, bf16[1,8,256,128]{3,2,1,0:T(8,128)(2,1)}, u32[]{:S(2)}, u32[]{:S(2)}) collective-permute-start(bf16[1,8,256,128]{3,2,1,0:T(8,128)(2,1)S(1)} %get-tuple-element.130), channel_id=1, source_target_pairs={{0,2},{2,4},{4,6},{6,8},{8,10},{10,12},{12,14},{14,16},{16,18},{18... | collective-permute-start | bytes 1572872 | tf_op jit(solution)/shard_map/ppermute | solution.py:19
  26.6 3.2 %slice.58 = bf16[16,2,2,2,64,128]{5,4,3,2,1,0:T(8,128)(2,1)} slice(bf16[16,4,2,2,64,128]{5,4,3,2,1,0:T(8,128)(2,1)} %bitcast.63), slice={[0:16], [1:3], [0:2], [0:2], [0:64], [0:128]} | slice | bytes 4194304 | tf_op jit(solution)/shard_map/slice | solution.py:487
  29.9 32.0 %all-to-all-done = bf16[16,4,2,64,128]{4,3,2,1,0:T(8,128)(2,1)S(1)} async-done(((bf16[16,4,2,64,128]{4,3,2,1,0:T(8,128)(2,1)}), bf16[16,4,2,64,128]{4,3,2,1,0:T(8,128)(2,1)S(1)}, u32[]{:S(2)}, u32[]{:S(2)}) %all-to-all-start) | async-done | bytes 2097184 | tf_op jit(solution)/shard_map/all_to_all | solution.py:474
  61.9 11.7 %all-to-all-start.1 = ((bf16[16,4,2,64,128]{4,3,2,1,0:T(8,128)(2,1)}), bf16[16,4,2,64,128]{4,3,2,1,0:T(8,128)(2,1)}, u32[]{:S(2)}, u32[]{:S(2)}) async-start(bf16[16,4,2,64,128]{4,3,2,1,0:T(8,128)(2,1)} %bitcast.58), calls=%async_computation.1 | async-start | bytes 4194304 | tf_op jit(solution)/shard_map/all_to_all | solution.py:474
  73.7 15.5 %shard_map.77 = (f32[8,8,256,128]{3,2,1,0:T(8,128)}, bf16[10,8,128,256]{3,2,1,0:T(8,128)(2,1)}) custom-call(bf16[8,8,256,128]{3,2,1,0:T(8,128)(2,1)} %bitcast.70, bf16[8,8,256,128]{3,2,1,0:T(8,128)(2,1)} %bitcast.71, bf16[1,8,256,128]{3,2,1,0:T(8,128)(2,1)} %collective-permute-done.left.left_before, ...), custom_call_target="tpu_custom_call" | custom-call | flops 64424509440 | bytes 29360128 | tf_op jit(solution)/shard_map/pallas_call | solution.py:154
  89.6 1.8 %multiply_convert_fusion = (bf16[1,8,256,128]{3,2,1,0:T(8,128)(2,1)S(1)}, bf16[1,8,256,128]{3,2,1,0:T(8,128)(2,1)S(1)}) fusion(f32[1,8,256,128]{3,2,1,0:T(8,128)S(1)} %bitcast.61, f32[8,8,256,128]{3,2,1,0:T(8,128)} %get-tuple-element.71.refs_1_.refs_2_, f32[1,8,256,128]{3,2,1,0:T(8,128)S(1)} %bitcast.60), kind=kLoop, calls=%fused_computation.3 | loop fusion | flops 1048576 | bytes 5242880 | tf_op jit(solution)/shard_map/convert_element_type | solution.py:513
  91.5 3.8 %collective-permute-start.2 = (bf16[1,8,256,128]{3,2,1,0:T(8,128)(2,1)S(1)}, bf16[1,8,256,128]{3,2,1,0:T(8,128)(2,1)S(1)}, u32[]{:S(2)}, u32[]{:S(2)}) collective-permute-start(bf16[1,8,256,128]{3,2,1,0:T(8,128)(2,1)S(1)} %get-tuple-element.84), channel_id=1, source_target_pairs={{0,2},{2,4},{4,6},{6,8},{8,10},{10,12},{12,14},{14,16},{16,18},{18... | collective-permute-start | bytes 1572872 | tf_op jit(solution)/shard_map/ppermute | solution.py:19
  95.3 1.5 collective-permute-start.3
  96.7 13.3 %shard_map.78 = (bf16[2,8,256,128]{3,2,1,0:T(8,128)(2,1)}, bf16[2,8,256,128]{3,2,1,0:T(8,128)(2,1)}, f32[12,128,128]{2,1,0:T(8,128)}) custom-call(f32[3,8]{1,0:T(4,128)} %copy-done.4, s32[1]{0:T(128)} %bitcast.side, bf16[4,4,4,2,64,128]{5,4,3,2,1,0:T(8,128)(2,1)} %bitcast.57, f32[8,8,256,128]{3,2,1,0:T(8,128)} %get-tuple-element.71.refs_1_.refs_2_, ...), custom_call_target="tpu_custom_call" | custom-call | flops 8053063680 | bytes 20971520 | tf_op jit(solution)/shard_map/pallas_call | solution.py:305
  110.0 11.2 %all-to-all-done.1 = bf16[16,4,2,64,128]{4,3,2,1,0:T(8,128)(2,1)} async-done(((bf16[16,4,2,64,128]{4,3,2,1,0:T(8,128)(2,1)}), bf16[16,4,2,64,128]{4,3,2,1,0:T(8,128)(2,1)}, u32[]{:S(2)}, u32[]{:S(2)}) %all-to-all-start.1) | async-done | bytes 2097184 | tf_op jit(solution)/shard_map/all_to_all | solution.py:474
  121.3 13.2 %shard_map.79 = (bf16[2,8,256,128]{3,2,1,0:T(8,128)(2,1)}, bf16[2,8,256,128]{3,2,1,0:T(8,128)(2,1)}, f32[6,128,128]{2,1,0:T(8,128)}, f32[6,128,128]{2,1,0:T(8,128)}) custom-call(f32[3,8]{1,0:T(4,128)} %copy-done.4, s32[1]{0:T(128)} %bitcast.side, bf16[4,4,4,2,64,128]{5,4,3,2,1,0:T(8,128)(2,1)} %bitcast.7.refs_0_, ...), custom_call_target="tpu_custom_call" | custom-call | flops 8053063680 | bytes 20971520 | tf_op jit(solution)/shard_map/pallas_call | solution.py:305
  134.8 1.7 collective-permute-done.4
  137.7 3.3 %collective-permute-start.6 = (f32[192,128]{1,0:T(8,128)S(1)}, f32[192,128]{1,0:T(8,128)S(1)}, u32[]{:S(2)}, u32[]{:S(2)}) collective-permute-start(f32[192,128]{1,0:T(8,128)S(1)} %get-tuple-element.138), channel_id=1, source_target_pairs={{0,4},{2,6},{4,0},{6,2},{1,5},{3,7},{5,1},{7,3},{8,12},{10,14},{12... | collective-permute-start | bytes 294920 | tf_op jit(solution)/shard_map/ppermute | solution.py:424
  141.1 1.4 collective-permute-start.7
  142.4 8.0 %shard_map.80.refs_8_ = bf16[8,8,256,128]{3,2,1,0:T(8,128)(2,1)} custom-call(bf16[1,8,256,128]{3,2,1,0:T(8,128)(2,1)} %copy-done.12, bf16[2,8,256,128]{3,2,1,0:T(8,128)(2,1)} %get-tuple-element.95.refs_1_.refs_2_, bf16[2,8,256,128]{3,2,1,0:T(8,128)(2,1)} %get-tuple-element.95.refs_1_.refs_2_, ...), custom_call_target="tpu_custom_call" | custom-call | flops 6442450944 | bytes 6291456 | tf_op jit(solution)/shard_map/pallas_call | solution.py:394
  150.6 6.1 %collective-permute-start.10 = (f32[192,128]{1,0:T(8,128)S(1)}, f32[192,128]{1,0:T(8,128)S(1)}, u32[]{:S(2)}, u32[]{:S(2)}) collective-permute-start(f32[192,128]{1,0:T(8,128)S(1)} %fusion.1), channel_id=1, source_target_pairs={{0,24},{8,16},{16,8},{24,0},{1,25},{9,17},{17,9},{25,1},{2,26},{10... | collective-permute-start | bytes 294920 | tf_op jit(solution)/shard_map/ppermute | solution.py:424
  157.3 8.0 %shard_map.81 = bf16[8,8,256,128]{3,2,1,0:T(8,128)(2,1)} custom-call(bf16[2,8,256,128]{3,2,1,0:T(8,128)(2,1)} %get-tuple-element.112.refs_3_.refs_4_.refs_0_, bf16[2,8,256,128]{3,2,1,0:T(8,128)(2,1)} %get-tuple-element.113.refs_5_.refs_1_.refs_2_, ...), custom_call_target="tpu_custom_call", output_to_operand_aliasing={{}: (8, {})} | custom-call | flops 6442450944 | bytes 6291456 | tf_op jit(solution)/shard_map/pallas_call | solution.py:394
  166.9 2.0 %collective-permute-start.12 = (f32[192,128]{1,0:T(8,128)S(1)}, f32[192,128]{1,0:T(8,128)S(1)}, u32[]{:S(2)}, u32[]{:S(2)}) collective-permute-start(f32[192,128]{1,0:T(8,128)S(1)} %add_add_fusion), channel_id=1, source_target_pairs={{0,4},{2,6},{4,0},{6,2},{1,5},{3,7},{5,1},{7,3},{8,12},{10,14},{12... | collective-permute-start | bytes 294920 | tf_op jit(solution)/shard_map/ppermute | solution.py:424
  169.1 1.9 %collective-permute-done.11 = f32[192,128]{1,0:T(8,128)S(1)} collective-permute-done((f32[192,128]{1,0:T(8,128)S(1)}, f32[192,128]{1,0:T(8,128)S(1)}, u32[]{:S(2)}, u32[]{:S(2)}) %collective-permute-start.11) | collective-permute-done | bytes 98336 | tf_op jit(solution)/shard_map/ppermute | solution.py:424
  171.0 1.5 collective-permute-done.12
  172.4 2.0 %collective-permute-done.13 = f32[192,128]{1,0:T(8,128)S(1)} collective-permute-done((f32[192,128]{1,0:T(8,128)S(1)}, f32[192,128]{1,0:T(8,128)S(1)}, u32[]{:S(2)}, u32[]{:S(2)}) %collective-permute-start.13) | collective-permute-done | bytes 98336 | tf_op jit(solution)/shard_map/ppermute | solution.py:424
  175.3 1.7 collective-permute-done.14
  (64 shorter events, 16.4 us)
Async XLA Ops:
  3.9 15.7 %copy-start.2 = (bf16[3,3,128,128]{3,2,1,0:T(8,128)(2,1)S(1)}, bf16[3,3,128,128]{3,2,1,0:T(8,128)(2,1)}, u32[]{:S(2)}) copy-start(bf16[3,3,128,128]{3,2,1,0:T(8,128)(2,1)} %spatial.1) | copy-start | bytes 884740
  3.9 15.7 %copy-start.3 = (bf16[3,128,128]{2,1,0:T(8,128)(2,1)S(1)}, bf16[3,128,128]{2,1,0:T(8,128)(2,1)}, u32[]{:S(2)}) copy-start(bf16[3,128,128]{2,1,0:T(8,128)(2,1)} %temporal.1) | copy-start | bytes 294916
  3.9 15.7 %copy-start.5 = (s32[4]{0:T(128)S(1)}, s32[4]{0:T(128)}, u32[]{:S(2)}) copy-start(s32[4]{0:T(128)} %lengths.1) | copy-start | bytes 52
  3.9 58.0 %all-to-all-start = ((bf16[16,4,2,64,128]{4,3,2,1,0:T(8,128)(2,1)}), bf16[16,4,2,64,128]{4,3,2,1,0:T(8,128)(2,1)S(1)}, u32[]{:S(2)}, u32[]{:S(2)}) async-start(bf16[16,4,2,64,128]{4,3,2,1,0:T(8,128)(2,1)} %bitcast.59), calls=%async_computation | async-start | bytes 4194304 | tf_op jit(solution)/shard_map/all_to_all | solution.py:474
  13.6 60.0 %collective-permute-start = (bf16[1,8,256,128]{3,2,1,0:T(8,128)(2,1)S(1)}, bf16[1,8,256,128]{3,2,1,0:T(8,128)(2,1)}, u32[]{:S(2)}, u32[]{:S(2)}) collective-permute-start(bf16[1,8,256,128]{3,2,1,0:T(8,128)(2,1)S(1)} %get-tuple-element.130), channel_id=1, source_target_pairs={{0,2},{2,4},{4,6},{6,8},{8,10},{10,12},{12,14},{14,16},{16,18},{18... | collective-permute-start | bytes 1572872 | tf_op jit(solution)/shard_map/ppermute | solution.py:19
  18.3 55.4 %collective-permute-start.1 = (bf16[1,8,256,128]{3,2,1,0:T(8,128)(2,1)S(1)}, bf16[1,8,256,128]{3,2,1,0:T(8,128)(2,1)}, u32[]{:S(2)}, u32[]{:S(2)}) collective-permute-start(bf16[1,8,256,128]{3,2,1,0:T(8,128)(2,1)S(1)} %get-tuple-element.129), channel_id=1, source_target_pairs={{2,0},{4,2},{6,4},{8,6},{10,8},{12,10},{14,12},{16,14},{18,16},{20... | collective-permute-start | bytes 1572872 | tf_op jit(solution)/shard_map/ppermute | solution.py:20
  23.9 1.0 copy-start.7
  61.9 27.3 %copy-start.10 = (bf16[16,4,2,64,128]{4,3,2,1,0:T(8,128)(2,1)}, bf16[16,4,2,64,128]{4,3,2,1,0:T(8,128)(2,1)S(1)}, u32[]{:S(2)}) copy-start(bf16[16,4,2,64,128]{4,3,2,1,0:T(8,128)(2,1)S(1)} %all-to-all-done) | copy-start | bytes 6291460
  61.9 59.4 %all-to-all-start.1 = ((bf16[16,4,2,64,128]{4,3,2,1,0:T(8,128)(2,1)}), bf16[16,4,2,64,128]{4,3,2,1,0:T(8,128)(2,1)}, u32[]{:S(2)}, u32[]{:S(2)}) async-start(bf16[16,4,2,64,128]{4,3,2,1,0:T(8,128)(2,1)} %bitcast.58), calls=%async_computation.1 | async-start | bytes 4194304 | tf_op jit(solution)/shard_map/all_to_all | solution.py:474
  91.5 43.1 %collective-permute-start.2 = (bf16[1,8,256,128]{3,2,1,0:T(8,128)(2,1)S(1)}, bf16[1,8,256,128]{3,2,1,0:T(8,128)(2,1)S(1)}, u32[]{:S(2)}, u32[]{:S(2)}) collective-permute-start(bf16[1,8,256,128]{3,2,1,0:T(8,128)(2,1)S(1)} %get-tuple-element.84), channel_id=1, source_target_pairs={{0,2},{2,4},{4,6},{6,8},{8,10},{10,12},{12,14},{14,16},{16,18},{18... | collective-permute-start | bytes 1572872 | tf_op jit(solution)/shard_map/ppermute | solution.py:19
  95.3 39.3 %collective-permute-start.3 = (bf16[1,8,256,128]{3,2,1,0:T(8,128)(2,1)S(1)}, bf16[1,8,256,128]{3,2,1,0:T(8,128)(2,1)S(1)}, u32[]{:S(2)}, u32[]{:S(2)}) collective-permute-start(bf16[1,8,256,128]{3,2,1,0:T(8,128)(2,1)S(1)} %get-tuple-element.85), channel_id=1, source_target_pairs={{2,0},{4,2},{6,4},{8,6},{10,8},{12,10},{14,12},{16,14},{18,16},{20... | collective-permute-start | bytes 1572872 | tf_op jit(solution)/shard_map/ppermute | solution.py:20
  134.5 7.9 %copy-start.12 = (bf16[1,8,256,128]{3,2,1,0:T(8,128)(2,1)}, bf16[1,8,256,128]{3,2,1,0:T(8,128)(2,1)S(1)}, u32[]{:S(2)}) copy-start(bf16[1,8,256,128]{3,2,1,0:T(8,128)(2,1)S(1)} %collective-permute-done.2.refs_0_) | copy-start | bytes 1572868
  134.5 15.9 %copy-start.11 = (bf16[1,8,256,128]{3,2,1,0:T(8,128)(2,1)}, bf16[1,8,256,128]{3,2,1,0:T(8,128)(2,1)S(1)}, u32[]{:S(2)}) copy-start(bf16[1,8,256,128]{3,2,1,0:T(8,128)(2,1)S(1)} %collective-permute-done.3.refs_5_) | copy-start | bytes 1572868
  134.6 2.0 %collective-permute-start.4 = (f32[768,128]{1,0:T(8,128)}, f32[768,128]{1,0:T(8,128)S(1)}, u32[]{:S(2)}, u32[]{:S(2)}) collective-permute-start(f32[768,128]{1,0:T(8,128)} %bitcast.76), channel_id=1, source_target_pairs={{0,1},{1,0},{2,3},{3,2},{4,5},{5,4},{6,7},{7,6},{8,9},{9,8},{10,11... | collective-permute-start | bytes 1179656 | tf_op jit(solution)/shard_map/ppermute | solution.py:424
  137.6 12.9 %collective-permute-start.5 = (f32[192,128]{1,0:T(8,128)S(1)}, f32[192,128]{1,0:T(8,128)S(1)}, u32[]{:S(2)}, u32[]{:S(2)}) collective-permute-start(f32[192,128]{1,0:T(8,128)S(1)} %get-tuple-element.139), channel_id=1, source_target_pairs={{0,2},{2,0},{4,6},{6,4},{1,3},{3,1},{5,7},{7,5},{8,10},{10,8},{12,... | collective-permute-start | bytes 294920 | tf_op jit(solution)/shard_map/ppermute | solution.py:424
  137.7 12.8 %collective-permute-start.6 = (f32[192,128]{1,0:T(8,128)S(1)}, f32[192,128]{1,0:T(8,128)S(1)}, u32[]{:S(2)}, u32[]{:S(2)}) collective-permute-start(f32[192,128]{1,0:T(8,128)S(1)} %get-tuple-element.138), channel_id=1, source_target_pairs={{0,4},{2,6},{4,0},{6,2},{1,5},{3,7},{5,1},{7,3},{8,12},{10,14},{12... | collective-permute-start | bytes 294920 | tf_op jit(solution)/shard_map/ppermute | solution.py:424
  141.1 9.5 %collective-permute-start.7 = (f32[192,128]{1,0:T(8,128)S(1)}, f32[192,128]{1,0:T(8,128)S(1)}, u32[]{:S(2)}, u32[]{:S(2)}) collective-permute-start(f32[192,128]{1,0:T(8,128)S(1)} %get-tuple-element.137), channel_id=1, source_target_pairs={{0,6},{2,4},{4,2},{6,0},{1,7},{3,5},{5,3},{7,1},{8,14},{10,12},{12... | collective-permute-start | bytes 294920 | tf_op jit(solution)/shard_map/ppermute | solution.py:424
  150.6 14.8 %collective-permute-start.10 = (f32[192,128]{1,0:T(8,128)S(1)}, f32[192,128]{1,0:T(8,128)S(1)}, u32[]{:S(2)}, u32[]{:S(2)}) collective-permute-start(f32[192,128]{1,0:T(8,128)S(1)} %fusion.1), channel_id=1, source_target_pairs={{0,24},{8,16},{16,8},{24,0},{1,25},{9,17},{17,9},{25,1},{2,26},{10... | collective-permute-start | bytes 294920 | tf_op jit(solution)/shard_map/ppermute | solution.py:424
  156.7 8.7 %collective-permute-start.8 = (f32[192,128]{1,0:T(8,128)S(1)}, f32[192,128]{1,0:T(8,128)S(1)}, u32[]{:S(2)}, u32[]{:S(2)}) collective-permute-start(f32[192,128]{1,0:T(8,128)S(1)} %fusion.1), channel_id=1, source_target_pairs={{0,8},{8,0},{16,24},{24,16},{1,9},{9,1},{17,25},{25,17},{2,10},{10... | collective-permute-start | bytes 294920 | tf_op jit(solution)/shard_map/ppermute | solution.py:424
  156.7 8.9 %collective-permute-start.9 = (f32[192,128]{1,0:T(8,128)S(1)}, f32[192,128]{1,0:T(8,128)S(1)}, u32[]{:S(2)}, u32[]{:S(2)}) collective-permute-start(f32[192,128]{1,0:T(8,128)S(1)} %fusion.1), channel_id=1, source_target_pairs={{0,16},{8,24},{16,0},{24,8},{1,17},{9,25},{17,1},{25,9},{2,18},{10... | collective-permute-start | bytes 294920 | tf_op jit(solution)/shard_map/ppermute | solution.py:424
  165.6 5.4 %collective-permute-start.11 = (f32[192,128]{1,0:T(8,128)S(1)}, f32[192,128]{1,0:T(8,128)S(1)}, u32[]{:S(2)}, u32[]{:S(2)}) collective-permute-start(f32[192,128]{1,0:T(8,128)S(1)} %add_add_fusion), channel_id=1, source_target_pairs={{0,2},{2,0},{4,6},{6,4},{1,3},{3,1},{5,7},{7,5},{8,10},{10,8},{12,... | collective-permute-start | bytes 294920 | tf_op jit(solution)/shard_map/ppermute | solution.py:424
  166.9 5.5 %collective-permute-start.12 = (f32[192,128]{1,0:T(8,128)S(1)}, f32[192,128]{1,0:T(8,128)S(1)}, u32[]{:S(2)}, u32[]{:S(2)}) collective-permute-start(f32[192,128]{1,0:T(8,128)S(1)} %add_add_fusion), channel_id=1, source_target_pairs={{0,4},{2,6},{4,0},{6,2},{1,5},{3,7},{5,1},{7,3},{8,12},{10,14},{12... | collective-permute-start | bytes 294920 | tf_op jit(solution)/shard_map/ppermute | solution.py:424
  168.9 5.5 %collective-permute-start.13 = (f32[192,128]{1,0:T(8,128)S(1)}, f32[192,128]{1,0:T(8,128)S(1)}, u32[]{:S(2)}, u32[]{:S(2)}) collective-permute-start(f32[192,128]{1,0:T(8,128)S(1)} %add_add_fusion), channel_id=1, source_target_pairs={{0,6},{2,4},{4,2},{6,0},{1,7},{3,5},{5,3},{7,1},{8,14},{10,12},{12... | collective-permute-start | bytes 294920 | tf_op jit(solution)/shard_map/ppermute | solution.py:424
  175.2 1.8 %collective-permute-start.14 = (f32[768,128]{1,0:T(8,128)S(1)}, f32[768,128]{1,0:T(8,128)S(1)}, u32[]{:S(2)}, u32[]{:S(2)}) collective-permute-start(f32[768,128]{1,0:T(8,128)S(1)} %bitcast_select_fusion), channel_id=1, source_target_pairs={{0,1},{1,0},{2,3},{3,2},{4,5},{5,4},{6,7},{7,6},{8,9},{9,8},{10,11... | collective-permute-start | bytes 1179656 | tf_op jit(solution)/shard_map/ppermute | solution.py:424
  (6 other events, 4.7 us)

commit v7 on v6

--- a/solution.py
+++ b/solution.py
@@ -514,9 +514,9 @@
 
     head = edge_delta(received, 0, 0)
     tail = edge_delta(received, width - 1, received.shape[2] - 1)
-    received, head, tail = lax.optimization_barrier((received, head, tail))
+    local = add(received, chunks[0], second is None)
+    local, head, tail = lax.optimization_barrier((local, head, tail))
     delta_left, delta_right = column_neighbours(head, tail)
-    local = add(received, chunks[0], second is None)
     if second is not None:
         local = add(second, chunks[1], True)
     local, deltas, delta_left, delta_right = lax.optimization_barrier(

time: 180 us -> 180 us (level)
    ppermute x2, waiting for transfers between devices: 0.01 us -> 1.83 us  [column_neighbours(): right = lax.ppermute(first, MESH_AXES, [(b, a) for a, b in pairs])]
  transfers between devices with their start and end apart: 17 -> 17, of which waited for: 8 -> 8; matrix products, arithmetic and copies ran while one was open for 4% -> 4% of each run, Pallas kernels for 33% -> 34%
where the time goes in v7:
time: 180 us; the launch traced here: 179 us
  Pallas kernels  60.8 us (34%)
  waiting for transfers between devices  52.1 us (29%)
  starting transfers between devices  45.7 us (25%)
  local copies, waits for them, and re-layouts  15.1 us (8%)
  other arithmetic  4.39 us (2%)
    all_to_all x2, waiting for transfers between devices, to_columns(): lax.all_to_all(part, ('tm', 'height'), split_axis=0, concat_axis=0, tiled...  42.6 us
    pallas_call x2, Pallas kernels, moments(): pl.pallas_call(functools.partial(moments_kernel, group, groups, places, f...  27.8 us
    all_to_all x2, starting transfers between devices, to_columns(): lax.all_to_all(part, ('tm', 'height'), split_axis=0, concat_axis=0, tiled...  20.2 us
    pallas_call x2, Pallas kernels, backward(): pl.pallas_call(functools.partial(backward_kernel, group, [0] * len(ext)),...  16.1 us
    pallas_call x1, Pallas kernels, forward(): pl.pallas_call(functools.partial(forward_kernel, group), grid=(frames //...  15.5 us
    ppermute x11, starting transfers between devices, exchanged(): lax.ppermute(parts(s), axis, [(i, i ^ s) for i in range(count)])  14.4 us
    ppermute x2, starting transfers between devices, column_neighbours(): left = lax.ppermute(last, MESH_AXES, pairs)  8.43 us
    ppermute x11, waiting for transfers between devices, exchanged(): lax.ppermute(parts(s), axis, [(i, i ^ s) for i in range(count)])  7.6 us
  transfers between devices with their start and end apart: 17, of which 8 were waited for; matrix products, arithmetic and copies ran while one was open for 4% of the time, Pallas kernels for 34%

profile of v7, /device:TPU:0, one launch (start us, length us, event | category | flops | bytes accessed | tf_op | source)
XLA Modules:
  0.0 179.0 jit_solution(7665054037514645657)
XLA Ops:
  0.6 3.3 %slice.43 = bf16[16,2,2,2,64,128]{5,4,3,2,1,0:T(8,128)(2,1)} slice(bf16[16,4,2,2,64,128]{5,4,3,2,1,0:T(8,128)(2,1)} %bitcast.62), slice={[0:16:1], [0:4:3], [0:2:1], [0:2:1], [0:64:1], [0:128:1]} | slice | bytes 4194304 | tf_op jit(solution)/shard_map/slice | solution.py:487
  3.9 8.4 %all-to-all-start = ((bf16[16,4,2,64,128]{4,3,2,1,0:T(8,128)(2,1)}), bf16[16,4,2,64,128]{4,3,2,1,0:T(8,128)(2,1)S(1)}, u32[]{:S(2)}, u32[]{:S(2)}) async-start(bf16[16,4,2,64,128]{4,3,2,1,0:T(8,128)(2,1)} %bitcast.59), calls=%async_computation | async-start | bytes 4194304 | tf_op jit(solution)/shard_map/all_to_all | solution.py:474
  13.6 4.6 %collective-permute-start = (bf16[1,8,256,128]{3,2,1,0:T(8,128)(2,1)S(1)}, bf16[1,8,256,128]{3,2,1,0:T(8,128)(2,1)}, u32[]{:S(2)}, u32[]{:S(2)}) collective-permute-start(bf16[1,8,256,128]{3,2,1,0:T(8,128)(2,1)S(1)} %get-tuple-element.130), channel_id=1, source_target_pairs={{0,2},{2,4},{4,6},{6,8},{8,10},{10,12},{12,14},{14,16},{16,18},{18... | collective-permute-start | bytes 1572872 | tf_op jit(solution)/shard_map/ppermute | solution.py:19
  26.6 3.2 %slice.58 = bf16[16,2,2,2,64,128]{5,4,3,2,1,0:T(8,128)(2,1)} slice(bf16[16,4,2,2,64,128]{5,4,3,2,1,0:T(8,128)(2,1)} %bitcast.63), slice={[0:16], [1:3], [0:2], [0:2], [0:64], [0:128]} | slice | bytes 4194304 | tf_op jit(solution)/shard_map/slice | solution.py:487
  29.9 32.0 %all-to-all-done = bf16[16,4,2,64,128]{4,3,2,1,0:T(8,128)(2,1)S(1)} async-done(((bf16[16,4,2,64,128]{4,3,2,1,0:T(8,128)(2,1)}), bf16[16,4,2,64,128]{4,3,2,1,0:T(8,128)(2,1)S(1)}, u32[]{:S(2)}, u32[]{:S(2)}) %all-to-all-start) | async-done | bytes 2097184 | tf_op jit(solution)/shard_map/all_to_all | solution.py:474
  61.9 11.7 %all-to-all-start.1 = ((bf16[16,4,2,64,128]{4,3,2,1,0:T(8,128)(2,1)}), bf16[16,4,2,64,128]{4,3,2,1,0:T(8,128)(2,1)}, u32[]{:S(2)}, u32[]{:S(2)}) async-start(bf16[16,4,2,64,128]{4,3,2,1,0:T(8,128)(2,1)} %bitcast.58), calls=%async_computation.1 | async-start | bytes 4194304 | tf_op jit(solution)/shard_map/all_to_all | solution.py:474
  73.7 15.5 %shard_map.77 = (f32[8,8,256,128]{3,2,1,0:T(8,128)}, bf16[10,8,128,256]{3,2,1,0:T(8,128)(2,1)}) custom-call(bf16[8,8,256,128]{3,2,1,0:T(8,128)(2,1)} %bitcast.70, bf16[8,8,256,128]{3,2,1,0:T(8,128)(2,1)} %bitcast.71, bf16[1,8,256,128]{3,2,1,0:T(8,128)(2,1)} %collective-permute-done.left.left_before, ...), custom_call_target="tpu_custom_call" | custom-call | flops 64424509440 | bytes 29360128 | tf_op jit(solution)/shard_map/pallas_call | solution.py:154
  89.6 1.8 %multiply_convert_fusion = (bf16[1,8,256,128]{3,2,1,0:T(8,128)(2,1)S(1)}, bf16[1,8,256,128]{3,2,1,0:T(8,128)(2,1)S(1)}) fusion(f32[1,8,256,128]{3,2,1,0:T(8,128)S(1)} %bitcast.60, f32[8,8,256,128]{3,2,1,0:T(8,128)} %get-tuple-element.71.refs_1_.refs_2_, f32[1,8,256,128]{3,2,1,0:T(8,128)S(1)} %bitcast.61), kind=kLoop, calls=%fused_computation.3 | loop fusion | flops 1048576 | bytes 5242880 | tf_op jit(solution)/shard_map/convert_element_type | solution.py:513
  91.5 13.9 %shard_map.78 = (bf16[2,8,256,128]{3,2,1,0:T(8,128)(2,1)}, bf16[2,8,256,128]{3,2,1,0:T(8,128)(2,1)}, f32[12,128,128]{2,1,0:T(8,128)}) custom-call(f32[3,8]{1,0:T(4,128)} %copy-done.4, s32[1]{0:T(128)} %bitcast.side, bf16[4,4,4,2,64,128]{5,4,3,2,1,0:T(8,128)(2,1)} %bitcast.57, f32[8,8,256,128]{3,2,1,0:T(8,128)} %get-tuple-element.71.refs_1_.refs_2_, ...), custom_call_target="tpu_custom_call" | custom-call | flops 8053063680 | bytes 20971520 | tf_op jit(solution)/shard_map/pallas_call | solution.py:305
  105.4 3.8 %collective-permute-start.2 = (bf16[1,8,256,128]{3,2,1,0:T(8,128)(2,1)S(1)}, bf16[1,8,256,128]{3,2,1,0:T(8,128)(2,1)S(1)}, u32[]{:S(2)}, u32[]{:S(2)}) collective-permute-start(bf16[1,8,256,128]{3,2,1,0:T(8,128)(2,1)S(1)} %get-tuple-element.84), channel_id=1, source_target_pairs={{0,2},{2,4},{4,6},{6,8},{8,10},{10,12},{12,14},{14,16},{16,18},{18... | collective-permute-start | bytes 1572872 | tf_op jit(solution)/shard_map/ppermute | solution.py:19
  109.2 1.5 collective-permute-start.3
  110.7 10.6 %all-to-all-done.1 = bf16[16,4,2,64,128]{4,3,2,1,0:T(8,128)(2,1)} async-done(((bf16[16,4,2,64,128]{4,3,2,1,0:T(8,128)(2,1)}), bf16[16,4,2,64,128]{4,3,2,1,0:T(8,128)(2,1)}, u32[]{:S(2)}, u32[]{:S(2)}) %all-to-all-start.1) | async-done | bytes 2097184 | tf_op jit(solution)/shard_map/all_to_all | solution.py:474
  121.3 13.9 %shard_map.79 = (bf16[2,8,256,128]{3,2,1,0:T(8,128)(2,1)}, bf16[2,8,256,128]{3,2,1,0:T(8,128)(2,1)}, f32[6,128,128]{2,1,0:T(8,128)}, f32[6,128,128]{2,1,0:T(8,128)}) custom-call(f32[3,8]{1,0:T(4,128)} %copy-done.4, s32[1]{0:T(128)} %bitcast.side, bf16[4,4,4,2,64,128]{5,4,3,2,1,0:T(8,128)(2,1)} %bitcast.7.refs_0_, ...), custom_call_target="tpu_custom_call" | custom-call | flops 8053063680 | bytes 20971520 | tf_op jit(solution)/shard_map/pallas_call | solution.py:305
  135.2 1.8 %collective-permute-done.3.refs_5_ = bf16[1,8,256,128]{3,2,1,0:T(8,128)(2,1)S(1)} collective-permute-done((bf16[1,8,256,128]{3,2,1,0:T(8,128)(2,1)S(1)}, bf16[1,8,256,128]{3,2,1,0:T(8,128)(2,1)S(1)}, u32[]{:S(2)}, u32[]{:S(2)}) %collective-permute-start.3) | collective-permute-done | bytes 524320 | tf_op jit(solution)/shard_map/ppermute | solution.py:20
  137.2 1.7 collective-permute-done.4
  141.7 1.9 %collective-permute-start.7 = (f32[192,128]{1,0:T(8,128)S(1)}, f32[192,128]{1,0:T(8,128)S(1)}, u32[]{:S(2)}, u32[]{:S(2)}) collective-permute-start(f32[192,128]{1,0:T(8,128)S(1)} %get-tuple-element.137), channel_id=1, source_target_pairs={{0,6},{2,4},{4,2},{6,0},{1,7},{3,5},{5,3},{7,1},{8,14},{10,12},{12... | collective-permute-start | bytes 294920 | tf_op jit(solution)/shard_map/ppermute | solution.py:424
  143.6 8.0 %shard_map.80.refs_8_ = bf16[8,8,256,128]{3,2,1,0:T(8,128)(2,1)} custom-call(bf16[1,8,256,128]{3,2,1,0:T(8,128)(2,1)} %copy-done.12, bf16[2,8,256,128]{3,2,1,0:T(8,128)(2,1)} %get-tuple-element.95.refs_1_.refs_2_, bf16[2,8,256,128]{3,2,1,0:T(8,128)(2,1)} %get-tuple-element.95.refs_1_.refs_2_, ...), custom_call_target="tpu_custom_call" | custom-call | flops 6442450944 | bytes 6291456 | tf_op jit(solution)/shard_map/pallas_call | solution.py:394
  151.7 4.8 %collective-permute-start.8 = (f32[192,128]{1,0:T(8,128)S(1)}, f32[192,128]{1,0:T(8,128)S(1)}, u32[]{:S(2)}, u32[]{:S(2)}) collective-permute-start(f32[192,128]{1,0:T(8,128)S(1)} %fusion.1), channel_id=1, source_target_pairs={{0,8},{8,0},{16,24},{24,16},{1,9},{9,1},{17,25},{25,17},{2,10},{10... | collective-permute-start | bytes 294920 | tf_op jit(solution)/shard_map/ppermute | solution.py:424
  156.6 2.3 %collective-permute-start.10 = (f32[192,128]{1,0:T(8,128)S(1)}, f32[192,128]{1,0:T(8,128)S(1)}, u32[]{:S(2)}, u32[]{:S(2)}) collective-permute-start(f32[192,128]{1,0:T(8,128)S(1)} %fusion.1), channel_id=1, source_target_pairs={{0,24},{8,16},{16,8},{24,0},{1,25},{9,17},{17,9},{25,1},{2,26},{10... | collective-permute-start | bytes 294920 | tf_op jit(solution)/shard_map/ppermute | solution.py:424
  158.9 8.0 %shard_map.81 = bf16[8,8,256,128]{3,2,1,0:T(8,128)(2,1)} custom-call(bf16[2,8,256,128]{3,2,1,0:T(8,128)(2,1)} %get-tuple-element.112.refs_3_.refs_4_.refs_0_, bf16[2,8,256,128]{3,2,1,0:T(8,128)(2,1)} %get-tuple-element.113.refs_5_.refs_1_.refs_2_, ...), custom_call_target="tpu_custom_call", output_to_operand_aliasing={{}: (8, {})} | custom-call | flops 6442450944 | bytes 6291456 | tf_op jit(solution)/shard_map/pallas_call | solution.py:394
  167.6 1.5 collective-permute-start.12
  170.5 1.7 collective-permute-done.11
  173.2 1.5 collective-permute-done.13
  175.5 1.7 collective-permute-done.14
  (64 shorter events, 18.7 us)
Async XLA Ops:
  3.9 15.7 %copy-start.2 = (bf16[3,3,128,128]{3,2,1,0:T(8,128)(2,1)S(1)}, bf16[3,3,128,128]{3,2,1,0:T(8,128)(2,1)}, u32[]{:S(2)}) copy-start(bf16[3,3,128,128]{3,2,1,0:T(8,128)(2,1)} %spatial.1) | copy-start | bytes 884740
  3.9 15.7 %copy-start.3 = (bf16[3,128,128]{2,1,0:T(8,128)(2,1)S(1)}, bf16[3,128,128]{2,1,0:T(8,128)(2,1)}, u32[]{:S(2)}) copy-start(bf16[3,128,128]{2,1,0:T(8,128)(2,1)} %temporal.1) | copy-start | bytes 294916
  3.9 15.7 %copy-start.5 = (s32[4]{0:T(128)S(1)}, s32[4]{0:T(128)}, u32[]{:S(2)}) copy-start(s32[4]{0:T(128)} %lengths.1) | copy-start | bytes 52
  3.9 58.0 %all-to-all-start = ((bf16[16,4,2,64,128]{4,3,2,1,0:T(8,128)(2,1)}), bf16[16,4,2,64,128]{4,3,2,1,0:T(8,128)(2,1)S(1)}, u32[]{:S(2)}, u32[]{:S(2)}) async-start(bf16[16,4,2,64,128]{4,3,2,1,0:T(8,128)(2,1)} %bitcast.59), calls=%async_computation | async-start | bytes 4194304 | tf_op jit(solution)/shard_map/all_to_all | solution.py:474
  13.6 60.0 %collective-permute-start = (bf16[1,8,256,128]{3,2,1,0:T(8,128)(2,1)S(1)}, bf16[1,8,256,128]{3,2,1,0:T(8,128)(2,1)}, u32[]{:S(2)}, u32[]{:S(2)}) collective-permute-start(bf16[1,8,256,128]{3,2,1,0:T(8,128)(2,1)S(1)} %get-tuple-element.130), channel_id=1, source_target_pairs={{0,2},{2,4},{4,6},{6,8},{8,10},{10,12},{12,14},{14,16},{16,18},{18... | collective-permute-start | bytes 1572872 | tf_op jit(solution)/shard_map/ppermute | solution.py:19
  18.3 55.4 %collective-permute-start.1 = (bf16[1,8,256,128]{3,2,1,0:T(8,128)(2,1)S(1)}, bf16[1,8,256,128]{3,2,1,0:T(8,128)(2,1)}, u32[]{:S(2)}, u32[]{:S(2)}) collective-permute-start(bf16[1,8,256,128]{3,2,1,0:T(8,128)(2,1)S(1)} %get-tuple-element.129), channel_id=1, source_target_pairs={{2,0},{4,2},{6,4},{8,6},{10,8},{12,10},{14,12},{16,14},{18,16},{20... | collective-permute-start | bytes 1572872 | tf_op jit(solution)/shard_map/ppermute | solution.py:20
  23.9 1.0 copy-start.7
  61.9 27.3 %copy-start.10 = (bf16[16,4,2,64,128]{4,3,2,1,0:T(8,128)(2,1)}, bf16[16,4,2,64,128]{4,3,2,1,0:T(8,128)(2,1)S(1)}, u32[]{:S(2)}) copy-start(bf16[16,4,2,64,128]{4,3,2,1,0:T(8,128)(2,1)S(1)} %all-to-all-done) | copy-start | bytes 6291460
  61.9 59.4 %all-to-all-start.1 = ((bf16[16,4,2,64,128]{4,3,2,1,0:T(8,128)(2,1)}), bf16[16,4,2,64,128]{4,3,2,1,0:T(8,128)(2,1)}, u32[]{:S(2)}, u32[]{:S(2)}) async-start(bf16[16,4,2,64,128]{4,3,2,1,0:T(8,128)(2,1)} %bitcast.58), calls=%async_computation.1 | async-start | bytes 4194304 | tf_op jit(solution)/shard_map/all_to_all | solution.py:474
  105.4 29.8 %collective-permute-start.2 = (bf16[1,8,256,128]{3,2,1,0:T(8,128)(2,1)S(1)}, bf16[1,8,256,128]{3,2,1,0:T(8,128)(2,1)S(1)}, u32[]{:S(2)}, u32[]{:S(2)}) collective-permute-start(bf16[1,8,256,128]{3,2,1,0:T(8,128)(2,1)S(1)} %get-tuple-element.84), channel_id=1, source_target_pairs={{0,2},{2,4},{4,6},{6,8},{8,10},{10,12},{12,14},{14,16},{16,18},{18... | collective-permute-start | bytes 1572872 | tf_op jit(solution)/shard_map/ppermute | solution.py:19
  109.2 27.8 %collective-permute-start.3 = (bf16[1,8,256,128]{3,2,1,0:T(8,128)(2,1)S(1)}, bf16[1,8,256,128]{3,2,1,0:T(8,128)(2,1)S(1)}, u32[]{:S(2)}, u32[]{:S(2)}) collective-permute-start(bf16[1,8,256,128]{3,2,1,0:T(8,128)(2,1)S(1)} %get-tuple-element.85), channel_id=1, source_target_pairs={{2,0},{4,2},{6,4},{8,6},{10,8},{12,10},{14,12},{16,14},{18,16},{20... | collective-permute-start | bytes 1572872 | tf_op jit(solution)/shard_map/ppermute | solution.py:20
  135.2 8.4 %copy-start.12 = (bf16[1,8,256,128]{3,2,1,0:T(8,128)(2,1)}, bf16[1,8,256,128]{3,2,1,0:T(8,128)(2,1)S(1)}, u32[]{:S(2)}) copy-start(bf16[1,8,256,128]{3,2,1,0:T(8,128)(2,1)S(1)} %collective-permute-done.2.refs_0_) | copy-start | bytes 1572868
  137.0 14.6 %copy-start.11 = (bf16[1,8,256,128]{3,2,1,0:T(8,128)(2,1)}, bf16[1,8,256,128]{3,2,1,0:T(8,128)(2,1)S(1)}, u32[]{:S(2)}) copy-start(bf16[1,8,256,128]{3,2,1,0:T(8,128)(2,1)S(1)} %collective-permute-done.3.refs_5_) | copy-start | bytes 1572868
  137.0 1.9 %collective-permute-start.4 = (f32[768,128]{1,0:T(8,128)}, f32[768,128]{1,0:T(8,128)S(1)}, u32[]{:S(2)}, u32[]{:S(2)}) collective-permute-start(f32[768,128]{1,0:T(8,128)} %bitcast.76), channel_id=1, source_target_pairs={{0,1},{1,0},{2,3},{3,2},{4,5},{5,4},{6,7},{7,6},{8,9},{9,8},{10,11... | collective-permute-start | bytes 1179656 | tf_op jit(solution)/shard_map/ppermute | solution.py:424
  140.0 11.6 %collective-permute-start.5 = (f32[192,128]{1,0:T(8,128)S(1)}, f32[192,128]{1,0:T(8,128)S(1)}, u32[]{:S(2)}, u32[]{:S(2)}) collective-permute-start(f32[192,128]{1,0:T(8,128)S(1)} %get-tuple-element.139), channel_id=1, source_target_pairs={{0,2},{2,0},{4,6},{6,4},{1,3},{3,1},{5,7},{7,5},{8,10},{10,8},{12,... | collective-permute-start | bytes 294920 | tf_op jit(solution)/shard_map/ppermute | solution.py:424
  141.1 10.6 %collective-permute-start.6 = (f32[192,128]{1,0:T(8,128)S(1)}, f32[192,128]{1,0:T(8,128)S(1)}, u32[]{:S(2)}, u32[]{:S(2)}) collective-permute-start(f32[192,128]{1,0:T(8,128)S(1)} %get-tuple-element.138), channel_id=1, source_target_pairs={{0,4},{2,6},{4,0},{6,2},{1,5},{3,7},{5,1},{7,3},{8,12},{10,14},{12... | collective-permute-start | bytes 294920 | tf_op jit(solution)/shard_map/ppermute | solution.py:424
  141.7 10.0 %collective-permute-start.7 = (f32[192,128]{1,0:T(8,128)S(1)}, f32[192,128]{1,0:T(8,128)S(1)}, u32[]{:S(2)}, u32[]{:S(2)}) collective-permute-start(f32[192,128]{1,0:T(8,128)S(1)} %get-tuple-element.137), channel_id=1, source_target_pairs={{0,6},{2,4},{4,2},{6,0},{1,7},{3,5},{5,3},{7,1},{8,14},{10,12},{12... | collective-permute-start | bytes 294920 | tf_op jit(solution)/shard_map/ppermute | solution.py:424
  151.7 15.2 %collective-permute-start.8 = (f32[192,128]{1,0:T(8,128)S(1)}, f32[192,128]{1,0:T(8,128)S(1)}, u32[]{:S(2)}, u32[]{:S(2)}) collective-permute-start(f32[192,128]{1,0:T(8,128)S(1)} %fusion.1), channel_id=1, source_target_pairs={{0,8},{8,0},{16,24},{24,16},{1,9},{9,1},{17,25},{25,17},{2,10},{10... | collective-permute-start | bytes 294920 | tf_op jit(solution)/shard_map/ppermute | solution.py:424
  156.4 10.5 %collective-permute-start.9 = (f32[192,128]{1,0:T(8,128)S(1)}, f32[192,128]{1,0:T(8,128)S(1)}, u32[]{:S(2)}, u32[]{:S(2)}) collective-permute-start(f32[192,128]{1,0:T(8,128)S(1)} %fusion.1), channel_id=1, source_target_pairs={{0,16},{8,24},{16,0},{24,8},{1,17},{9,25},{17,1},{25,9},{2,18},{10... | collective-permute-start | bytes 294920 | tf_op jit(solution)/shard_map/ppermute | solution.py:424
  156.6 10.3 %collective-permute-start.10 = (f32[192,128]{1,0:T(8,128)S(1)}, f32[192,128]{1,0:T(8,128)S(1)}, u32[]{:S(2)}, u32[]{:S(2)}) collective-permute-start(f32[192,128]{1,0:T(8,128)S(1)} %fusion.1), channel_id=1, source_target_pairs={{0,24},{8,16},{16,8},{24,0},{1,25},{9,17},{17,9},{25,1},{2,26},{10... | collective-permute-start | bytes 294920 | tf_op jit(solution)/shard_map/ppermute | solution.py:424
  167.0 5.2 %collective-permute-start.11 = (f32[192,128]{1,0:T(8,128)S(1)}, f32[192,128]{1,0:T(8,128)S(1)}, u32[]{:S(2)}, u32[]{:S(2)}) collective-permute-start(f32[192,128]{1,0:T(8,128)S(1)} %add_add_fusion), channel_id=1, source_target_pairs={{0,2},{2,0},{4,6},{6,4},{1,3},{3,1},{5,7},{7,5},{8,10},{10,8},{12,... | collective-permute-start | bytes 294920 | tf_op jit(solution)/shard_map/ppermute | solution.py:424
  167.6 5.6 %collective-permute-start.12 = (f32[192,128]{1,0:T(8,128)S(1)}, f32[192,128]{1,0:T(8,128)S(1)}, u32[]{:S(2)}, u32[]{:S(2)}) collective-permute-start(f32[192,128]{1,0:T(8,128)S(1)} %add_add_fusion), channel_id=1, source_target_pairs={{0,4},{2,6},{4,0},{6,2},{1,5},{3,7},{5,1},{7,3},{8,12},{10,14},{12... | collective-permute-start | bytes 294920 | tf_op jit(solution)/shard_map/ppermute | solution.py:424
  169.2 5.5 %collective-permute-start.13 = (f32[192,128]{1,0:T(8,128)S(1)}, f32[192,128]{1,0:T(8,128)S(1)}, u32[]{:S(2)}, u32[]{:S(2)}) collective-permute-start(f32[192,128]{1,0:T(8,128)S(1)} %add_add_fusion), channel_id=1, source_target_pairs={{0,6},{2,4},{4,2},{6,0},{1,7},{3,5},{5,3},{7,1},{8,14},{10,12},{12... | collective-permute-start | bytes 294920 | tf_op jit(solution)/shard_map/ppermute | solution.py:424
  175.5 1.8 collective-permute-start.14
  (6 other events, 4.7 us)
